TPU v7x, 32 devices: a whole 2x2x4 slice. The times are simulated.
32 devices in a mesh: grp: 2 (over y), sp: 16 (over z, x, core).
Axes of the slice: x: 2, y: 2, z: 4, core: 2. Of those that a mesh axis runs over, the one named last changes fastest.
Arguments:
- tokens: bfloat16 [128, 256, 512], P(('grp', 'sp')), may hold values from -6 to 6
- frame_slot: int32 [16, 8], P('grp'), may hold values from 0 to 7, each once within a row
- norm_gain: float32 [4, 512], replicated, may hold values from 0.1 to 1.9
- norm_shift: float32 [4, 512], replicated, may hold values from -4 to 4
- w_qkv: bfloat16 [2, 512, 1536], replicated, may hold values from -0.375 to 0.375
- w_out: bfloat16 [2, 512, 512], replicated, may hold values from -0.75 to 0.75
- w_up: bfloat16 [2, 512, 2048], replicated, may hold values from -0.25 to 0.25
- b_up: float32 [2, 2048], replicated, may hold values from -4 to 4
- w_down: bfloat16 [2, 2048, 512], replicated, may hold values from -0.125 to 0.125
- b_down: float32 [2, 512], replicated, may hold values from -4 to 4
- cotangent: bfloat16 [128, 256, 512], P(('grp', 'sp')), may hold values from -6 to 6
Outputs:
- output: bfloat16 [128, 256, 512], P(('grp', 'sp'))
- grad_tokens: bfloat16 [128, 256, 512], P(('grp', 'sp'))
- grad_norm_gain: float32 [4, 512], P(None, 'sp')
- grad_norm_shift: float32 [4, 512], P(None, 'sp')
- grad_w_qkv: float32 [2, 512, 1536], P(None, 'sp')
- grad_w_out: float32 [2, 512, 512], P(None, 'sp')
- grad_w_up: float32 [2, 512, 2048], P(None, 'sp')
- grad_b_up: float32 [2, 2048], P(None, 'sp')
- grad_w_down: float32 [2, 2048, 512], P(None, 'sp')
- grad_b_down: float32 [2, 512], P(None, 'sp')
Inputs may be any that keep to these rules, and one draw needn't show every extreme that they name: `frame_slot`: each row names every slot of a group once; slots 0 to 5 are the video's time steps, the others are images.
All inputs are finite; a program needn't handle non-finite values.
Results may differ from a plain program's by a relative error of at most 0.028.
Values may be sent and summed in bfloat16 or wider, within the bound.
No kernel may reach another device: no remote copies, remote signals or barrier semaphores. Data moves between devices by JAX's collectives and lax.ppermute only.
A program may use at most 192 MiB of HBM per device.

v0:
```python
import jax
import jax.numpy as jnp
from jax import lax
from jax.sharding import PartitionSpec as P

HEADS = 8
HEAD = 64
VIDEO_STEPS = 6
GROUP_FRAMES = 8


FAR = -1e30
NORM_EPS = 1e-05


def norm_fwd(values_in, gain, shift):
    average = jnp.mean(values_in, axis=-1, keepdims=True)
    centred = values_in - average
    inv_scale = lax.rsqrt(jnp.mean(centred * centred, axis=-1, keepdims=True) + NORM_EPS)
    unit = centred * inv_scale
    return (unit * gain + shift, unit, inv_scale)


def norm_back(grad_out, unit, inv_scale, gain):
    grad_unit = grad_out * gain
    grad_in = inv_scale * (
        grad_unit
        - jnp.mean(grad_unit, axis=-1, keepdims=True)
        - unit * jnp.mean(grad_unit * unit, axis=-1, keepdims=True)
    )
    width = grad_out.shape[-1]
    grad_gain = jnp.sum((grad_out * unit).reshape(-1, width), axis=0)
    grad_shift = jnp.sum(grad_out.reshape(-1, width), axis=0)
    return (grad_in, grad_gain, grad_shift)


def matmul(left, right):
    return jnp.dot(left, right, preferred_element_type=jnp.float32)


def outer_sum(left, right):
    return lax.dot_general(
        left, right, (((0,), (0,)), ((), ())), preferred_element_type=jnp.float32
    )


def back_dot(grad_rows, weight):
    return lax.dot_general(
        grad_rows, weight, (((1,), (1,)), ((), ())), preferred_element_type=jnp.float32
    )


def score_table(query, keys, forms, allowed):
    scores = jnp.einsum(forms[0], query, keys, preferred_element_type=jnp.float32) * HEAD ** (-0.5)
    if allowed is not None:
        scores = jnp.where(allowed, scores, FAR)
    return scores


def core_fwd(query, keys, values, forms, allowed):
    scores = score_table(query, keys, forms, allowed)
    log_total = jax.nn.logsumexp(scores, axis=-1, keepdims=True)
    probs = jnp.exp(scores - log_total).astype(jnp.bfloat16)
    mixed = jnp.einsum(forms[1], probs, values, preferred_element_type=jnp.float32)
    return (mixed, log_total)


def core_back(query, keys, values, log_total, grad_mixed, forms, allowed):
    probs = jnp.exp(score_table(query, keys, forms, allowed) - log_total)
    probs_low = probs.astype(jnp.bfloat16)
    grad_probs = jnp.einsum(forms[0], grad_mixed, values, preferred_element_type=jnp.float32)
    centre = jnp.sum(probs * grad_probs, axis=-1, keepdims=True)
    grad_scores = (probs * (grad_probs - centre)).astype(jnp.bfloat16)
    grad_query = jnp.einsum(
        forms[1], grad_scores, keys, preferred_element_type=jnp.float32
    ) * HEAD ** (-0.5)
    grad_keys = jnp.einsum(
        forms[2], grad_scores, query, preferred_element_type=jnp.float32
    ) * HEAD ** (-0.5)
    grad_values = jnp.einsum(forms[2], probs_low, grad_mixed, preferred_element_type=jnp.float32)
    return (grad_query, grad_keys, grad_values)


def branch_fwd(values_in, gain, shift, weight_qkv, weight_out, forms, allowed):
    leading = values_in.shape[:-1]
    width = values_in.shape[-1]
    normed, unit, inv_scale = norm_fwd(values_in, gain, shift)
    normed_low = normed.astype(jnp.bfloat16).reshape(-1, width)
    joined = matmul(normed_low, weight_qkv).astype(jnp.bfloat16).reshape(leading + (3, HEADS, HEAD))
    mixed, log_total = core_fwd(
        joined[..., 0, :, :], joined[..., 1, :, :], joined[..., 2, :, :], forms, allowed
    )
    mixed_low = mixed.astype(jnp.bfloat16).reshape(-1, width)
    branch = matmul(mixed_low, weight_out).reshape(leading + (width,))
    return (branch, (unit, inv_scale, normed_low, joined, log_total, mixed_low))


def branch_back(grad_branch, kept, gain, weight_qkv, weight_out, forms, allowed):
    unit, inv_scale, normed_low, joined, log_total, mixed_low = kept
    leading = unit.shape[:-1]
    width = unit.shape[-1]
    grad_low = grad_branch.astype(jnp.bfloat16).reshape(-1, width)
    grad_w_out = outer_sum(mixed_low, grad_low)
    grad_mixed = (
        back_dot(grad_low, weight_out).astype(jnp.bfloat16).reshape(leading + (HEADS, HEAD))
    )
    grad_query, grad_keys, grad_values = core_back(
        joined[..., 0, :, :],
        joined[..., 1, :, :],
        joined[..., 2, :, :],
        log_total,
        grad_mixed,
        forms,
        allowed,
    )
    grad_joined = jnp.stack([grad_query, grad_keys, grad_values], axis=-3).astype(jnp.bfloat16)
    grad_joined = grad_joined.reshape(-1, 3 * width)
    grad_w_qkv = outer_sum(normed_low, grad_joined)
    grad_normed = back_dot(grad_joined, weight_qkv).reshape(leading + (width,))
    grad_in, grad_gain, grad_shift = norm_back(grad_normed, unit, inv_scale, gain)
    return (grad_in, (grad_gain, grad_shift, grad_w_qkv, grad_w_out))


def mlp_fwd(rows_in, gain, shift, weight_up, bias_up, weight_down, bias_down):
    normed, unit, inv_scale = norm_fwd(rows_in, gain, shift)
    normed_low = normed.astype(jnp.bfloat16)
    preact = matmul(normed_low, weight_up) + bias_up
    activated = jax.nn.gelu(preact).astype(jnp.bfloat16)
    result = rows_in + matmul(activated, weight_down) + bias_down
    return (result, (unit, inv_scale, normed_low, preact, activated))


def mlp_back(grad_out, kept, gain, weight_up, weight_down):
    unit, inv_scale, normed_low, preact, activated = kept
    grad_low = grad_out.astype(jnp.bfloat16)
    grad_w_down = outer_sum(activated, grad_low)
    grad_b_down = jnp.sum(grad_low.astype(jnp.float32), axis=0)
    grad_act = back_dot(grad_low, weight_down)
    unused, gelu_pull = jax.vjp(jax.nn.gelu, preact)
    grad_pre = gelu_pull(grad_act)[0].astype(jnp.bfloat16)
    grad_w_up = outer_sum(normed_low, grad_pre)
    grad_b_up = jnp.sum(grad_pre.astype(jnp.float32), axis=0)
    grad_normed = back_dot(grad_pre, weight_up)
    grad_in, grad_gain, grad_shift = norm_back(grad_normed, unit, inv_scale, gain)
    return (
        grad_out + grad_in,
        (grad_gain, grad_shift, grad_w_up, grad_b_up, grad_w_down, grad_b_down),
    )


def pack_grads(attn_grads, mlp_grads):
    return (
        jnp.stack([attn_grads[0], mlp_grads[0]]),
        jnp.stack([attn_grads[1], mlp_grads[1]]),
        attn_grads[2][None],
        attn_grads[3][None],
        mlp_grads[2][None],
        mlp_grads[3][None],
        mlp_grads[4][None],
        mlp_grads[5][None],
    )


def shards(
    tokens, frame_slot, norm_gain, norm_shift, w_qkv, w_out, w_up, b_up, w_down, b_down, cotangent
):
    frames, patches, width = tokens.shape
    space_forms = ("fqhe,fkhe->fhqk", "fhqk,fkhe->fqhe", "fhqk,fqhe->fkhe")
    time_forms = ("gtphe,gsphe->gphts", "gphts,gsphe->gtphe", "gphts,gtphe->gsphe")
    start = tokens.astype(jnp.float32)
    space_branch, space_kept = branch_fwd(
        start, norm_gain[0], norm_shift[0], w_qkv[0], w_out[0], space_forms, None
    )
    after_space = (start + space_branch).reshape(-1, width)
    first_out, first_kept = mlp_fwd(
        after_space, norm_gain[1], norm_shift[1], w_up[0], b_up[0], w_down[0], b_down[0]
    )
    sent = first_out.astype(jnp.bfloat16).reshape(frames, patches, width)
    by_place = lax.all_to_all(sent, "sp", split_axis=1, concat_axis=0, tiled=True)
    span = by_place.shape[0]
    places = by_place.shape[1]
    group_count = span // GROUP_FRAMES
    query_slot = frame_slot[:, :, None]
    key_slot = frame_slot[:, None, :]
    allowed = (key_slot <= query_slot) & ((query_slot < VIDEO_STEPS) | (key_slot == query_slot))
    allowed = allowed[:, None, None, :, :]
    time_in = by_place.astype(jnp.float32).reshape(group_count, GROUP_FRAMES, places, width)
    time_branch, time_kept = branch_fwd(
        time_in, norm_gain[2], norm_shift[2], w_qkv[1], w_out[1], time_forms, allowed
    )
    time_low = time_branch.astype(jnp.bfloat16).reshape(span, places, width)
    returned = lax.all_to_all(time_low, "sp", split_axis=0, concat_axis=1, tiled=True)
    after_time = first_out + returned.reshape(-1, width).astype(jnp.float32)
    final, second_kept = mlp_fwd(
        after_time, norm_gain[3], norm_shift[3], w_up[1], b_up[1], w_down[1], b_down[1]
    )
    output = final.astype(jnp.bfloat16).reshape(frames, patches, width)
    grad_after_time, second_grads = mlp_back(
        cotangent.astype(jnp.float32).reshape(-1, width),
        second_kept,
        norm_gain[3],
        w_up[1],
        w_down[1],
    )
    grad_rows_low = grad_after_time.astype(jnp.bfloat16).reshape(frames, patches, width)
    grad_places = lax.all_to_all(grad_rows_low, "sp", split_axis=1, concat_axis=0, tiled=True)
    grad_time_in, time_grads = branch_back(
        grad_places.reshape(group_count, GROUP_FRAMES, places, width),
        time_kept,
        norm_gain[2],
        w_qkv[1],
        w_out[1],
        time_forms,
        allowed,
    )
    grad_time_low = grad_time_in.astype(jnp.bfloat16).reshape(span, places, width)
    grad_back_rows = lax.all_to_all(grad_time_low, "sp", split_axis=0, concat_axis=1, tiled=True)
    time_pack = pack_grads(time_grads, second_grads)
    grad_first = grad_after_time + grad_back_rows.reshape(-1, width).astype(jnp.float32)
    grad_after_space, first_grads = mlp_back(
        grad_first, first_kept, norm_gain[1], w_up[0], w_down[0]
    )
    grad_space_rows = grad_after_space.reshape(frames, patches, width)
    grad_start, space_grads = branch_back(
        grad_space_rows, space_kept, norm_gain[0], w_qkv[0], w_out[0], space_forms, None
    )
    grad_tokens = (grad_space_rows + grad_start).astype(jnp.bfloat16)
    space_pack = pack_grads(space_grads, first_grads)
    joined = [jnp.concatenate([space_pack[index], time_pack[index]], axis=0) for index in range(8)]
    row_sums = (
        lax.psum_scatter(
            joined[0].astype(jnp.bfloat16), "sp", scatter_dimension=1, tiled=True
        ).astype(jnp.float32),
        lax.psum_scatter(
            joined[1].astype(jnp.bfloat16), "sp", scatter_dimension=1, tiled=True
        ).astype(jnp.float32),
        lax.psum_scatter(
            joined[2].astype(jnp.bfloat16), "sp", scatter_dimension=1, tiled=True
        ).astype(jnp.float32),
        lax.psum_scatter(
            joined[3].astype(jnp.bfloat16), "sp", scatter_dimension=1, tiled=True
        ).astype(jnp.float32),
        lax.psum_scatter(
            joined[4].astype(jnp.bfloat16), "sp", scatter_dimension=1, tiled=True
        ).astype(jnp.float32),
        lax.psum_scatter(
            joined[5].astype(jnp.bfloat16), "sp", scatter_dimension=1, tiled=True
        ).astype(jnp.float32),
        lax.psum_scatter(
            joined[6].astype(jnp.bfloat16), "sp", scatter_dimension=1, tiled=True
        ).astype(jnp.float32),
        lax.psum_scatter(
            joined[7].astype(jnp.bfloat16), "sp", scatter_dimension=1, tiled=True
        ).astype(jnp.float32),
    )
    totals = (
        lax.psum(row_sums[0].astype(jnp.bfloat16), "grp").astype(jnp.float32),
        lax.psum(row_sums[1].astype(jnp.bfloat16), "grp").astype(jnp.float32),
        lax.psum(row_sums[2].astype(jnp.bfloat16), "grp").astype(jnp.float32),
        lax.psum(row_sums[3].astype(jnp.bfloat16), "grp").astype(jnp.float32),
        lax.psum(row_sums[4].astype(jnp.bfloat16), "grp").astype(jnp.float32),
        lax.psum(row_sums[5].astype(jnp.bfloat16), "grp").astype(jnp.float32),
        lax.psum(row_sums[6].astype(jnp.bfloat16), "grp").astype(jnp.float32),
        lax.psum(row_sums[7].astype(jnp.bfloat16), "grp").astype(jnp.float32),
    )
    return (
        output,
        grad_tokens,
        totals[0],
        totals[1],
        totals[2],
        totals[3],
        totals[4],
        totals[5],
        totals[6],
        totals[7],
    )


def solution(mesh):
    in_specs = (
        P(("grp", "sp"), None, None),
        P("grp", None),
        P(),
        P(),
        P(),
        P(),
        P(),
        P(),
        P(),
        P(),
        P(("grp", "sp"), None, None),
    )
    out_specs = (
        P(("grp", "sp"), None, None),
        P(("grp", "sp"), None, None),
        P(None, "sp"),
        P(None, "sp"),
        P(None, "sp", None),
        P(None, "sp", None),
        P(None, "sp", None),
        P(None, "sp"),
        P(None, "sp", None),
        P(None, "sp"),
    )
    return jax.shard_map(shards, mesh=mesh, in_specs=in_specs, out_specs=out_specs, check_vma=False)
```

profile of v0, /device:TPU:0, one launch (start us, length us, event | category | flops | bytes accessed | tf_op | source)
XLA Modules:
  0.0 881.4 jit_solution(1106841932387299549)
XLA Ops:
  12.8 3.5 convolution_convert_fusion.1
  16.3 8.9 %reshape.446 = bf16[4,256,3,8,64]{4,3,2,1,0:T(8,128)(2,1)} reshape(bf16[1024,1536]{1,0:T(8,128)(2,1)} %convolution_convert_fusion.1) | data formatting | bytes 6291456 | tf_op jit(solution)/shard_map/reshape | solution.py:89
  25.1 5.7 fusion.132
  35.7 3.7 copy.147
  53.1 4.6 fusion.138
  59.4 7.9 all-to-all-start
  67.5 22.8 %all-to-all-done = bf16[4,256,512]{2,0,1:T(4,128)(2,1)S(1)} async-done(((bf16[4,256,512]{2,0,1:T(4,128)(2,1)}), bf16[4,256,512]{2,0,1:T(4,128)(2,1)S(1)}, u32[]{:S(2)}, u32[]{:S(2)}) %all-to-all-start) | async-done | bytes 1048608 | tf_op jit(solution)/shard_map/all_to_all | solution.py:179
  94.5 3.5 convolution_convert_fusion
  98.0 8.8 %reshape.415 = bf16[8,8,16,3,8,64]{5,4,3,2,1,0:T(8,128)(2,1)} reshape(bf16[1024,1536]{1,0:T(8,128)(2,1)} %convolution_convert_fusion) | data formatting | bytes 6291456 | tf_op jit(solution)/shard_map/reshape | solution.py:89
  106.9 5.5 fusion.131
  112.4 3.4 fusion.15
  122.4 4.0 dot_general.124
  128.5 31.5 %all_to_all.42 = bf16[64,16,512]{2,1,0:T(8,128)(2,1)S(1)} all-to-all(bf16[64,16,512]{2,1,0:T(8,128)(2,1)S(1)} %bitcast.348), channel_id=1, replica_groups=mesh['grp'=2,'sp'=16] {'sp'}, dimensions={0} | all-to-all | bytes 2097152 | tf_op jit(solution)/shard_map/all_to_all | solution.py:192
  164.8 6.1 multiply_convert_fusion.1
  170.9 8.0 fusion.139
  178.9 3.0 multiply_reduce_fusion.3
  185.7 5.3 all-to-all-start.2
  194.1 19.9 %all-to-all-done.2 = bf16[4,256,512]{2,0,1:T(4,128)(2,1)} async-done(((bf16[4,256,512]{2,0,1:T(4,128)(2,1)}), bf16[4,256,512]{2,0,1:T(4,128)(2,1)}, u32[]{:S(2)}, u32[]{:S(2)}) %all-to-all-start.2) | async-done | bytes 1048608 | tf_op jit(solution)/shard_map/all_to_all | solution.py:206
  218.3 3.9 reshape.420
  222.2 5.2 convert_bitcast_fusion.2
  227.5 3.7 multiply_reduce_fusion.2
  238.1 4.4 copy.114
  242.5 9.2 %convert_element_type.289 = bf16[1024,1536]{1,0:T(8,128)(2,1)} reshape(bf16[8,8,16,3,8,64]{5,4,3,2,1,0:T(8,128)(2,1)} %copy.114) | data formatting | bytes 6291456 | tf_op jit(solution)/shard_map/convert_element_type | solution.py:116
  251.7 6.5 multiply_reduce_fusion.4
  258.3 3.3 fusion.43
  261.6 7.0 all-to-all-start.3
  270.9 3.3 reshape.426
  277.1 3.0 fusion.17
  280.1 11.6 %all-to-all-done.3 = bf16[64,16,512]{2,1,0:T(8,128)(2,1)} async-done(((bf16[64,16,512]{2,1,0:T(8,128)(2,1)}), bf16[64,16,512]{2,1,0:T(8,128)(2,1)}, u32[]{:S(2)}, u32[]{:S(2)}) %all-to-all-start.3) | async-done | bytes 1048608 | tf_op jit(solution)/shard_map/all_to_all | solution.py:217
  297.4 9.7 %fusion.140 = (bf16[2048]{0:T(1024)(128)(2,1)S(1)}, bf16[1024,2048]{1,0:T(8,128)(2,1)S(1)}) fusion(f32[1024,2048]{1,0:T(8,128)} %copy-done.71, f32[2048]{0:T(1024)S(1)} %bitcast.380, bf16[1024,512]{1,0:T(8,128)(2,1)S(1)} %get-tuple-element.35, bf16[2,2048,512]{2,1,0:T(8,128)(2,1)S(1)} %copy-done.68), kind=kOutput, calls=%fused_computation.233 | convolution fusion | flops 2193618944 | bytes 15740928 | tf_op jit(solution)/shard_map/dot_general | solution.py:48
  307.2 3.4 multiply_reduce_fusion.5
  318.5 3.1 copy.117
  321.6 5.2 multiply_reduce_fusion
  326.8 4.8 multiply_convert_fusion
  345.6 4.7 fusion.21
  350.2 7.6 fusion.20
  360.8 5.5 fusion.19
  372.6 4.4 fusion.126
  381.4 6.8 add_convert_fusion.1
  388.2 57.1 %reduce-scatter.17.cloned.1.call-done = bf16[2,32,1536]{2,1,0:T(8,128)(2,1)} async-done(((bf16[2,512,1536]{2,1,0:T(8,128)(2,1)}), bf16[2,32,1536]{2,1,0:T(8,128)(2,1)}) %reduce-scatter.17.cloned.1.call-update) | async-done | bytes 196624 | tf_op jit(solution)/shard_map/reduce_scatter | solution.py:237
  445.4 76.1 %reduce-scatter.23.cloned.1.call-done = bf16[2,128,512]{2,1,0:T(8,128)(2,1)} async-done(((bf16[2,2048,512]{2,1,0:T(8,128)(2,1)}), bf16[2,128,512]{2,1,0:T(8,128)(2,1)}) %reduce-scatter.23.cloned.1.call-update) | async-done | bytes 262160 | tf_op jit(solution)/shard_map/reduce_scatter | solution.py:249
  521.5 75.1 %reduce-scatter.21.cloned.1.call-done = bf16[2,32,2048]{2,1,0:T(8,128)(2,1)} async-done(((bf16[2,512,2048]{2,1,0:T(8,128)(2,1)}), bf16[2,32,2048]{2,1,0:T(8,128)(2,1)}) %reduce-scatter.21.cloned.1.call-update) | async-done | bytes 262160 | tf_op jit(solution)/shard_map/reduce_scatter | solution.py:243
  599.5 55.6 %reduce-scatter.31.cloned.1.call-done = bf16[32,2]{1,0:T(8,128)(2,1)} async-done(((bf16[512,2]{1,0:T(8,128)(2,1)}), bf16[32,2]{1,0:T(8,128)(2,1)}) %reduce-scatter.31.cloned.1.call-update) | async-done | bytes 144
  655.9 57.6 %reduce-scatter.25.cloned.1.call-done = bf16[32,4]{1,0:T(8,128)(2,1)} async-done(((bf16[512,4]{1,0:T(8,128)(2,1)}), bf16[32,4]{1,0:T(8,128)(2,1)}) %reduce-scatter.25.cloned.1.call-update) | async-done | bytes 272
  714.3 57.8 %reduce-scatter.27.cloned.1.call-done = bf16[32,4]{1,0:T(8,128)(2,1)} async-done(((bf16[512,4]{1,0:T(8,128)(2,1)}), bf16[32,4]{1,0:T(8,128)(2,1)}) %reduce-scatter.27.cloned.1.call-update) | async-done | bytes 272
  772.9 58.6 %reduce-scatter.29.cloned.1.call-done = bf16[128,2]{1,0:T(8,128)(2,1)} async-done(((bf16[2048,2]{1,0:T(8,128)(2,1)}), bf16[128,2]{1,0:T(8,128)(2,1)}) %reduce-scatter.29.cloned.1.call-update) | async-done | bytes 528
  832.3 4.9 all-reduce
  839.5 28.4 %all-reduce.4.cloned.1.call-done = (bf16[2,32,1536]{2,1,0:T(8,128)(2,1)}, bf16[2,32,512]{2,1,0:T(8,128)(2,1)}, bf16[2,32,2048]{2,1,0:T(8,128)(2,1)}, bf16[2,128,512]{2,1,0:T(8,128)(2,1)}) async-done(((bf16[2,32,1536]{2,1,0:T(8,128)(2,1)}, bf16[2,32,512]{2,1,0:T(8,128)(2,1)}, bf16[2,32,2048]{2,1,0:T(8,128)(2,1)}, bf16[2,128,512]{2,1,0:T(8,128)(2,1)}), (bf16[2,32,1536]{2,1,0:T(8,128)(2,1)}, ...) | async-done | bytes 786448 | tf_op jit(solution)/shard_map/psum | solution.py:259
  (300 shorter events, 122.4 us)
Async XLA Ops:
  7.2 4.1 copy-start.3
  7.2 4.0 copy-start.57
  7.2 4.0 copy-start.58
  7.2 4.0 copy-start.54
  7.2 5.5 copy-start.69
  11.2 37.0 %copy-start.52 = (f32[1,512]{1,0:T(1,128)}, f32[1,512]{1,0:T(1,128)S(1)}, u32[]{:S(2)}) copy-start(f32[1,512]{1,0:T(1,128)S(1)} %get-tuple-element.50) | copy-start | bytes 6148
  11.2 37.0 %copy-start.55 = (f32[1,512]{1,0:T(1,128)}, f32[1,512]{1,0:T(1,128)S(1)}, u32[]{:S(2)}) copy-start(f32[1,512]{1,0:T(1,128)S(1)} %get-tuple-element.54) | copy-start | bytes 6148
  11.2 151.4 %copy-start.61 = (f32[1,512]{1,0:T(1,128)}, f32[1,512]{1,0:T(1,128)S(1)}, u32[]{:S(2)}) copy-start(f32[1,512]{1,0:T(1,128)S(1)} %get-tuple-element.53) | copy-start | bytes 6148
  33.0 6.3 copy-start.16
  35.7 7.8 copy-start.12
  47.8 259.3 %copy-start.5 = (f32[4,256,512]{2,1,0:T(8,128)}, f32[4,256,512]{2,1,0:T(8,128)S(1)}, u32[]{:S(2)}) copy-start(f32[4,256,512]{2,1,0:T(8,128)S(1)} %get-tuple-element.66) | copy-start | bytes 6291460
  53.1 4.6 copy-start.71
  57.7 9.7 %copy-start.49 = (s32[8,8]{1,0:T(8,128)S(1)}, s32[8,8]{1,0:T(8,128)}, u32[]{:S(2)}) copy-start(s32[8,8]{1,0:T(8,128)} %param.12) | copy-start | bytes 772
  59.4 30.9 %all-to-all-start = ((bf16[4,256,512]{2,0,1:T(4,128)(2,1)}), bf16[4,256,512]{2,0,1:T(4,128)(2,1)S(1)}, u32[]{:S(2)}, u32[]{:S(2)}) async-start(bf16[4,256,512]{2,0,1:T(4,128)(2,1)} %copy.100), calls=%async_computation | async-start | bytes 2097152 | tf_op jit(solution)/shard_map/all_to_all | solution.py:179
  112.4 5.6 copy-start.10
  162.2 19.7 %copy-start.6 = (f32[1024,512]{1,0:T(8,128)}, f32[1024,512]{1,0:T(8,128)S(1)}, u32[]{:S(2)}) copy-start(f32[1024,512]{1,0:T(8,128)S(1)} %get-tuple-element.39) | copy-start | bytes 6291460
  164.8 6.1 copy-start.25
  164.8 6.1 copy-start.67
  185.7 28.2 %all-to-all-start.2 = ((bf16[4,256,512]{2,0,1:T(4,128)(2,1)}), bf16[4,256,512]{2,0,1:T(4,128)(2,1)}, u32[]{:S(2)}, u32[]{:S(2)}) async-start(bf16[4,256,512]{2,0,1:T(4,128)(2,1)} %copy.108), calls=%async_computation.2 | async-start | bytes 2097152 | tf_op jit(solution)/shard_map/all_to_all | solution.py:206
  222.2 5.3 copy-start.2
  222.2 5.3 copy-start.9
  222.2 5.3 copy-start.11
  261.6 7.1 copy-start.20
  261.6 30.1 %all-to-all-start.3 = ((bf16[64,16,512]{2,1,0:T(8,128)(2,1)}), bf16[64,16,512]{2,1,0:T(8,128)(2,1)}, u32[]{:S(2)}, u32[]{:S(2)}) async-start(bf16[64,16,512]{2,1,0:T(8,128)(2,1)} %fusion.43), calls=%async_computation.3 | async-start | bytes 2097152 | tf_op jit(solution)/shard_map/all_to_all | solution.py:217
  268.7 119.5 %reduce-scatter.19.cloned.1.call-start = ((), (), s32[]{:S(2)}) async-start(), calls=%async_computation.13 | async-start | bytes 1114112 | tf_op jit(solution)/shard_map/reduce_scatter | solution.py:240
  295.4 11.7 %copy-start.40 = (bf16[1024,512]{1,0:T(8,128)(2,1)}, bf16[1024,512]{1,0:T(8,128)(2,1)S(1)}, u32[]{:S(2)}) copy-start(bf16[1024,512]{1,0:T(8,128)(2,1)S(1)} %get-tuple-element.35) | copy-start | bytes 3145732
  297.4 9.8 %copy-start.53 = (f32[1,512]{1,0:T(1,128)S(1)}, f32[1,512]{1,0:T(1,128)}, u32[]{:S(2)}) copy-start(f32[1,512]{1,0:T(1,128)} %copy-done.52) | copy-start | bytes 6148
  297.4 9.8 %copy-start.56 = (f32[1,512]{1,0:T(1,128)S(1)}, f32[1,512]{1,0:T(1,128)}, u32[]{:S(2)}) copy-start(f32[1,512]{1,0:T(1,128)} %copy-done.55) | copy-start | bytes 6148
  297.4 9.8 %copy-start.65 = (bf16[2,512,2048]{2,1,0:T(8,128)(2,1)S(1)}, bf16[2,512,2048]{2,1,0:T(8,128)(2,1)}, u32[]{:S(2)}) copy-start(bf16[2,512,2048]{2,1,0:T(8,128)(2,1)} %param.17) | copy-start | bytes 12582916
  307.1 3.5 copy-start.72
  316.1 129.3 %reduce-scatter.17.cloned.1.call-start = ((), (), s32[]{:S(2)}) async-start(), calls=%async_computation.12 | async-start | bytes 3342336 | tf_op jit(solution)/shard_map/reduce_scatter | solution.py:237
  321.6 12.3 %slice-start = ((s8[8388608]{0:T(1024)(128)(4,1)}), s8[4194304]{0:T(1024)(128)(4,1)S(1)}, s32[]{:S(2)}) async-start(s8[8388608]{0:T(1024)(128)(4,1)} %bitcast.321), calls=%async_computation.21 | async-start | bytes 8388608
  326.8 4.8 copy-start.17
  326.8 7.1 slice-start.1
  344.4 177.2 %reduce-scatter.23.cloned.1.call-start = ((), (), s32[]{:S(2)}) async-start(), calls=%async_computation.15 | async-start | bytes 4456448 | tf_op jit(solution)/shard_map/reduce_scatter | solution.py:249
  345.6 4.7 copy-start.41
  360.2 236.4 %reduce-scatter.21.cloned.1.call-start = ((), (), s32[]{:S(2)}) async-start(), calls=%async_computation.14 | async-start | bytes 4456448 | tf_op jit(solution)/shard_map/reduce_scatter | solution.py:243
  360.8 5.6 copy-start.73
  360.8 5.6 copy-start.74
  371.2 283.9 %reduce-scatter.31.cloned.1.call-start = ((), (), s32[]{:S(2)}) async-start(), calls=%async_computation.19 | async-start | bytes 139264
  372.6 4.4 copy-start.4
  372.6 4.4 copy-start.46
  372.6 4.4 copy-start.48
  377.0 4.4 copy-start.60
  378.3 335.2 %reduce-scatter.25.cloned.1.call-start = ((), (), s32[]{:S(2)}) async-start(), calls=%async_computation.16 | async-start | bytes 139264
  379.2 392.8 %reduce-scatter.27.cloned.1.call-start = ((), (), s32[]{:S(2)}) async-start(), calls=%async_computation.17 | async-start | bytes 139264
  380.2 451.3 %reduce-scatter.29.cloned.1.call-start = ((), (), s32[]{:S(2)}) async-start(), calls=%async_computation.18 | async-start | bytes 557056
  381.3 486.5 %all-reduce.4.cloned.1.call-start = ((), (), s32[]{:S(2)}) async-start(), calls=%async_computation.20 | async-start | bytes 1572864 | tf_op jit(solution)/shard_map/psum | solution.py:259
  (42 other events, 82.9 us)
Sparse Core Ops, SparseCore 0:
  316.2 59.5 reduce-scatter.18
  380.1 65.2 reduce-scatter.16
  449.7 71.7 reduce-scatter.22
  525.2 71.3 reduce-scatter.20
  600.9 54.1 reduce-scatter.30
  659.4 54.0 reduce-scatter.24
  717.9 54.0 reduce-scatter.26
  776.6 54.7 reduce-scatter.28
  833.9 33.8 all-reduce.3
where the time goes:
time: 888 us; the launch traced here: 881 us
  waiting for transfers between devices  521 us (59%)
  matrix products  128 us (14%)
  local copies, waits for them, and re-layouts  110 us (12%)
  other arithmetic  50.5 us (6%)
  blocking collectives  36.5 us (4%)
  starting transfers between devices  21.2 us (2%)
  between operations  15.4 us (2%)
    unnamed x13, waiting for transfers between devices  230 us
    reduce_scatter x1, waiting for transfers between devices, shards(): lax.psum_scatter(joined[6].astype(jnp.bfloat16), 'sp', scatter_dimension=...  76.1 us
    reduce_scatter x1, waiting for transfers between devices, shards(): lax.psum_scatter(joined[4].astype(jnp.bfloat16), 'sp', scatter_dimension=...  75.1 us
    reduce_scatter x1, waiting for transfers between devices, shards(): lax.psum_scatter(joined[2].astype(jnp.bfloat16), 'sp', scatter_dimension=...  57.1 us
    dot_general x8, matrix products, back_dot(): lax.dot_general(grad_rows, weight, (((1,), (1,)), ((), ())), preferred_el...  37.3 us
    unnamed x171, local copies, waits for them, and re-layouts  35.3 us
    all_to_all x1, blocking collectives, shards(): lax.all_to_all(time_low, 'sp', split_axis=0, concat_axis=1, tiled=True)  31.5 us
    dot_general x8, matrix products, matmul(): return jnp.dot(left, right, preferred_element_type=jnp.float32)  29.7 us
  transfers between devices with their start and end apart: 12, of which 11 were waited for; matrix products, arithmetic and copies ran while one was open for 10% of the time, Pallas kernels for 0%

commit v1 on v0

v1 whole, which is shorter than its diff:
```python
import functools

import jax
import jax.numpy as jnp
from jax import lax
from jax.experimental import pallas as pl
from jax.experimental.pallas import tpu as pltpu
from jax.sharding import PartitionSpec as P

HEADS = 8
HEAD = 64
VIDEO_STEPS = 6
GROUP_FRAMES = 8
NORM_EPS = 1e-05
TILE = 512
SCALE = HEAD**-0.5
TANH_A = 0.7978845608028654
TANH_B = TANH_A * 0.044715
PAIRS = [(t, s) for t in range(VIDEO_STEPS) for s in range(t + 1)]
F32 = jnp.float32
BF16 = jnp.bfloat16
MIB = 1024 * 1024


def dot(left, right):
    return jnp.dot(left, right, preferred_element_type=F32)


def dot_nt(left, right):
    return lax.dot_general(left, right, (((1,), (1,)), ((), ())), preferred_element_type=F32)


def dot_tn(left, right):
    return lax.dot_general(left, right, (((0,), (0,)), ((), ())), preferred_element_type=F32)


def norm(rows, gain, shift):
    centred = rows - jnp.mean(rows, axis=-1, keepdims=True)
    inv = lax.rsqrt(jnp.mean(centred * centred, axis=-1, keepdims=True) + NORM_EPS)
    unit = centred * inv
    return unit * gain + shift, unit, inv


def norm_back(grad, unit, inv, gain):
    grad_unit = grad * gain
    mean_grad = jnp.mean(grad_unit, axis=-1, keepdims=True)
    mean_both = jnp.mean(grad_unit * unit, axis=-1, keepdims=True)
    return inv * (grad_unit - mean_grad - unit * mean_both)


def column_sum(rows):
    return jnp.sum(rows, axis=0, keepdims=True)


def gelu_pair(u):
    square = u * u
    t = jnp.tanh(u * (TANH_A + TANH_B * square))
    half = 0.5 * u
    act = half + half * t
    slope = 0.5 + 0.5 * t + half * (1.0 - t * t) * (TANH_A + 3.0 * TANH_B * square)
    return act.astype(BF16), slope.astype(BF16)


def head_mask(lanes, which):
    lane = lax.broadcasted_iota(jnp.int32, lanes.shape, 1)
    return (lane < HEAD) if which == 0 else (lane >= HEAD)


def qkv_rows(normed, weight):
    out = []
    for part in range(3):
        piece = dot(normed, weight[:, part * TILE : (part + 1) * TILE])
        if part == 0:
            out.append(piece.astype(BF16) * BF16(SCALE))
        else:
            out.append(piece.astype(BF16))
    return out


def mlp_forward(normed, w_up, b_up, w_down, act_ref, slope_ref):
    total = None
    for j in range(w_up.shape[1] // TILE):
        cols = slice(j * TILE, (j + 1) * TILE)
        u = dot(normed, w_up[:, cols]) + b_up[:, cols]
        act, slope = gelu_pair(u)
        act_ref[:, cols] = act
        slope_ref[:, cols] = slope
        piece = dot(act, w_down[cols, :])
        total = piece if total is None else total + piece
    return total


def mlp_backward(grad_low, w_up, w_down, slope_ref, du_ref, small_ref):
    total = None
    for j in range(w_up.shape[1] // TILE):
        cols = slice(j * TILE, (j + 1) * TILE)
        du = (dot_nt(grad_low, w_down[cols, :]) * slope_ref[:, cols].astype(F32)).astype(BF16)
        du_ref[:, cols] = du
        small_ref[4 + j : 5 + j, :] += column_sum(du.astype(F32))
        piece = dot_nt(du, w_up[:, cols])
        total = piece if total is None else total + piece
    return total


def clear_first(small_ref):
    @pl.when(pl.program_id(0) == 0)
    def _():
        small_ref[...] = jnp.zeros_like(small_ref)


def space_forward_kernel(
    tok_ref, gain_ref, shift_ref, wqkv_ref, wout_ref, wup_ref, bup_ref, wdown_ref, bdown_ref,
    keep_ref, send_ref, h0_ref, qkv_ref, lse_ref, o_ref, xa_ref, h1_ref, act_ref, slope_ref,
    x1_scr,
):
    part = lax.rem(lax.axis_index("sp"), 2)
    x0 = tok_ref[0].astype(F32)
    rows = x0.shape[0]
    h0 = norm(x0, gain_ref[0:1, :], shift_ref[0:1, :])[0].astype(BF16)
    h0_ref[0] = h0
    q, k, v = qkv_rows(h0, wqkv_ref[0])
    qkv_ref[0, :, 0:TILE] = q
    qkv_ref[0, :, TILE : 2 * TILE] = k
    qkv_ref[0, :, 2 * TILE :] = v
    lane = lax.broadcasted_iota(jnp.int32, (rows, 128), 1)
    lse_all = jnp.zeros((rows, 128), F32)
    mixed = []
    for pair in range(HEADS // 2):
        cols = slice(pair * 128, (pair + 1) * 128)
        qp, kp, vp = q[:, cols], k[:, cols], v[:, cols]
        both = []
        for e in range(2):
            s = dot_nt(jnp.where(head_mask(qp, e), qp, jnp.zeros_like(qp)), kp)
            top = jnp.max(s, axis=-1, keepdims=True)
            p = jnp.exp(s - top)
            total = jnp.sum(p, axis=-1, keepdims=True)
            both.append(dot(p.astype(BF16), vp) * (1.0 / total))
            lse_all = jnp.where(lane == 2 * pair + e, top + jnp.log(total), lse_all)
        mixed.append(jnp.where(head_mask(both[0], 0), both[0], both[1]).astype(BF16))
    lse_ref[0] = jnp.transpose(lse_all)[0:HEADS, :]
    o = jnp.concatenate(mixed, axis=1)
    o_ref[0] = o
    xa = x0 + dot(o, wout_ref[0])
    xa_ref[0] = xa
    h1 = norm(xa, gain_ref[1:2, :], shift_ref[1:2, :])[0].astype(BF16)
    h1_ref[0] = h1
    branch = mlp_forward(h1, wup_ref[0], bup_ref[0:1, :], wdown_ref[0], act_ref.at[0], slope_ref.at[0])
    x1_scr[...] = xa + branch + bdown_ref[0:1, :]
    half = rows // 2
    keep_ref[0] = x1_scr[pl.ds(pl.multiple_of(part * half, half), half), :].astype(BF16)
    send_ref[0] = x1_scr[pl.ds(pl.multiple_of((1 - part) * half, half), half), :].astype(BF16)


def pick_rows(where_ref, both_scr, step_rows):
    return jnp.concatenate([both_scr[where_ref[s]] for s in range(GROUP_FRAMES)], axis=0)


def lane_heads(dtype):
    c = lax.broadcasted_iota(jnp.int32, (TILE, 128), 0)
    h = lax.broadcasted_iota(jnp.int32, (TILE, 128), 1)
    return (c // HEAD == h).astype(dtype)


def slot_places(slots_ref, where_scr, frames):
    sp = lax.axis_index("sp")
    group = (sp * frames) // GROUP_FRAMES
    part = lax.rem(sp, GROUP_FRAMES // frames)
    for t in range(GROUP_FRAMES):
        where_scr[slots_ref[group, t]] = lax.rem(t + GROUP_FRAMES - part * frames, GROUP_FRAMES)


def time_scores(q, k, spread, count):
    parts = []
    for t, s in PAIRS:
        parts.append((q[t] * k[s]).astype(BF16))
    return dot(jnp.concatenate(parts, axis=0), spread)


def time_probs(scores, count):
    blocks = [scores[i * count : (i + 1) * count] for i in range(len(PAIRS))]
    probs = []
    at = 0
    for t in range(VIDEO_STEPS):
        mine = blocks[at : at + t + 1]
        at += t + 1
        top = functools.reduce(jnp.maximum, mine)
        raw = [jnp.exp(b - top) for b in mine]
        inv = 1.0 / functools.reduce(lambda a, b: a + b, raw)
        probs.extend([r * inv for r in raw])
    return probs


def time_forward_kernel(
    slots_ref, keep_ref, recv_ref, cot_ref, cotr_ref, gain_ref, shift_ref,
    wqkv_ref, wout_ref, wup_ref, bup_ref, wdown_ref, bdown_ref,
    own_ref, send_ref, x_ref, h2_ref, qkv_ref, o_ref, h3_ref, act_ref, du_ref, gr_ref, dxb_ref,
    small_ref,
    where_scr, both_scr, slope_scr,
):
    frames = keep_ref.shape[0]
    count = keep_ref.shape[1]
    step = pl.program_id(0)
    part = lax.rem(lax.axis_index("sp"), GROUP_FRAMES // frames)
    clear_first(small_ref)

    @pl.when(step == 0)
    def _():
        slot_places(slots_ref, where_scr, frames)

    both_scr[0:frames] = keep_ref[...]
    both_scr[frames:] = recv_ref[...]
    x_low = pick_rows(where_scr, both_scr, count)
    x_ref[...] = x_low
    x = x_low.astype(F32)
    h2 = norm(x, gain_ref[2:3, :], shift_ref[2:3, :])[0].astype(BF16)
    h2_ref[...] = h2
    q, k, v = qkv_rows(h2, wqkv_ref[0])
    qkv_ref[:, 0:TILE] = q
    qkv_ref[:, TILE : 2 * TILE] = k
    qkv_ref[:, 2 * TILE :] = v

    def split(rows):
        return [rows[s * count : (s + 1) * count].astype(F32) for s in range(GROUP_FRAMES)]

    qs, ks, vs = split(q), split(k), split(v)
    spread = lane_heads(BF16)
    probs = time_probs(time_scores(qs, ks, spread, count), count)
    wide = dot_nt(jnp.concatenate([p.astype(BF16) for p in probs], axis=0), spread)
    mixed = []
    at = 0
    for t in range(VIDEO_STEPS):
        total = None
        for s in range(t + 1):
            piece = wide[at * count : (at + 1) * count] * vs[s]
            total = piece if total is None else total + piece
            at += 1
        mixed.append(total)
    mixed.extend(vs[VIDEO_STEPS:])
    o = jnp.concatenate([m.astype(BF16) for m in mixed], axis=0)
    o_ref[...] = o
    xb = x + dot(o, wout_ref[0]).astype(BF16).astype(F32)
    h3, unit, inv = norm(xb, gain_ref[3:4, :], shift_ref[3:4, :])
    h3 = h3.astype(BF16)
    h3_ref[...] = h3
    branch = mlp_forward(h3, wup_ref[0], bup_ref[1:2, :], wdown_ref[0], act_ref, slope_scr)
    out = (xb + branch + bdown_ref[1:2, :]).astype(BF16)
    for s in range(GROUP_FRAMES):
        both_scr[where_scr[s]] = out[s * count : (s + 1) * count]
    own_ref[...] = both_scr[0:frames]
    send_ref[...] = both_scr[frames:]

    places = pl.ds(pl.multiple_of(part * (cot_ref.shape[1] // 2) + step * count, count), count)
    both_scr[0:frames] = cot_ref[:, places, :]
    both_scr[frames:] = cotr_ref[:, places, :]
    grad_low = pick_rows(where_scr, both_scr, count)
    gr_ref[...] = grad_low
    grad = grad_low.astype(F32)
    dh = mlp_backward(grad_low, wup_ref[0], wdown_ref[0], slope_scr, du_ref, small_ref)
    small_ref[0:1, :] += column_sum(dh * unit)
    small_ref[1:2, :] += column_sum(dh)
    small_ref[2:3, :] += column_sum(grad)
    dxb_ref[...] = grad + norm_back(dh, unit, inv, gain_ref[3:4, :])


def time_backward_kernel(
    slots_ref, x_ref, qkv_ref, dxb_ref, gain_ref, shift_ref, wqkv_ref, wout_ref,
    own_ref, send_ref, ar_ref, dqkv_ref, small_ref,
    where_scr, both_scr,
):
    frames = own_ref.shape[0]
    count = own_ref.shape[1]
    clear_first(small_ref)

    @pl.when(pl.program_id(0) == 0)
    def _():
        slot_places(slots_ref, where_scr, frames)

    def split(rows):
        return [rows[s * count : (s + 1) * count].astype(F32) for s in range(GROUP_FRAMES)]

    dxb = dxb_ref[...]
    ar = dxb.astype(BF16)
    ar_ref[...] = ar
    do = split(dot_nt(ar, wout_ref[0]).astype(BF16))
    qs = split(qkv_ref[:, 0:TILE])
    ks = split(qkv_ref[:, TILE : 2 * TILE])
    vs = split(qkv_ref[:, 2 * TILE :])
    spread = lane_heads(BF16)
    probs = time_probs(time_scores(qs, ks, spread, count), count)
    dps = time_scores(do, vs, spread, count)
    dps = [dps[i * count : (i + 1) * count] for i in range(len(PAIRS))]
    dss = []
    at = 0
    for t in range(VIDEO_STEPS):
        centre = functools.reduce(
            lambda a, b: a + b, [probs[at + s] * dps[at + s] for s in range(t + 1)]
        )
        dss.extend([probs[at + s] * (dps[at + s] - centre) for s in range(t + 1)])
        at += t + 1
    wide_p = dot_nt(jnp.concatenate([p.astype(BF16) for p in probs], axis=0), spread)
    wide_ds = dot_nt(jnp.concatenate([d.astype(BF16) for d in dss], axis=0), spread)
    dq = [None] * GROUP_FRAMES
    dk = [None] * GROUP_FRAMES
    dv = [None] * GROUP_FRAMES

    def add(table, index, piece):
        table[index] = piece if table[index] is None else table[index] + piece

    for i, (t, s) in enumerate(PAIRS):
        rows = slice(i * count, (i + 1) * count)
        add(dq, t, wide_ds[rows] * ks[s])
        add(dk, s, wide_ds[rows] * qs[t])
        add(dv, s, wide_p[rows] * do[t])
    for t in range(VIDEO_STEPS, GROUP_FRAMES):
        dq[t] = jnp.zeros_like(do[t])
        dk[t] = jnp.zeros_like(do[t])
        dv[t] = do[t]
    dq = jnp.concatenate([(d * SCALE).astype(BF16) for d in dq], axis=0)
    dk = jnp.concatenate([d.astype(BF16) for d in dk], axis=0)
    dv = jnp.concatenate([d.astype(BF16) for d in dv], axis=0)
    dqkv_ref[:, 0:TILE] = dq
    dqkv_ref[:, TILE : 2 * TILE] = dk
    dqkv_ref[:, 2 * TILE :] = dv
    dh = (
        dot_nt(dq, wqkv_ref[0, :, 0:TILE])
        + dot_nt(dk, wqkv_ref[0, :, TILE : 2 * TILE])
        + dot_nt(dv, wqkv_ref[0, :, 2 * TILE :])
    )
    gain = gain_ref[2:3, :]
    unit, inv = norm(x_ref[...].astype(F32), gain, shift_ref[2:3, :])[1:]
    small_ref[0:1, :] += column_sum(dh * unit)
    small_ref[1:2, :] += column_sum(dh)
    dxp = norm_back(dh, unit, inv, gain).astype(BF16).astype(F32)
    dx1 = (dxb + dxp).astype(BF16)
    for s in range(GROUP_FRAMES):
        both_scr[where_scr[s]] = dx1[s * count : (s + 1) * count]
    own_ref[...] = both_scr[0:frames]
    send_ref[...] = both_scr[frames:]


def space_mlp_back_kernel(
    own_ref, recv_ref, xa_ref, slope_ref, gain_ref, shift_ref, wup_ref, wdown_ref,
    gr_ref, du_ref, dxa_ref, small_ref,
):
    part = lax.rem(lax.axis_index("sp"), 2)
    clear_first(small_ref)
    half = own_ref.shape[1]
    gr_ref[0, pl.ds(pl.multiple_of(part * half, half), half), :] = own_ref[0]
    gr_ref[0, pl.ds(pl.multiple_of((1 - part) * half, half), half), :] = recv_ref[0]
    grad_low = gr_ref[0]
    grad = grad_low.astype(F32)
    dh = mlp_backward(grad_low, wup_ref[0], wdown_ref[0], slope_ref.at[0], du_ref.at[0], small_ref)
    gain = gain_ref[1:2, :]
    unit, inv = norm(xa_ref[0], gain, shift_ref[1:2, :])[1:]
    small_ref[0:1, :] += column_sum(dh * unit)
    small_ref[1:2, :] += column_sum(dh)
    small_ref[2:3, :] += column_sum(grad)
    dxa_ref[0] = grad + norm_back(dh, unit, inv, gain)


def space_attn_back_kernel(
    tok_ref, dxa_ref, qkv_ref, lse_ref, o_ref, own_ref, recv_ref, gain_ref, shift_ref, wqkv_ref,
    wout_ref, ar_ref, dqkv_ref, gtok_ref, out_ref, small_ref,
):
    part = lax.rem(lax.axis_index("sp"), 2)
    clear_first(small_ref)
    half = own_ref.shape[1]
    out_ref[0, pl.ds(pl.multiple_of(part * half, half), half), :] = own_ref[0]
    out_ref[0, pl.ds(pl.multiple_of((1 - part) * half, half), half), :] = recv_ref[0]
    dxa = dxa_ref[0]
    ar = dxa.astype(BF16)
    ar_ref[0] = ar
    do = dot_nt(ar, wout_ref[0]).astype(BF16)
    both = do.astype(F32) * o_ref[0].astype(F32)
    high = both.astype(BF16)
    rest = (both - high.astype(F32)).astype(BF16)
    h = lax.broadcasted_iota(jnp.int32, (HEADS, TILE), 0)
    c = lax.broadcasted_iota(jnp.int32, (HEADS, TILE), 1)
    pick = (c // HEAD == h).astype(BF16)
    centre = dot_nt(pick, high) + dot_nt(pick, rest)
    dq, dk, dv = [], [], []
    for pair in range(HEADS // 2):
        cols = slice(pair * 128, (pair + 1) * 128)
        qp = qkv_ref[0, :, pair * 128 : (pair + 1) * 128]
        kp = qkv_ref[0, :, TILE + pair * 128 : TILE + (pair + 1) * 128]
        vp = qkv_ref[0, :, 2 * TILE + pair * 128 : 2 * TILE + (pair + 1) * 128]
        dop = do[:, cols]
        parts = []
        for e in range(2):
            row = slice(2 * pair + e, 2 * pair + e + 1)
            mask = head_mask(kp, e)
            zero = jnp.zeros_like(kp)
            st = dot_nt(jnp.where(mask, kp, zero), qp)
            pt = jnp.exp(st - lse_ref[0, row, :])
            dpt = dot_nt(jnp.where(mask, vp, zero), dop)
            dst = (pt * (dpt - centre[row, :])).astype(BF16)
            parts.append((dot_tn(dst, kp) * SCALE, dot(dst, qp), dot(pt.astype(BF16), dop)))
        mask = head_mask(parts[0][0], 0)
        for table, index in ((dq, 0), (dk, 1), (dv, 2)):
            table.append(jnp.where(mask, parts[0][index], parts[1][index]).astype(BF16))
    dh = None
    for index, table in enumerate((dq, dk, dv)):
        whole = jnp.concatenate(table, axis=1)
        cols = slice(index * TILE, (index + 1) * TILE)
        dqkv_ref[0, :, cols] = whole
        piece = dot_nt(whole, wqkv_ref[0, :, cols])
        dh = piece if dh is None else dh + piece
    gain = gain_ref[0:1, :]
    unit, inv = norm(tok_ref[0].astype(F32), gain, shift_ref[0:1, :])[1:]
    small_ref[0:1, :] += column_sum(dh * unit)
    small_ref[1:2, :] += column_sum(dh)
    gtok_ref[0] = (dxa + norm_back(dh, unit, inv, gain)).astype(BF16)


def place_of(block, order, sp):
    bits = len(order)
    mixed = jnp.bitwise_xor(block, sp)
    slot = jnp.int32(0)
    for i, b in enumerate(order):
        bit = jnp.bitwise_and(lax.shift_right_logical(mixed, jnp.int32(b)), 1)
        slot = slot + lax.shift_left(bit, jnp.int32(bits - 1 - i))
    return slot


def put_blocks(result, first, size, at, order, keep_ref, send_ref):
    sp = lax.axis_index("sp")
    part = lax.rem(sp, 2)
    low = result.astype(BF16)
    for j in range(result.shape[0] // (2 * size)):
        even = low[2 * j * size : (2 * j + 1) * size]
        odd = low[(2 * j + 1) * size : (2 * j + 2) * size]
        slot = place_of(first + 2 * j, order[1:], sp)
        keep_ref[slot, at : at + size, :] = jnp.where(part == 0, even, odd)
        send_ref[slot, at : at + size, :] = jnp.where(part == 0, odd, even)


def mlp_weights_kernel(order, h_ref, du_ref, act_ref, gr_ref, keep_ref, send_ref):
    slots = 2 * keep_ref.shape[0]
    up_size = h_ref.shape[1] // slots
    chunks = 4
    down_size = chunks * TILE // slots
    j = pl.program_id(0)
    up = dot_tn(h_ref[...], du_ref[...])
    at = pl.multiple_of(j * up_size, up_size)
    sp = lax.axis_index("sp")
    part = lax.rem(sp, 2)
    low = up.astype(BF16)
    for i in range(slots // 2):
        even = low[2 * i * up_size : (2 * i + 1) * up_size]
        odd = low[(2 * i + 1) * up_size : (2 * i + 2) * up_size]
        slot = place_of(jnp.int32(2 * i), order[1:], sp)
        keep_ref[slot, pl.ds(at, up_size), :] = jnp.where(part == 0, even, odd)
        send_ref[slot, pl.ds(at, up_size), :] = jnp.where(part == 0, odd, even)
    down = dot_tn(act_ref[...], gr_ref[...])
    put_blocks(down, j * (TILE // down_size), down_size, chunks * up_size, order, keep_ref, send_ref)


def attn_weights_kernel(order, h_ref, dqkv_ref, o_ref, ar_ref, keep_ref, send_ref):
    size = h_ref.shape[1] // (2 * keep_ref.shape[0])
    zero = jnp.int32(0)
    for j in range(3):
        cols = slice(j * TILE, (j + 1) * TILE)
        put_blocks(dot_tn(h_ref[...], dqkv_ref[:, cols]), zero, size, j * size, order, keep_ref, send_ref)
    put_blocks(dot_tn(o_ref[...], ar_ref[...]), zero, size, 3 * size, order, keep_ref, send_ref)


def whole_spec(array):
    rank = len(array.shape)
    return pl.BlockSpec(array.shape, lambda i: (0,) * rank)


def layer_spec(array, layer):
    return pl.BlockSpec((1,) + array.shape[1:], lambda i: (layer,) + (0,) * (len(array.shape) - 1))


def step_spec(shape, axis=0):
    rank = len(shape)
    return pl.BlockSpec(shape, lambda i: (0,) * axis + (i,) + (0,) * (rank - axis - 1))


def params(limit_mib):
    return pltpu.CompilerParams(dimension_semantics=("arbitrary",), vmem_limit_bytes=limit_mib * MIB)


def cost(flops, read):
    return pl.CostEstimate(flops=int(flops), bytes_accessed=int(read), transcendentals=0)


def sds(shape, dtype):
    return jax.ShapeDtypeStruct(shape, dtype)


def add_low(a, b):
    return (a.astype(F32) + b.astype(F32)).astype(BF16)


def swap(array, axis, size, bit):
    return lax.ppermute(array, axis, [(i, i ^ (1 << bit)) for i in range(size)])


def sum_scatter(keep, send, order, sp_size, grp_size):
    recv = swap(send, "sp", sp_size, order[0])
    for b in order[1:]:
        half = keep.shape[0] // 2
        send = add_low(keep[half:], recv[half:])
        keep = add_low(keep[:half], recv[:half])
        recv = swap(send, "sp", sp_size, b)
    now = add_low(keep, recv)
    for b in range(grp_size.bit_length() - 1):
        now = add_low(now, swap(now, "grp", grp_size, b))
    return now[0].astype(F32)


def shards(sizes, tokens, frame_slot, norm_gain, norm_shift, w_qkv, w_out, w_up, b_up, w_down, b_down, cotangent):
    grp_size, sp_size = sizes
    frames, patches, width = tokens.shape
    hidden = w_up.shape[2]
    assert GROUP_FRAMES == 2 * frames
    half = patches // 2
    rows = frames * patches
    sp_bits = sp_size.bit_length() - 1
    core_swap = functools.partial(swap, axis="sp", size=sp_size, bit=0)
    macs = rows * width

    cot_recv = core_swap(cotangent)

    def frame_out(cols, dtype):
        return sds((frames, patches, cols), dtype)

    frame_block = lambda cols: step_spec((1, patches, cols))
    half_block = step_spec((1, half, width))
    (x_keep, x_send, h0, qkv0, lse0, o0, xa, h1, act0, slope0) = pl.pallas_call(
        space_forward_kernel,
        grid=(frames,),
        in_specs=[
            frame_block(width), whole_spec(norm_gain), whole_spec(norm_shift), layer_spec(w_qkv, 0),
            layer_spec(w_out, 0), layer_spec(w_up, 0), whole_spec(b_up), layer_spec(w_down, 0),
            whole_spec(b_down),
        ],
        out_specs=[
            half_block, half_block, frame_block(width), frame_block(3 * width),
            step_spec((1, HEADS, patches)), frame_block(width), frame_block(width),
            frame_block(width), frame_block(hidden), frame_block(hidden),
        ],
        out_shape=[
            sds((frames, half, width), BF16), sds((frames, half, width), BF16), frame_out(width, BF16),
            frame_out(3 * width, BF16), sds((frames, HEADS, patches), F32), frame_out(width, BF16),
            frame_out(width, F32), frame_out(width, BF16), frame_out(hidden, BF16),
            frame_out(hidden, BF16),
        ],
        scratch_shapes=[pltpu.VMEM((patches, width), F32)],
        compiler_params=params(56),
        cost_estimate=cost(2 * macs * (4 * width + 2 * hidden), 30e6),
    )(tokens, norm_gain, norm_shift, w_qkv, w_out, w_up, b_up, w_down, b_down)
    x_recv = core_swap(x_send)

    steps = 4
    count = half // steps
    step_rows = GROUP_FRAMES * count
    place_block = step_spec((frames, count, width), 1)
    row_block = lambda cols: step_spec((step_rows, cols))
    smem = pl.BlockSpec(memory_space=pltpu.SMEM)
    place_scratch = [
        pltpu.SMEM((GROUP_FRAMES,), jnp.int32),
        pltpu.VMEM((GROUP_FRAMES, count, width), BF16),
    ]
    small_shape = sds((8, TILE), F32)
    small_spec = pl.BlockSpec((8, TILE), lambda i: (0, 0))
    half_shape = sds((frames, half, width), BF16)
    (out_own, out_send, xt, h2, qkv1, o1, h3, act1, du1, gr1, dxb, small3) = pl.pallas_call(
        time_forward_kernel,
        grid=(steps,),
        in_specs=[
            smem, place_block, place_block, whole_spec(cotangent), whole_spec(cotangent),
            whole_spec(norm_gain), whole_spec(norm_shift), layer_spec(w_qkv, 1), layer_spec(w_out, 1),
            layer_spec(w_up, 1), whole_spec(b_up), layer_spec(w_down, 1), whole_spec(b_down),
        ],
        out_specs=[
            place_block, place_block, row_block(width), row_block(width), row_block(3 * width),
            row_block(width), row_block(width), row_block(hidden), row_block(hidden), row_block(width),
            row_block(width), small_spec,
        ],
        out_shape=[
            half_shape, half_shape, sds((rows, width), BF16), sds((rows, width), BF16),
            sds((rows, 3 * width), BF16), sds((rows, width), BF16), sds((rows, width), BF16),
            sds((rows, hidden), BF16), sds((rows, hidden), BF16), sds((rows, width), BF16),
            sds((rows, width), F32), small_shape,
        ],
        scratch_shapes=place_scratch + [pltpu.VMEM((step_rows, hidden), BF16)],
        compiler_params=params(56),
        cost_estimate=cost(2 * macs * (4 * width + 4 * hidden), 30e6),
    )(
        frame_slot, x_keep, x_recv, cotangent, cot_recv, norm_gain, norm_shift, w_qkv, w_out, w_up,
        b_up, w_down, b_down,
    )
    out_recv = core_swap(out_send)

    def mlp_weights(order, h, du, act, gr):
        slots = sp_size // 2
        shape = sds((slots, 4 * (width // sp_size) + hidden // sp_size, TILE), BF16)
        return pl.pallas_call(
            functools.partial(mlp_weights_kernel, order),
            grid=(hidden // TILE,),
            in_specs=[
                whole_spec(h), pl.BlockSpec((rows, TILE), lambda i: (0, i)),
                pl.BlockSpec((rows, TILE), lambda i: (0, i)), whole_spec(gr),
            ],
            out_specs=[pl.BlockSpec(shape.shape, lambda i: (0, 0, 0))] * 2,
            out_shape=[shape, shape],
            compiler_params=params(40),
            cost_estimate=cost(2 * macs * 2 * hidden, 14e6),
        )(h, du, act, gr)

    def attn_weights(order, h, dqkv, o, ar):
        slots = sp_size // 2
        shape = sds((slots, 4 * (width // sp_size), TILE), BF16)
        return pl.pallas_call(
            functools.partial(attn_weights_kernel, order),
            grid=(1,),
            in_specs=[whole_spec(h), whole_spec(dqkv), whole_spec(o), whole_spec(ar)],
            out_specs=[pl.BlockSpec(shape.shape, lambda i: (0, 0, 0))] * 2,
            out_shape=[shape, shape],
            compiler_params=params(40),
            cost_estimate=cost(2 * macs * 4 * width, 8e6),
        )(h, dqkv, o, ar)

    order_a = list(range(sp_bits))
    order_b = [0, 2, 1] + list(range(3, sp_bits))
    mlp1 = sum_scatter(*mlp_weights(order_a, h3, du1, act1, gr1), order_a, sp_size, grp_size)

    (dx_own, dx_send, ar1, dqkv1, small2) = pl.pallas_call(
        time_backward_kernel,
        grid=(steps,),
        in_specs=[
            smem, row_block(width), row_block(3 * width), row_block(width), whole_spec(norm_gain),
            whole_spec(norm_shift), layer_spec(w_qkv, 1), layer_spec(w_out, 1),
        ],
        out_specs=[place_block, place_block, row_block(width), row_block(3 * width), small_spec],
        out_shape=[
            half_shape, half_shape, sds((rows, width), BF16), sds((rows, 3 * width), BF16), small_shape,
        ],
        scratch_shapes=place_scratch,
        compiler_params=params(56),
        cost_estimate=cost(2 * macs * 4 * width, 15e6),
    )(frame_slot, xt, qkv1, dxb, norm_gain, norm_shift, w_qkv, w_out)
    dx_recv = core_swap(dx_send)
    attn1 = sum_scatter(*attn_weights(order_b, h2, dqkv1, o1, ar1), order_b, sp_size, grp_size)

    (gr0, du0, dxa, small1) = pl.pallas_call(
        space_mlp_back_kernel,
        grid=(frames,),
        in_specs=[
            half_block, half_block, frame_block(width), frame_block(hidden), whole_spec(norm_gain),
            whole_spec(norm_shift), layer_spec(w_up, 0), layer_spec(w_down, 0),
        ],
        out_specs=[frame_block(width), frame_block(hidden), frame_block(width), small_spec],
        out_shape=[frame_out(width, BF16), frame_out(hidden, BF16), frame_out(width, F32), small_shape],
        compiler_params=params(56),
        cost_estimate=cost(2 * macs * 2 * hidden, 20e6),
    )(dx_own, dx_recv, xa, slope0, norm_gain, norm_shift, w_up, w_down)
    flat = lambda a: a.reshape(rows, a.shape[-1])
    mlp0 = sum_scatter(
        *mlp_weights(order_b, flat(h1), flat(du0), flat(act0), flat(gr0)), order_b, sp_size, grp_size
    )

    (ar0, dqkv0, grad_tokens, output, small0) = pl.pallas_call(
        space_attn_back_kernel,
        grid=(frames,),
        in_specs=[
            frame_block(width), frame_block(width), frame_block(3 * width),
            step_spec((1, HEADS, patches)), frame_block(width), half_block, half_block,
            whole_spec(norm_gain), whole_spec(norm_shift), layer_spec(w_qkv, 0), layer_spec(w_out, 0),
        ],
        out_specs=[
            frame_block(width), frame_block(3 * width), frame_block(width), frame_block(width),
            small_spec,
        ],
        out_shape=[
            frame_out(width, BF16), frame_out(3 * width, BF16), frame_out(width, BF16),
            frame_out(width, BF16), small_shape,
        ],
        compiler_params=params(56),
        cost_estimate=cost(2 * macs * 6 * width, 20e6),
    )(tokens, dxa, qkv0, lse0, o0, out_own, out_recv, norm_gain, norm_shift, w_qkv, w_out)
    attn0 = sum_scatter(
        *attn_weights(order_a, flat(h0), flat(dqkv0), flat(o0), flat(ar0)), order_a, sp_size, grp_size
    )

    small = jnp.concatenate([small0, small1, small2, small3], axis=0).astype(BF16)
    for b in range(sp_bits):
        small = add_low(small, swap(small, "sp", sp_size, b))
    for b in range(grp_size.bit_length() - 1):
        small = add_low(small, swap(small, "grp", grp_size, b))
    small = small.astype(F32).reshape(4, 8, TILE)
    sp = lax.axis_index("sp")

    def mine(array):
        size = array.shape[1] // sp_size
        return lax.dynamic_slice_in_dim(array, sp * size, size, axis=1)

    def up_part(a):
        size = width // sp_size
        return a[: 4 * size].reshape(4, size, TILE).transpose(1, 0, 2).reshape(size, hidden)

    def qkv_part(a):
        size = width // sp_size
        return a[: 3 * size].reshape(3, size, TILE).transpose(1, 0, 2).reshape(size, 3 * width)

    size = width // sp_size
    return (
        output,
        grad_tokens,
        mine(small[:, 0]),
        mine(small[:, 1]),
        jnp.stack([qkv_part(attn0), qkv_part(attn1)]),
        jnp.stack([attn0[3 * size :], attn1[3 * size :]]),
        jnp.stack([up_part(mlp0), up_part(mlp1)]),
        mine(small[1::2, 4:].reshape(2, hidden)),
        jnp.stack([mlp0[4 * size :], mlp1[4 * size :]]),
        mine(small[1::2, 2]),
    )


def solution(mesh):
    rows = P(("grp", "sp"), None, None)
    in_specs = (rows, P("grp", None), P(), P(), P(), P(), P(), P(), P(), P(), rows)
    out_specs = (
        rows, rows, P(None, "sp"), P(None, "sp"), P(None, "sp", None), P(None, "sp", None),
        P(None, "sp", None), P(None, "sp"), P(None, "sp", None), P(None, "sp"),
    )
    body = functools.partial(shards, (mesh.shape["grp"], mesh.shape["sp"]))
    return jax.shard_map(body, mesh=mesh, in_specs=in_specs, out_specs=out_specs, check_vma=False)
```

time: 888 us -> 242 us (0.27)
  waiting for transfers between devices: 521 us -> 70.5 us
  matrix products: 128 us -> 0 us
  Pallas kernels: 0 us -> 112 us
  local copies, waits for them, and re-layouts: 110 us -> 11.9 us
  blocking collectives: 36.5 us -> 0 us
  other arithmetic: 50.5 us -> 18.4 us
  between operations: 15.4 us -> 1.06 us
    unnamed x13 -> x0, waiting for transfers between devices: 230 us -> none
    reduce_scatter x4 -> x0, waiting for transfers between devices: 208 us -> none  [the longest x1 76.1 us: shards(): lax.psum_scatter(joined[6].astype(jnp.bfloat16), 'sp', scatter_dimension=...]
    dot_general x36 -> x0, matrix products: 128 us -> none  [the longest x8 37.3 us: back_dot(): lax.dot_general(grad_rows, weight, (((1,), (1,)), ((), ())), preferred_el...]
    pallas_call x0 -> x9, Pallas kernels: none -> 112 us  [the longest x1 28.6 us: shards(): pl.pallas_call(time_forward_kernel, grid=(steps,), in_specs=[smem, place_...]
    ppermute x0 -> x29, waiting for transfers between devices: none -> 70.5 us  [swap(): return lax.ppermute(array, axis, [(i, i ^ 1 << bit) for i in range(size)])]
    all_to_all x3 -> x0, waiting for transfers between devices: 54.3 us -> none  [the longest x1 22.8 us: shards(): lax.all_to_all(sent, 'sp', split_axis=1, concat_axis=0, tiled=True)]
    reshape x8 -> x2, local copies, waits for them, and re-layouts: 33.9 us -> 0.28 us  [qkv_part(): a[:3 * size].reshape(3, size, TILE).transpose(1, 0, 2)]
    all_to_all x1 -> x0, blocking collectives: 31.5 us -> none  [shards(): lax.all_to_all(time_low, 'sp', split_axis=0, concat_axis=1, tiled=True)]
  transfers between devices with their start and end apart: 12 -> 29, of which waited for: 11 -> 16; matrix products, arithmetic and copies ran while one was open for 10% -> 8% of each run, Pallas kernels for 0% -> 22%
where the time goes in v1:
time: 242 us; the launch traced here: 241 us
  Pallas kernels  112 us (46%)
  waiting for transfers between devices  70.5 us (29%)
  starting transfers between devices  27.8 us (11%)
  other arithmetic  18.4 us (8%)
  local copies, waits for them, and re-layouts  11.9 us (5%)
    ppermute x29, waiting for transfers between devices, swap(): return lax.ppermute(array, axis, [(i, i ^ 1 << bit) for i in range(size)])  70.5 us
    pallas_call x1, Pallas kernels, shards(): pl.pallas_call(time_forward_kernel, grid=(steps,), in_specs=[smem, place_...  28.6 us
    ppermute x29, starting transfers between devices, swap(): return lax.ppermute(array, axis, [(i, i ^ 1 << bit) for i in range(size)])  27.8 us
    pallas_call x1, Pallas kernels, shards(): pl.pallas_call(space_forward_kernel, grid=(frames,), in_specs=[frame_bloc...  22.6 us
    pallas_call x1, Pallas kernels, shards(): pl.pallas_call(space_attn_back_kernel, grid=(frames,), in_specs=[frame_bl...  19.9 us
    pallas_call x2, Pallas kernels, mlp_weights(): pl.pallas_call(functools.partial(mlp_weights_kernel, order), grid=(hidden...  13.7 us
    convert_element_type x20, other arithmetic, add_low(): return (a.astype(F32) + b.astype(F32)).astype(BF16)  12.9 us
    pallas_call x1, Pallas kernels, shards(): pl.pallas_call(space_mlp_back_kernel, grid=(frames,), in_specs=[half_bloc...  11.2 us
  transfers between devices with their start and end apart: 29, of which 16 were waited for; matrix products, arithmetic and copies ran while one was open for 8% of the time, Pallas kernels for 22%

profile of v1, /device:TPU:0, one launch (start us, length us, event | category | flops | bytes accessed | tf_op | source)
XLA Modules:
  0.0 241.4 jit_solution(14044894434152162057)
XLA Ops:
  1.2 22.6 %shard_map.186 = (bf16[4,128,512]{2,1,0:T(8,128)(2,1)}, bf16[4,128,512]{2,1,0:T(8,128)(2,1)}, bf16[4,256,512]{2,1,0:T(8,128)(2,1)}, bf16[4,256,1536]{2,1,0:T(8,1...) custom-call(bf16[4,256,512]{2,1,0:T(8,128)(2,1)} %tok_ref.3, ...), custom_call_target="tpu_custom_call" | custom-call | flops 6442450944 | bytes 30000000 | tf_op jit(solution)/shard_map/pallas_call | solution.py:532
  23.9 2.1 collective-permute-done.recv_ref
  27.1 28.6 %shard_map.187 = (bf16[4,128,512]{2,1,0:T(8,128)(2,1)}, bf16[4,128,512]{2,1,0:T(8,128)(2,1)}, bf16[1024,512]{1,0:T(8,128)(2,1)}, bf16[1024,512]{1,0:T(8,128)(2,1...) custom-call(s32[8,8]{1,0:T(8,128)} %slots_ref.3, ...), custom_call_target="tpu_custom_call" | custom-call | flops 10737418240 | bytes 30000000 | tf_op jit(solution)/shard_map/pallas_call | solution.py:570
  55.8 11.0 %shard_map.188 = (bf16[4,128,512]{2,1,0:T(8,128)(2,1)}, bf16[4,128,512]{2,1,0:T(8,128)(2,1)}, bf16[1024,512]{1,0:T(8,128)(2,1)}, bf16[1024,1536]{1,0:T(8,128)(2,1)}, f32[8,512]{1,0:T(8,128)}) custom-call(s32[8,8]{1,0:T(8,128)} %slots_ref.3, bf16[1024,512]{1,0:T(8,128)(2,1)} %get-tuple-element.56.x_ref, bf16[1024,1536]{1,0:T(8,128)(2,1)} %get-tuple-element.57.qkv_ref, ...), custom_call_target="tpu_custom_call" | custom-call | flops 2147483648 | bytes 15000000 | tf_op jit(solution)/shard_map/pallas_call | solution.py:631
  68.1 0.9 collective-permute-done.2.recv_ref
  69.8 11.2 %shard_map.189 = (bf16[4,256,512]{2,1,0:T(8,128)(2,1)}, bf16[4,256,2048]{2,1,0:T(8,128)(2,1)}, f32[4,256,512]{2,1,0:T(8,128)}, f32[8,512]{1,0:T(8,128)}) custom-call(bf16[4,128,512]{2,1,0:T(8,128)(2,1)} %get-tuple-element.59.own_ref, bf16[4,128,512]{2,1,0:T(8,128)(2,1)} %copy-done.20, f32[4,256,512]{2,1,0:T(8,128)} %get-tuple-element.61.xa_ref, ...), custom_call_target="tpu_custom_call" | custom-call | flops 4294967296 | bytes 20000000 | tf_op jit(solution)/shard_map/pallas_call | solution.py:649
  82.5 19.9 %shard_map.190 = (bf16[4,256,512]{2,1,0:T(8,128)(2,1)}, bf16[4,256,1536]{2,1,0:T(8,128)(2,1)}, bf16[4,256,512]{2,1,0:T(8,128)(2,1)}, bf16[4,256,512]{2,1,0:T(8,128)(2,1)}, f32[8,512]{1,0:T(8,128)}) custom-call(bf16[4,256,512]{2,1,0:T(8,128)(2,1)} %tok_ref.3, f32[4,256,512]{2,1,0:T(8,128)} %get-tuple-element.63.dxa_ref, ...), custom_call_target="tpu_custom_call" | custom-call | flops 3221225472 | bytes 20000000 | tf_op jit(solution)/shard_map/pallas_call | solution.py:666
  103.2 1.0 collective-permute-done.4
  104.3 2.7 %collective-permute-start.5 = (bf16[32,512]{1,0:T(8,128)(2,1)S(1)}, bf16[32,512]{1,0:T(8,128)(2,1)S(1)}, u32[]{:S(2)}, u32[]{:S(2)}) collective-permute-start(bf16[32,512]{1,0:T(8,128)(2,1)S(1)} %add_convert_fusion.36), channel_id=1, source_target_pairs={{0,2},{1,3},{2,0},{3,1},{4,6},{5,7},{6,4},{7,5},{8,10},{9,11},{10,... | collective-permute-start | bytes 98312 | tf_op jit(solution)/shard_map/ppermute | solution.py:498
  107.0 1.2 copy-done.4
  108.2 1.2 copy-done.9
  109.4 1.2 copy-done.10
  110.7 2.4 shard_map.192
  113.2 1.7 collective-permute-start.6
  114.9 2.2 copy-done.11
  117.1 6.8 %shard_map.194 = (bf16[8,256,512]{2,1,0:T(8,128)(2,1)S(1)}, bf16[8,256,512]{2,1,0:T(8,128)(2,1)S(1)}) custom-call(bf16[1024,512]{1,0:T(8,128)(2,1)S(1)} %copy-done.12, bf16[1024,2048]{1,0:T(8,128)(2,1)S(1)} %copy-done.11, bf16[1024,2048]{1,0:T(8,128)(2,1)} %get-tuple-element.94.act_ref, bf16[1024,512]{1,0:T(8,128)(2,1)S(1)} %copy-done.13), custom_call_target="tpu_custom_call" | custom-call | flops 4294967296 | bytes 14000000 | tf_op jit(solution)/shard_map/pallas_call | solution.py:601
  124.2 2.6 %collective-permute-start.7 = (bf16[32,512]{1,0:T(8,128)(2,1)S(1)}, bf16[32,512]{1,0:T(8,128)(2,1)S(1)}, u32[]{:S(2)}, u32[]{:S(2)}) collective-permute-start(bf16[32,512]{1,0:T(8,128)(2,1)S(1)} %add_convert_fusion.34), channel_id=1, source_target_pairs={{0,8},{1,9},{2,10},{3,11},{4,12},{5,13},{6,14},{7,15},{8,0},{9,1},... | collective-permute-start | bytes 98312 | tf_op jit(solution)/shard_map/ppermute | solution.py:498
  126.8 2.4 shard_map.191
  129.3 1.6 collective-permute-start.8
  131.7 6.9 %shard_map.193 = (bf16[8,256,512]{2,1,0:T(8,128)(2,1)S(1)}, bf16[8,256,512]{2,1,0:T(8,128)(2,1)S(1)}) custom-call(bf16[1024,512]{1,0:T(8,128)(2,1)S(1)} %bitcast.43, bf16[1024,2048]{1,0:T(8,128)(2,1)S(1)} %bitcast.42, bf16[1024,2048]{1,0:T(8,128)(2,1)} %bitcast.56, bf16[1024,512]{1,0:T(8,128)(2,1)S(1)} %bitcast.45), custom_call_target="tpu_custom_call" | custom-call | flops 4294967296 | bytes 14000000 | tf_op jit(solution)/shard_map/pallas_call | solution.py:601
  138.7 6.6 %collective-permute-done.15 = bf16[4,128,512]{2,1,0:T(8,128)(2,1)S(1)} collective-permute-done((bf16[4,128,512]{2,1,0:T(8,128)(2,1)S(1)}, bf16[4,128,512]{2,1,0:T(8,128)(2,1)S(1)}, u32[]{:S(2)}, u32[]{:S(2)}) %collective-permute-start.15) | collective-permute-done | bytes 524320 | tf_op jit(solution)/shard_map/ppermute | solution.py:498
  147.4 5.7 %collective-permute-done.16 = bf16[2,128,512]{2,1,0:T(8,128)(2,1)S(1)} collective-permute-done((bf16[2,128,512]{2,1,0:T(8,128)(2,1)S(1)}, bf16[2,128,512]{2,1,0:T(8,128)(2,1)S(1)}, u32[]{:S(2)}, u32[]{:S(2)}) %collective-permute-start.16) | collective-permute-done | bytes 262176 | tf_op jit(solution)/shard_map/ppermute | solution.py:498
  154.1 6.5 %collective-permute-done.17 = bf16[1,128,512]{2,1,0:T(8,128)(2,1)S(1)} collective-permute-done((bf16[1,128,512]{2,1,0:T(8,128)(2,1)S(1)}, bf16[1,128,512]{2,1,0:T(8,128)(2,1)S(1)}, u32[]{:S(2)}, u32[]{:S(2)}) %collective-permute-start.17) | collective-permute-done | bytes 131104 | tf_op jit(solution)/shard_map/ppermute | solution.py:498
  161.2 1.6 add_convert_fusion.1
  163.3 4.0 %collective-permute-done.10 = bf16[4,128,512]{2,1,0:T(8,128)(2,1)S(1)} collective-permute-done((bf16[4,128,512]{2,1,0:T(8,128)(2,1)S(1)}, bf16[4,128,512]{2,1,0:T(8,128)(2,1)S(1)}, u32[]{:S(2)}, u32[]{:S(2)}) %collective-permute-start.10) | collective-permute-done | bytes 524320 | tf_op jit(solution)/shard_map/ppermute | solution.py:498
  167.4 0.8 add_convert_fusion.23
  168.2 1.5 collective-permute-start.11
  169.7 1.7 add_convert_fusion.3
  172.9 6.3 %collective-permute-done.11 = bf16[2,128,512]{2,1,0:T(8,128)(2,1)} collective-permute-done((bf16[2,128,512]{2,1,0:T(8,128)(2,1)}, bf16[2,128,512]{2,1,0:T(8,128)(2,1)}, u32[]{:S(2)}, u32[]{:S(2)}) %collective-permute-start.11) | collective-permute-done | bytes 262176 | tf_op jit(solution)/shard_map/ppermute | solution.py:498
  179.2 0.9 add_convert_fusion.30
  180.1 2.6 %collective-permute-start.12 = (bf16[1,128,512]{2,1,0:T(8,128)(2,1)S(1)}, bf16[1,128,512]{2,1,0:T(8,128)(2,1)S(1)}, u32[]{:S(2)}, u32[]{:S(2)}) collective-permute-start(bf16[1,128,512]{2,1,0:T(8,128)(2,1)S(1)} %add_convert_fusion.30), channel_id=1, source_target_pairs={{0,8},{1,9},{2,10},{3,11},{4,12},{5,13},{6,14},{7,15},{8,0},{9,1},... | collective-permute-start | bytes 393224 | tf_op jit(solution)/shard_map/ppermute | solution.py:498
  182.7 5.6 %collective-permute-done.25 = bf16[4,256,512]{2,1,0:T(8,128)(2,1)} collective-permute-done((bf16[4,256,512]{2,1,0:T(8,128)(2,1)}, bf16[4,256,512]{2,1,0:T(8,128)(2,1)}, u32[]{:S(2)}, u32[]{:S(2)}) %collective-permute-start.25) | collective-permute-done | bytes 1048608 | tf_op jit(solution)/shard_map/ppermute | solution.py:498
  188.4 2.3 add_convert_fusion.5
  191.1 10.5 %collective-permute-done.12 = bf16[1,128,512]{2,1,0:T(8,128)(2,1)S(1)} collective-permute-done((bf16[1,128,512]{2,1,0:T(8,128)(2,1)S(1)}, bf16[1,128,512]{2,1,0:T(8,128)(2,1)S(1)}, u32[]{:S(2)}, u32[]{:S(2)}) %collective-permute-start.12) | collective-permute-done | bytes 131104 | tf_op jit(solution)/shard_map/ppermute | solution.py:498
  201.6 1.0 add_convert_fusion.29
  203.2 1.5 add_convert_fusion.7
  205.5 2.1 collective-permute-done.13
  207.9 1.6 collective-permute-done.26
  209.5 1.0 add_convert_fusion.14
  210.5 5.1 %collective-permute-start.27 = (bf16[1,256,512]{2,1,0:T(8,128)(2,1)S(1)}, bf16[1,256,512]{2,1,0:T(8,128)(2,1)S(1)}, u32[]{:S(2)}, u32[]{:S(2)}) collective-permute-start(bf16[1,256,512]{2,1,0:T(8,128)(2,1)S(1)} %add_convert_fusion.14), channel_id=1, source_target_pairs={{0,8},{1,9},{2,10},{3,11},{4,12},{5,13},{6,14},{7,15},{8,0},{9,1},... | collective-permute-start | bytes 786440 | tf_op jit(solution)/shard_map/ppermute | solution.py:498
  216.5 0.9 collective-permute-start.22
  217.4 10.5 %collective-permute-done.27 = bf16[1,256,512]{2,1,0:T(8,128)(2,1)S(1)} collective-permute-done((bf16[1,256,512]{2,1,0:T(8,128)(2,1)S(1)}, bf16[1,256,512]{2,1,0:T(8,128)(2,1)S(1)}, u32[]{:S(2)}, u32[]{:S(2)}) %collective-permute-start.27) | collective-permute-done | bytes 262176 | tf_op jit(solution)/shard_map/ppermute | solution.py:498
  227.9 1.1 add_convert_fusion.13
  230.8 1.3 collective-permute-start.23
  232.1 4.4 %collective-permute-done.28 = bf16[1,256,512]{2,1,0:T(8,128)(2,1)S(1)} collective-permute-done((bf16[1,256,512]{2,1,0:T(8,128)(2,1)S(1)}, bf16[1,256,512]{2,1,0:T(8,128)(2,1)S(1)}, u32[]{:S(2)}, u32[]{:S(2)}) %collective-permute-start.28) | collective-permute-done | bytes 262176 | tf_op jit(solution)/shard_map/ppermute | solution.py:498
  237.0 2.3 collective-permute-done.23
  239.8 0.8 pad_maximum_fusion.1
  240.6 0.8 pad_maximum_fusion
  (117 shorter events, 19.2 us)
Async XLA Ops:
  0.6 25.4 %collective-permute-start.1 = (bf16[4,256,512]{2,1,0:T(8,128)(2,1)}, bf16[4,256,512]{2,1,0:T(8,128)(2,1)S(1)}, u32[]{:S(2)}, u32[]{:S(2)}) collective-permute-start(bf16[4,256,512]{2,1,0:T(8,128)(2,1)} %cot_ref.1), channel_id=1, source_target_pairs={{0,1},{1,0},{2,3},{3,2},{4,5},{5,4},{6,7},{7,6},{8,9},{9,8},{10,11... | collective-permute-start | bytes 3145736 | tf_op jit(solution)/shard_map/ppermute | solution.py:498
  23.8 2.2 collective-permute-start
  26.0 1.1 copy-start.17
  55.8 11.2 %copy-start.18 = (bf16[4,128,512]{2,1,0:T(8,128)(2,1)S(1)}, bf16[4,128,512]{2,1,0:T(8,128)(2,1)}, u32[]{:S(2)}) copy-start(bf16[4,128,512]{2,1,0:T(8,128)(2,1)} %get-tuple-element.68) | copy-start | bytes 1572868
  55.8 12.3 %copy-start.16 = (f32[8,512]{1,0:T(8,128)S(1)}, f32[8,512]{1,0:T(8,128)}, u32[]{:S(2)}) copy-start(f32[8,512]{1,0:T(8,128)} %get-tuple-element.74) | copy-start | bytes 49156
  66.8 2.2 collective-permute-start.2
  67.0 14.6 %collective-permute-start.3 = (bf16[4,128,512]{2,1,0:T(8,128)(2,1)S(1)}, bf16[4,128,512]{2,1,0:T(8,128)(2,1)S(1)}, u32[]{:S(2)}, u32[]{:S(2)}) collective-permute-start(bf16[4,128,512]{2,1,0:T(8,128)(2,1)S(1)} %copy-done.18), channel_id=1, source_target_pairs={{0,1},{1,0},{2,3},{3,2},{4,5},{5,4},{6,7},{7,6},{8,9},{9,8},{10,11... | collective-permute-start | bytes 1572872 | tf_op jit(solution)/shard_map/ppermute | solution.py:498
  82.5 24.5 %copy-start.2 = (bf16[1024,1536]{1,0:T(8,128)(2,1)S(1)}, bf16[1024,1536]{1,0:T(8,128)(2,1)}, u32[]{:S(2)}) copy-start(bf16[1024,1536]{1,0:T(8,128)(2,1)} %get-tuple-element.81.dqkv_ref) | copy-start | bytes 9437188
  103.1 1.2 collective-permute-start.4
  104.3 8.9 %collective-permute-start.5 = (bf16[32,512]{1,0:T(8,128)(2,1)S(1)}, bf16[32,512]{1,0:T(8,128)(2,1)S(1)}, u32[]{:S(2)}, u32[]{:S(2)}) collective-permute-start(bf16[32,512]{1,0:T(8,128)(2,1)S(1)} %add_convert_fusion.36), channel_id=1, source_target_pairs={{0,2},{1,3},{2,0},{3,1},{4,6},{5,7},{6,4},{7,5},{8,10},{9,11},{10,... | collective-permute-start | bytes 98312 | tf_op jit(solution)/shard_map/ppermute | solution.py:498
  107.0 1.2 copy-start.4
  108.2 1.2 copy-start.9
  109.4 1.2 copy-start.10
  110.7 4.3 %copy-start.12 = (bf16[1024,512]{1,0:T(8,128)(2,1)S(1)}, bf16[1024,512]{1,0:T(8,128)(2,1)}, u32[]{:S(2)}) copy-start(bf16[1024,512]{1,0:T(8,128)(2,1)} %get-tuple-element.92.h_ref) | copy-start | bytes 3145732
  110.7 4.3 %copy-start.13 = (bf16[1024,512]{1,0:T(8,128)(2,1)S(1)}, bf16[1024,512]{1,0:T(8,128)(2,1)}, u32[]{:S(2)}) copy-start(bf16[1024,512]{1,0:T(8,128)(2,1)} %get-tuple-element.95.gr_ref) | copy-start | bytes 3145732
  113.0 17.9 %collective-permute-start.14 = (bf16[8,128,512]{2,1,0:T(8,128)(2,1)S(1)}, bf16[8,128,512]{2,1,0:T(8,128)(2,1)S(1)}, u32[]{:S(2)}, u32[]{:S(2)}) collective-permute-start(bf16[8,128,512]{2,1,0:T(8,128)(2,1)S(1)} %get-tuple-element.85), channel_id=1, source_target_pairs={{0,1},{1,0},{2,3},{3,2},{4,5},{5,4},{6,7},{7,6},{8,9},{9,8},{10,11... | collective-permute-start | bytes 3145736 | tf_op jit(solution)/shard_map/ppermute | solution.py:498
  113.2 11.0 %collective-permute-start.6 = (bf16[32,512]{1,0:T(8,128)(2,1)S(1)}, bf16[32,512]{1,0:T(8,128)(2,1)S(1)}, u32[]{:S(2)}, u32[]{:S(2)}) collective-permute-start(bf16[32,512]{1,0:T(8,128)(2,1)S(1)} %add_convert_fusion.35), channel_id=1, source_target_pairs={{0,4},{1,5},{2,6},{3,7},{4,0},{5,1},{6,2},{7,3},{8,12},{9,13},{10,... | collective-permute-start | bytes 98312 | tf_op jit(solution)/shard_map/ppermute | solution.py:498
  114.9 2.2 copy-start.11
  117.1 9.6 %copy-start = (bf16[4,256,512]{2,1,0:T(8,128)(2,1)S(1)}, bf16[4,256,512]{2,1,0:T(8,128)(2,1)}, u32[]{:S(2)}) copy-start(bf16[4,256,512]{2,1,0:T(8,128)(2,1)} %get-tuple-element.66.o_ref) | copy-start | bytes 3145732
  117.1 9.6 %copy-start.1 = (bf16[4,256,1536]{2,1,0:T(8,128)(2,1)S(1)}, bf16[4,256,1536]{2,1,0:T(8,128)(2,1)}, u32[]{:S(2)}) copy-start(bf16[4,256,1536]{2,1,0:T(8,128)(2,1)} %get-tuple-element.76) | copy-start | bytes 9437188
  117.1 9.6 %copy-start.3 = (bf16[4,256,512]{2,1,0:T(8,128)(2,1)S(1)}, bf16[4,256,512]{2,1,0:T(8,128)(2,1)}, u32[]{:S(2)}) copy-start(bf16[4,256,512]{2,1,0:T(8,128)(2,1)} %get-tuple-element.77) | copy-start | bytes 3145732
  117.1 9.7 %copy-start.7 = (bf16[4,256,512]{2,1,0:T(8,128)(2,1)S(1)}, bf16[4,256,512]{2,1,0:T(8,128)(2,1)}, u32[]{:S(2)}) copy-start(bf16[4,256,512]{2,1,0:T(8,128)(2,1)} %get-tuple-element.75) | copy-start | bytes 3145732
  123.9 37.2 %collective-permute-start.24 = (bf16[8,256,512]{2,1,0:T(8,128)(2,1)S(1)}, bf16[8,256,512]{2,1,0:T(8,128)(2,1)S(1)}, u32[]{:S(2)}, u32[]{:S(2)}) collective-permute-start(bf16[8,256,512]{2,1,0:T(8,128)(2,1)S(1)} %get-tuple-element.97), channel_id=1, source_target_pairs={{0,1},{1,0},{2,3},{3,2},{4,5},{5,4},{6,7},{7,6},{8,9},{9,8},{10,11... | collective-permute-start | bytes 6291464 | tf_op jit(solution)/shard_map/ppermute | solution.py:498
  124.2 5.1 %collective-permute-start.7 = (bf16[32,512]{1,0:T(8,128)(2,1)S(1)}, bf16[32,512]{1,0:T(8,128)(2,1)S(1)}, u32[]{:S(2)}, u32[]{:S(2)}) collective-permute-start(bf16[32,512]{1,0:T(8,128)(2,1)S(1)} %add_convert_fusion.34), channel_id=1, source_target_pairs={{0,8},{1,9},{2,10},{3,11},{4,12},{5,13},{6,14},{7,15},{8,0},{9,1},... | collective-permute-start | bytes 98312 | tf_op jit(solution)/shard_map/ppermute | solution.py:498
  126.8 5.0 %copy-start.5 = (bf16[4,256,2048]{2,1,0:T(8,128)(2,1)S(1)}, bf16[4,256,2048]{2,1,0:T(8,128)(2,1)}, u32[]{:S(2)}) copy-start(bf16[4,256,2048]{2,1,0:T(8,128)(2,1)} %get-tuple-element.87) | copy-start | bytes 12582916
  129.2 2.6 %copy-start.6 = (bf16[4,256,512]{2,1,0:T(8,128)(2,1)S(1)}, bf16[4,256,512]{2,1,0:T(8,128)(2,1)}, u32[]{:S(2)}) copy-start(bf16[4,256,512]{2,1,0:T(8,128)(2,1)} %get-tuple-element.86) | copy-start | bytes 3145732
  129.2 2.6 %copy-start.8 = (bf16[4,256,512]{2,1,0:T(8,128)(2,1)S(1)}, bf16[4,256,512]{2,1,0:T(8,128)(2,1)}, u32[]{:S(2)}) copy-start(bf16[4,256,512]{2,1,0:T(8,128)(2,1)} %get-tuple-element.89) | copy-start | bytes 3145732
  129.2 24.0 %collective-permute-start.9 = (bf16[8,128,512]{2,1,0:T(8,128)(2,1)S(1)}, bf16[8,128,512]{2,1,0:T(8,128)(2,1)S(1)}, u32[]{:S(2)}, u32[]{:S(2)}) collective-permute-start(bf16[8,128,512]{2,1,0:T(8,128)(2,1)S(1)} %get-tuple-element.79), channel_id=1, source_target_pairs={{0,1},{1,0},{2,3},{3,2},{4,5},{5,4},{6,7},{7,6},{8,9},{9,8},{10,11... | collective-permute-start | bytes 3145736 | tf_op jit(solution)/shard_map/ppermute | solution.py:498
  129.3 9.4 %collective-permute-start.8 = (bf16[32,512]{1,0:T(8,128)(2,1)S(1)}, bf16[32,512]{1,0:T(8,128)(2,1)S(1)}, u32[]{:S(2)}, u32[]{:S(2)}) collective-permute-start(bf16[32,512]{1,0:T(8,128)(2,1)S(1)} %add_convert_fusion.33), channel_id=1, source_target_pairs={{0,16},{16,0},{1,17},{17,1},{2,18},{18,2},{3,19},{19,3},{4,20},{20... | collective-permute-start | bytes 98312 | tf_op jit(solution)/shard_map/ppermute | solution.py:498
  131.3 14.0 %collective-permute-start.15 = (bf16[4,128,512]{2,1,0:T(8,128)(2,1)S(1)}, bf16[4,128,512]{2,1,0:T(8,128)(2,1)S(1)}, u32[]{:S(2)}, u32[]{:S(2)}) collective-permute-start(bf16[4,128,512]{2,1,0:T(8,128)(2,1)S(1)} %get-tuple-element.109), channel_id=1, source_target_pairs={{0,4},{1,5},{2,6},{3,7},{4,0},{5,1},{6,2},{7,3},{8,12},{9,13},{10,... | collective-permute-start | bytes 1572872 | tf_op jit(solution)/shard_map/ppermute | solution.py:498
  138.6 31.1 %collective-permute-start.19 = (bf16[8,256,512]{2,1,0:T(8,128)(2,1)S(1)}, bf16[8,256,512]{2,1,0:T(8,128)(2,1)S(1)}, u32[]{:S(2)}, u32[]{:S(2)}) collective-permute-start(bf16[8,256,512]{2,1,0:T(8,128)(2,1)S(1)} %get-tuple-element.91), channel_id=1, source_target_pairs={{0,1},{1,0},{2,3},{3,2},{4,5},{5,4},{6,7},{7,6},{8,9},{9,8},{10,11... | collective-permute-start | bytes 6291464 | tf_op jit(solution)/shard_map/ppermute | solution.py:498
  145.5 7.6 %collective-permute-start.16 = (bf16[2,128,512]{2,1,0:T(8,128)(2,1)S(1)}, bf16[2,128,512]{2,1,0:T(8,128)(2,1)S(1)}, u32[]{:S(2)}, u32[]{:S(2)}) collective-permute-start(bf16[2,128,512]{2,1,0:T(8,128)(2,1)S(1)} %get-tuple-element.113), channel_id=1, source_target_pairs={{0,2},{1,3},{2,0},{3,1},{4,6},{5,7},{6,4},{7,5},{8,10},{9,11},{10,... | collective-permute-start | bytes 786440 | tf_op jit(solution)/shard_map/ppermute | solution.py:498
  153.1 7.4 %collective-permute-start.17 = (bf16[1,128,512]{2,1,0:T(8,128)(2,1)S(1)}, bf16[1,128,512]{2,1,0:T(8,128)(2,1)S(1)}, u32[]{:S(2)}, u32[]{:S(2)}) collective-permute-start(bf16[1,128,512]{2,1,0:T(8,128)(2,1)S(1)} %add_convert_fusion.26), channel_id=1, source_target_pairs={{0,8},{1,9},{2,10},{3,11},{4,12},{5,13},{6,14},{7,15},{8,0},{9,1},... | collective-permute-start | bytes 393224 | tf_op jit(solution)/shard_map/ppermute | solution.py:498
  153.5 13.9 %collective-permute-start.10 = (bf16[4,128,512]{2,1,0:T(8,128)(2,1)S(1)}, bf16[4,128,512]{2,1,0:T(8,128)(2,1)S(1)}, u32[]{:S(2)}, u32[]{:S(2)}) collective-permute-start(bf16[4,128,512]{2,1,0:T(8,128)(2,1)S(1)} %get-tuple-element.107), channel_id=1, source_target_pairs={{0,2},{1,3},{2,0},{3,1},{4,6},{5,7},{6,4},{7,5},{8,10},{9,11},{10,... | collective-permute-start | bytes 1572872 | tf_op jit(solution)/shard_map/ppermute | solution.py:498
  160.6 11.9 %collective-permute-start.18 = (bf16[1,128,512]{2,1,0:T(8,128)(2,1)S(1)}, bf16[1,128,512]{2,1,0:T(8,128)(2,1)S(1)}, u32[]{:S(2)}, u32[]{:S(2)}) collective-permute-start(bf16[1,128,512]{2,1,0:T(8,128)(2,1)S(1)} %add_convert_fusion.25), channel_id=1, source_target_pairs={{0,16},{16,0},{1,17},{17,1},{2,18},{18,2},{3,19},{19,3},{4,20},{20... | collective-permute-start | bytes 393224 | tf_op jit(solution)/shard_map/ppermute | solution.py:498
  162.8 25.6 %collective-permute-start.25 = (bf16[4,256,512]{2,1,0:T(8,128)(2,1)}, bf16[4,256,512]{2,1,0:T(8,128)(2,1)}, u32[]{:S(2)}, u32[]{:S(2)}) collective-permute-start(bf16[4,256,512]{2,1,0:T(8,128)(2,1)} %get-tuple-element.101), channel_id=1, source_target_pairs={{0,2},{1,3},{2,0},{3,1},{4,6},{5,7},{6,4},{7,5},{8,10},{9,11},{10,... | collective-permute-start | bytes 3145736 | tf_op jit(solution)/shard_map/ppermute | solution.py:498
  168.2 11.0 %collective-permute-start.11 = (bf16[2,128,512]{2,1,0:T(8,128)(2,1)}, bf16[2,128,512]{2,1,0:T(8,128)(2,1)}, u32[]{:S(2)}, u32[]{:S(2)}) collective-permute-start(bf16[2,128,512]{2,1,0:T(8,128)(2,1)} %get-tuple-element.111), channel_id=1, source_target_pairs={{0,4},{1,5},{2,6},{3,7},{4,0},{5,1},{6,2},{7,3},{8,12},{9,13},{10,... | collective-permute-start | bytes 786440 | tf_op jit(solution)/shard_map/ppermute | solution.py:498
  171.4 31.8 %collective-permute-start.20 = (bf16[4,256,512]{2,1,0:T(8,128)(2,1)}, bf16[4,256,512]{2,1,0:T(8,128)(2,1)}, u32[]{:S(2)}, u32[]{:S(2)}) collective-permute-start(bf16[4,256,512]{2,1,0:T(8,128)(2,1)} %get-tuple-element.99), channel_id=1, source_target_pairs={{0,4},{1,5},{2,6},{3,7},{4,0},{5,1},{6,2},{7,3},{8,12},{9,13},{10,... | collective-permute-start | bytes 3145736 | tf_op jit(solution)/shard_map/ppermute | solution.py:498
  172.5 18.1 %copy-start.14 = (f32[1,128,512]{2,1,0:T(8,128)}, f32[1,128,512]{2,1,0:T(8,128)S(1)}, u32[]{:S(2)}) copy-start(f32[1,128,512]{2,1,0:T(8,128)S(1)} %fusion.3) | copy-start | bytes 786436
  180.1 21.4 %collective-permute-start.12 = (bf16[1,128,512]{2,1,0:T(8,128)(2,1)S(1)}, bf16[1,128,512]{2,1,0:T(8,128)(2,1)S(1)}, u32[]{:S(2)}, u32[]{:S(2)}) collective-permute-start(bf16[1,128,512]{2,1,0:T(8,128)(2,1)S(1)} %add_convert_fusion.30), channel_id=1, source_target_pairs={{0,8},{1,9},{2,10},{3,11},{4,12},{5,13},{6,14},{7,15},{8,0},{9,1},... | collective-permute-start | bytes 393224 | tf_op jit(solution)/shard_map/ppermute | solution.py:498
  190.6 18.9 %collective-permute-start.26 = (bf16[2,256,512]{2,1,0:T(8,128)(2,1)}, bf16[2,256,512]{2,1,0:T(8,128)(2,1)}, u32[]{:S(2)}, u32[]{:S(2)}) collective-permute-start(bf16[2,256,512]{2,1,0:T(8,128)(2,1)} %get-tuple-element.105), channel_id=1, source_target_pairs={{0,4},{1,5},{2,6},{3,7},{4,0},{5,1},{6,2},{7,3},{8,12},{9,13},{10,... | collective-permute-start | bytes 1572872 | tf_op jit(solution)/shard_map/ppermute | solution.py:498
  202.5 5.0 %collective-permute-start.13 = (bf16[1,128,512]{2,1,0:T(8,128)(2,1)S(1)}, bf16[1,128,512]{2,1,0:T(8,128)(2,1)S(1)}, u32[]{:S(2)}, u32[]{:S(2)}) collective-permute-start(bf16[1,128,512]{2,1,0:T(8,128)(2,1)S(1)} %add_convert_fusion.29), channel_id=1, source_target_pairs={{0,16},{16,0},{1,17},{17,1},{2,18},{18,2},{3,19},{19,3},{4,20},{20... | collective-permute-start | bytes 393224 | tf_op jit(solution)/shard_map/ppermute | solution.py:498
  204.7 11.8 %collective-permute-start.21 = (bf16[2,256,512]{2,1,0:T(8,128)(2,1)S(1)}, bf16[2,256,512]{2,1,0:T(8,128)(2,1)S(1)}, u32[]{:S(2)}, u32[]{:S(2)}) collective-permute-start(bf16[2,256,512]{2,1,0:T(8,128)(2,1)S(1)} %get-tuple-element.103), channel_id=1, source_target_pairs={{0,2},{1,3},{2,0},{3,1},{4,6},{5,7},{6,4},{7,5},{8,10},{9,11},{10,... | collective-permute-start | bytes 1572872 | tf_op jit(solution)/shard_map/ppermute | solution.py:498
  207.7 21.8 %slice-start = ((f32[1,128,512]{2,1,0:T(8,128)}), f32[1,32,512]{2,1,0:T(8,128)S(1)}, s32[]{:S(2)}) async-start(f32[1,128,512]{2,1,0:T(8,128)} %copy-done.14), calls=%async_computation | async-start | bytes 131072 | tf_op jit(solution)/shard_map/slice | solution.py:716
  210.5 17.4 %collective-permute-start.27 = (bf16[1,256,512]{2,1,0:T(8,128)(2,1)S(1)}, bf16[1,256,512]{2,1,0:T(8,128)(2,1)S(1)}, u32[]{:S(2)}, u32[]{:S(2)}) collective-permute-start(bf16[1,256,512]{2,1,0:T(8,128)(2,1)S(1)} %add_convert_fusion.14), channel_id=1, source_target_pairs={{0,8},{1,9},{2,10},{3,11},{4,12},{5,13},{6,14},{7,15},{8,0},{9,1},... | collective-permute-start | bytes 786440 | tf_op jit(solution)/shard_map/ppermute | solution.py:498
  216.5 14.2 %collective-permute-start.22 = (bf16[1,256,512]{2,1,0:T(8,128)(2,1)S(1)}, bf16[1,256,512]{2,1,0:T(8,128)(2,1)S(1)}, u32[]{:S(2)}, u32[]{:S(2)}) collective-permute-start(bf16[1,256,512]{2,1,0:T(8,128)(2,1)S(1)} %add_convert_fusion.18), channel_id=1, source_target_pairs={{0,8},{1,9},{2,10},{3,11},{4,12},{5,13},{6,14},{7,15},{8,0},{9,1},... | collective-permute-start | bytes 786440 | tf_op jit(solution)/shard_map/ppermute | solution.py:498
  228.9 7.5 %collective-permute-start.28 = (bf16[1,256,512]{2,1,0:T(8,128)(2,1)S(1)}, bf16[1,256,512]{2,1,0:T(8,128)(2,1)S(1)}, u32[]{:S(2)}, u32[]{:S(2)}) collective-permute-start(bf16[1,256,512]{2,1,0:T(8,128)(2,1)S(1)} %add_convert_fusion.13), channel_id=1, source_target_pairs={{0,16},{16,0},{1,17},{17,1},{2,18},{18,2},{3,19},{19,3},{4,20},{20... | collective-permute-start | bytes 786440 | tf_op jit(solution)/shard_map/ppermute | solution.py:498
  230.8 8.5 %collective-permute-start.23 = (bf16[1,256,512]{2,1,0:T(8,128)(2,1)S(1)}, bf16[1,256,512]{2,1,0:T(8,128)(2,1)S(1)}, u32[]{:S(2)}, u32[]{:S(2)}) collective-permute-start(bf16[1,256,512]{2,1,0:T(8,128)(2,1)S(1)} %add_convert_fusion.17), channel_id=1, source_target_pairs={{0,16},{16,0},{1,17},{17,1},{2,18},{18,2},{3,19},{19,3},{4,20},{20... | collective-permute-start | bytes 786440 | tf_op jit(solution)/shard_map/ppermute | solution.py:498
  (3 other events, 2.4 us)

commit v2 on v1

--- a/solution.py
+++ b/solution.py
@@ -263,7 +263,7 @@
 
 
 def time_backward_kernel(
-    slots_ref, x_ref, qkv_ref, dxb_ref, gain_ref, shift_ref, wqkv_ref, wout_ref,
+    after_ref, slots_ref, x_ref, qkv_ref, dxb_ref, gain_ref, shift_ref, wqkv_ref, wout_ref,
     own_ref, send_ref, ar_ref, dqkv_ref, small_ref,
     where_scr, both_scr,
 ):
@@ -339,8 +339,8 @@
 
 
 def space_mlp_back_kernel(
-    own_ref, recv_ref, xa_ref, slope_ref, gain_ref, shift_ref, wup_ref, wdown_ref,
-    gr_ref, du_ref, dxa_ref, small_ref,
+    after_ref, own_ref, recv_ref, xa_ref, slope_ref, gain_ref, shift_ref, wup_ref, wdown_ref,
+    gr_ref, du_ref, dxa_ref, ar_ref, small_ref,
 ):
     part = lax.rem(lax.axis_index("sp"), 2)
     clear_first(small_ref)
@@ -355,22 +355,15 @@
     small_ref[0:1, :] += column_sum(dh * unit)
     small_ref[1:2, :] += column_sum(dh)
     small_ref[2:3, :] += column_sum(grad)
-    dxa_ref[0] = grad + norm_back(dh, unit, inv, gain)
+    dxa = grad + norm_back(dh, unit, inv, gain)
+    dxa_ref[0] = dxa
+    ar_ref[0] = dxa.astype(BF16)
 
 
 def space_attn_back_kernel(
-    tok_ref, dxa_ref, qkv_ref, lse_ref, o_ref, own_ref, recv_ref, gain_ref, shift_ref, wqkv_ref,
-    wout_ref, ar_ref, dqkv_ref, gtok_ref, out_ref, small_ref,
+    after_ref, dxa_ref, qkv_ref, lse_ref, o_ref, wout_ref, dqkv_ref,
 ):
-    part = lax.rem(lax.axis_index("sp"), 2)
-    clear_first(small_ref)
-    half = own_ref.shape[1]
-    out_ref[0, pl.ds(pl.multiple_of(part * half, half), half), :] = own_ref[0]
-    out_ref[0, pl.ds(pl.multiple_of((1 - part) * half, half), half), :] = recv_ref[0]
-    dxa = dxa_ref[0]
-    ar = dxa.astype(BF16)
-    ar_ref[0] = ar
-    do = dot_nt(ar, wout_ref[0]).astype(BF16)
+    do = dot_nt(dxa_ref[0].astype(BF16), wout_ref[0]).astype(BF16)
     both = do.astype(F32) * o_ref[0].astype(F32)
     high = both.astype(BF16)
     rest = (both - high.astype(F32)).astype(BF16)
@@ -378,7 +371,6 @@
     c = lax.broadcasted_iota(jnp.int32, (HEADS, TILE), 1)
     pick = (c // HEAD == h).astype(BF16)
     centre = dot_nt(pick, high) + dot_nt(pick, rest)
-    dq, dk, dv = [], [], []
     for pair in range(HEADS // 2):
         cols = slice(pair * 128, (pair + 1) * 128)
         qp = qkv_ref[0, :, pair * 128 : (pair + 1) * 128]
@@ -396,20 +388,26 @@
             dst = (pt * (dpt - centre[row, :])).astype(BF16)
             parts.append((dot_tn(dst, kp) * SCALE, dot(dst, qp), dot(pt.astype(BF16), dop)))
         mask = head_mask(parts[0][0], 0)
-        for table, index in ((dq, 0), (dk, 1), (dv, 2)):
-            table.append(jnp.where(mask, parts[0][index], parts[1][index]).astype(BF16))
-    dh = None
-    for index, table in enumerate((dq, dk, dv)):
-        whole = jnp.concatenate(table, axis=1)
-        cols = slice(index * TILE, (index + 1) * TILE)
-        dqkv_ref[0, :, cols] = whole
-        piece = dot_nt(whole, wqkv_ref[0, :, cols])
-        dh = piece if dh is None else dh + piece
+        for index in range(3):
+            at = index * TILE + pair * 128
+            dqkv_ref[0, :, at : at + 128] = jnp.where(mask, parts[0][index], parts[1][index]).astype(BF16)
+
+
+def finish_kernel(
+    after_ref, tok_ref, dxa_ref, dqkv_ref, own_ref, recv_ref, gain_ref, shift_ref, wqkv_ref,
+    gtok_ref, out_ref, small_ref,
+):
+    part = lax.rem(lax.axis_index("sp"), 2)
+    clear_first(small_ref)
+    half = own_ref.shape[1]
+    out_ref[0, pl.ds(pl.multiple_of(part * half, half), half), :] = own_ref[0]
+    out_ref[0, pl.ds(pl.multiple_of((1 - part) * half, half), half), :] = recv_ref[0]
+    dh = dot_nt(dqkv_ref[0], wqkv_ref[0])
     gain = gain_ref[0:1, :]
     unit, inv = norm(tok_ref[0].astype(F32), gain, shift_ref[0:1, :])[1:]
     small_ref[0:1, :] += column_sum(dh * unit)
     small_ref[1:2, :] += column_sum(dh)
-    gtok_ref[0] = (dxa + norm_back(dh, unit, inv, gain)).astype(BF16)
+    gtok_ref[0] = (dxa_ref[0] + norm_back(dh, unit, inv, gain)).astype(BF16)
 
 
 def place_of(block, order, sp):
@@ -422,37 +420,39 @@
     return slot
 
 
-def put_blocks(result, first, size, at, order, keep_ref, send_ref):
+def put_blocks(result, first, size, at, order, keep_ref, send_ref, cut=None):
     sp = lax.axis_index("sp")
     part = lax.rem(sp, 2)
     low = result.astype(BF16)
+    take = slice(0, size) if cut is None else cut
+    width = take.stop - take.start
     for j in range(result.shape[0] // (2 * size)):
-        even = low[2 * j * size : (2 * j + 1) * size]
-        odd = low[(2 * j + 1) * size : (2 * j + 2) * size]
+        even = low[2 * j * size : (2 * j + 1) * size][take]
+        odd = low[(2 * j + 1) * size : (2 * j + 2) * size][take]
         slot = place_of(first + 2 * j, order[1:], sp)
-        keep_ref[slot, at : at + size, :] = jnp.where(part == 0, even, odd)
-        send_ref[slot, at : at + size, :] = jnp.where(part == 0, odd, even)
-
-
-def mlp_weights_kernel(order, h_ref, du_ref, act_ref, gr_ref, keep_ref, send_ref):
-    slots = 2 * keep_ref.shape[0]
+        keep_ref[slot, pl.ds(at, width), :] = jnp.where(part == 0, even, odd)
+        send_ref[slot, pl.ds(at, width), :] = jnp.where(part == 0, odd, even)
+
+
+def mlp_weights_kernel(orders, *refs):
+    h_ref, du_ref, act_ref, gr_ref = refs[:4]
+    extra = refs[4:-4]
+    keep_a, send_a, keep_b, send_b = refs[-4:]
+    slots = 2 * keep_a.shape[0]
     up_size = h_ref.shape[1] // slots
-    chunks = 4
-    down_size = chunks * TILE // slots
+    down_size = 4 * TILE // slots
+    zero = jnp.int32(0)
     j = pl.program_id(0)
     up = dot_tn(h_ref[...], du_ref[...])
-    at = pl.multiple_of(j * up_size, up_size)
-    sp = lax.axis_index("sp")
-    part = lax.rem(sp, 2)
-    low = up.astype(BF16)
-    for i in range(slots // 2):
-        even = low[2 * i * up_size : (2 * i + 1) * up_size]
-        odd = low[(2 * i + 1) * up_size : (2 * i + 2) * up_size]
-        slot = place_of(jnp.int32(2 * i), order[1:], sp)
-        keep_ref[slot, pl.ds(at, up_size), :] = jnp.where(part == 0, even, odd)
-        send_ref[slot, pl.ds(at, up_size), :] = jnp.where(part == 0, odd, even)
+    put_blocks(up, zero, up_size, pl.multiple_of(j * up_size, up_size), orders[0], keep_a, send_a)
     down = dot_tn(act_ref[...], gr_ref[...])
-    put_blocks(down, j * (TILE // down_size), down_size, chunks * up_size, order, keep_ref, send_ref)
+    put_blocks(down, j * (TILE // down_size), down_size, 0, orders[1], keep_b, send_b)
+    if extra:
+
+        @pl.when(j == 0)
+        def _():
+            out = dot_tn(extra[0][...], extra[1][...])
+            put_blocks(out, zero, up_size, down_size, orders[1], keep_b, send_b)
 
 
 def attn_weights_kernel(order, h_ref, dqkv_ref, o_ref, ar_ref, keep_ref, send_ref):
@@ -462,6 +462,17 @@
         cols = slice(j * TILE, (j + 1) * TILE)
         put_blocks(dot_tn(h_ref[...], dqkv_ref[:, cols]), zero, size, j * size, order, keep_ref, send_ref)
     put_blocks(dot_tn(o_ref[...], ar_ref[...]), zero, size, 3 * size, order, keep_ref, send_ref)
+
+
+def qkv_weights_kernel(orders, h_ref, dqkv_ref, keep_a, send_a, keep_b, send_b):
+    size = h_ref.shape[1] // (2 * keep_a.shape[0])
+    zero = jnp.int32(0)
+    half = size // 2
+    put_blocks(dot_tn(h_ref[...], dqkv_ref[:, :TILE]), zero, size, 0, orders[0], keep_a, send_a)
+    put_blocks(dot_tn(h_ref[...], dqkv_ref[:, TILE : 2 * TILE]), zero, size, 0, orders[1], keep_b, send_b)
+    last = dot_tn(h_ref[...], dqkv_ref[:, 2 * TILE :])
+    put_blocks(last, zero, size, size, orders[0], keep_a, send_a, slice(0, half))
+    put_blocks(last, zero, size, size, orders[1], keep_b, send_b, slice(half, size))
 
 
 def whole_spec(array):
@@ -595,45 +606,46 @@
     )
     out_recv = core_swap(out_send)
 
-    def mlp_weights(order, h, du, act, gr):
-        slots = sp_size // 2
-        shape = sds((slots, 4 * (width // sp_size) + hidden // sp_size, TILE), BF16)
+    slots = sp_size // 2
+    size = width // sp_size
+    down_size = hidden // sp_size
+
+    def buffer_specs(*heights):
+        shapes = []
+        for height in heights:
+            shapes += [sds((slots, height, TILE), BF16)] * 2
+        return [pl.BlockSpec(s.shape, lambda i: (0, 0, 0)) for s in shapes], shapes
+
+    def mlp_weights(h, du, act, gr, *extra):
+        specs, shapes = buffer_specs(4 * size, down_size + (size if extra else 0))
         return pl.pallas_call(
-            functools.partial(mlp_weights_kernel, order),
+            functools.partial(mlp_weights_kernel, (order_a, order_b)),
             grid=(hidden // TILE,),
             in_specs=[
                 whole_spec(h), pl.BlockSpec((rows, TILE), lambda i: (0, i)),
                 pl.BlockSpec((rows, TILE), lambda i: (0, i)), whole_spec(gr),
-            ],
-            out_specs=[pl.BlockSpec(shape.shape, lambda i: (0, 0, 0))] * 2,
-            out_shape=[shape, shape],
+            ] + [whole_spec(e) for e in extra],
+            out_specs=specs,
+            out_shape=shapes,
             compiler_params=params(40),
             cost_estimate=cost(2 * macs * 2 * hidden, 14e6),
-        )(h, du, act, gr)
-
-    def attn_weights(order, h, dqkv, o, ar):
-        slots = sp_size // 2
-        shape = sds((slots, 4 * (width // sp_size), TILE), BF16)
-        return pl.pallas_call(
-            functools.partial(attn_weights_kernel, order),
-            grid=(1,),
-            in_specs=[whole_spec(h), whole_spec(dqkv), whole_spec(o), whole_spec(ar)],
-            out_specs=[pl.BlockSpec(shape.shape, lambda i: (0, 0, 0))] * 2,
-            out_shape=[shape, shape],
-            compiler_params=params(40),
-            cost_estimate=cost(2 * macs * 4 * width, 8e6),
-        )(h, dqkv, o, ar)
+        )(h, du, act, gr, *extra)
 
     order_a = list(range(sp_bits))
     order_b = [0, 2, 1] + list(range(3, sp_bits))
-    mlp1 = sum_scatter(*mlp_weights(order_a, h3, du1, act1, gr1), order_a, sp_size, grp_size)
+    any_spec = pl.BlockSpec(memory_space=pl.ANY)
+    collect = functools.partial(sum_scatter, sp_size=sp_size, grp_size=grp_size)
+
+    up1_keep, up1_send, down1_keep, down1_send = mlp_weights(h3, du1, act1, gr1)
+    up1 = collect(up1_keep, up1_send, order_a)
+    down1 = collect(down1_keep, down1_send, order_b)
 
     (dx_own, dx_send, ar1, dqkv1, small2) = pl.pallas_call(
         time_backward_kernel,
         grid=(steps,),
         in_specs=[
-            smem, row_block(width), row_block(3 * width), row_block(width), whole_spec(norm_gain),
-            whole_spec(norm_shift), layer_spec(w_qkv, 1), layer_spec(w_out, 1),
+            any_spec, smem, row_block(width), row_block(3 * width), row_block(width),
+            whole_spec(norm_gain), whole_spec(norm_shift), layer_spec(w_qkv, 1), layer_spec(w_out, 1),
         ],
         out_specs=[place_block, place_block, row_block(width), row_block(3 * width), small_spec],
         out_shape=[
@@ -642,49 +654,82 @@
         scratch_shapes=place_scratch,
         compiler_params=params(56),
         cost_estimate=cost(2 * macs * 4 * width, 15e6),
-    )(frame_slot, xt, qkv1, dxb, norm_gain, norm_shift, w_qkv, w_out)
+    )(up1_keep, frame_slot, xt, qkv1, dxb, norm_gain, norm_shift, w_qkv, w_out)
     dx_recv = core_swap(dx_send)
-    attn1 = sum_scatter(*attn_weights(order_b, h2, dqkv1, o1, ar1), order_b, sp_size, grp_size)
-
-    (gr0, du0, dxa, small1) = pl.pallas_call(
+    specs, shapes = buffer_specs(4 * size)
+    attn1_keep, attn1_send = pl.pallas_call(
+        functools.partial(attn_weights_kernel, order_a),
+        grid=(1,),
+        in_specs=[whole_spec(h2), whole_spec(dqkv1), whole_spec(o1), whole_spec(ar1)],
+        out_specs=specs,
+        out_shape=shapes,
+        compiler_params=params(40),
+        cost_estimate=cost(2 * macs * 4 * width, 8e6),
+    )(h2, dqkv1, o1, ar1)
+    attn1 = collect(attn1_keep, attn1_send, order_a)
+
+    (gr0, du0, dxa, ar0, small1) = pl.pallas_call(
         space_mlp_back_kernel,
         grid=(frames,),
         in_specs=[
-            half_block, half_block, frame_block(width), frame_block(hidden), whole_spec(norm_gain),
-            whole_spec(norm_shift), layer_spec(w_up, 0), layer_spec(w_down, 0),
-        ],
-        out_specs=[frame_block(width), frame_block(hidden), frame_block(width), small_spec],
-        out_shape=[frame_out(width, BF16), frame_out(hidden, BF16), frame_out(width, F32), small_shape],
+            any_spec, half_block, half_block, frame_block(width), frame_block(hidden),
+            whole_spec(norm_gain), whole_spec(norm_shift), layer_spec(w_up, 0), layer_spec(w_down, 0),
+        ],
+        out_specs=[
+            frame_block(width), frame_block(hidden), frame_block(width), frame_block(width), small_spec,
+        ],
+        out_shape=[
+            frame_out(width, BF16), frame_out(hidden, BF16), frame_out(width, F32),
+            frame_out(width, BF16), small_shape,
+        ],
         compiler_params=params(56),
         cost_estimate=cost(2 * macs * 2 * hidden, 20e6),
-    )(dx_own, dx_recv, xa, slope0, norm_gain, norm_shift, w_up, w_down)
+    )(attn1_keep, dx_own, dx_recv, xa, slope0, norm_gain, norm_shift, w_up, w_down)
     flat = lambda a: a.reshape(rows, a.shape[-1])
-    mlp0 = sum_scatter(
-        *mlp_weights(order_b, flat(h1), flat(du0), flat(act0), flat(gr0)), order_b, sp_size, grp_size
+    up0_keep, up0_send, down0_keep, down0_send = mlp_weights(
+        flat(h1), flat(du0), flat(act0), flat(gr0), flat(o0), flat(ar0)
     )
-
-    (ar0, dqkv0, grad_tokens, output, small0) = pl.pallas_call(
+    up0 = collect(up0_keep, up0_send, order_a)
+    down0 = collect(down0_keep, down0_send, order_b)
+
+    dqkv0 = pl.pallas_call(
         space_attn_back_kernel,
         grid=(frames,),
         in_specs=[
-            frame_block(width), frame_block(width), frame_block(3 * width),
-            step_spec((1, HEADS, patches)), frame_block(width), half_block, half_block,
-            whole_spec(norm_gain), whole_spec(norm_shift), layer_spec(w_qkv, 0), layer_spec(w_out, 0),
-        ],
-        out_specs=[
-            frame_block(width), frame_block(3 * width), frame_block(width), frame_block(width),
-            small_spec,
-        ],
-        out_shape=[
-            frame_out(width, BF16), frame_out(3 * width, BF16), frame_out(width, BF16),
-            frame_out(width, BF16), small_shape,
-        ],
+            any_spec, frame_block(width), frame_block(3 * width), step_spec((1, HEADS, patches)),
+            frame_block(width), layer_spec(w_out, 0),
+        ],
+        out_specs=frame_block(3 * width),
+        out_shape=frame_out(3 * width, BF16),
         compiler_params=params(56),
         cost_estimate=cost(2 * macs * 6 * width, 20e6),
-    )(tokens, dxa, qkv0, lse0, o0, out_own, out_recv, norm_gain, norm_shift, w_qkv, w_out)
-    attn0 = sum_scatter(
-        *attn_weights(order_a, flat(h0), flat(dqkv0), flat(o0), flat(ar0)), order_a, sp_size, grp_size
-    )
+    )(up0_keep, dxa, qkv0, lse0, o0, w_out)
+
+    specs, shapes = buffer_specs(size + size // 2, size + size // 2)
+    qkva_keep, qkva_send, qkvb_keep, qkvb_send = pl.pallas_call(
+        functools.partial(qkv_weights_kernel, (order_a, order_b)),
+        grid=(1,),
+        in_specs=[whole_spec(flat(h0)), whole_spec(flat(dqkv0))],
+        out_specs=specs,
+        out_shape=shapes,
+        compiler_params=params(40),
+        cost_estimate=cost(2 * macs * 3 * width, 8e6),
+    )(flat(h0), flat(dqkv0))
+    qkva = collect(qkva_keep, qkva_send, order_a)
+    qkvb = collect(qkvb_keep, qkvb_send, order_b)
+
+    grad_tokens, output, small0 = pl.pallas_call(
+        finish_kernel,
+        grid=(frames,),
+        in_specs=[
+            any_spec, frame_block(width), frame_block(width), frame_block(3 * width), half_block,
+            half_block, whole_spec(norm_gain), whole_spec(norm_shift), layer_spec(w_qkv, 0),
+        ],
+        out_specs=[frame_block(width), frame_block(width), small_spec],
+        out_shape=[frame_out(width, BF16), frame_out(width, BF16), small_shape],
+        compiler_params=params(56),
+        cost_estimate=cost(2 * macs * 3 * width, 8e6),
+    )(qkva_keep, tokens, dxa, dqkv0, out_own, out_recv, norm_gain, norm_shift, w_qkv)
 
     small = jnp.concatenate([small0, small1, small2, small3], axis=0).astype(BF16)
     for b in range(sp_bits):
@@ -698,25 +743,23 @@
         size = array.shape[1] // sp_size
         return lax.dynamic_slice_in_dim(array, sp * size, size, axis=1)
 
-    def up_part(a):
-        size = width // sp_size
-        return a[: 4 * size].reshape(4, size, TILE).transpose(1, 0, 2).reshape(size, hidden)
-
-    def qkv_part(a):
-        size = width // sp_size
-        return a[: 3 * size].reshape(3, size, TILE).transpose(1, 0, 2).reshape(size, 3 * width)
-
-    size = width // sp_size
+    def columns(parts):
+        return jnp.concatenate(parts, axis=1)
+
+    def blocks(a, count):
+        return columns([a[i * size : (i + 1) * size] for i in range(count)])
+
+    third = jnp.concatenate([qkva[size:], qkvb[size:]], axis=0)
     return (
         output,
         grad_tokens,
         mine(small[:, 0]),
         mine(small[:, 1]),
-        jnp.stack([qkv_part(attn0), qkv_part(attn1)]),
-        jnp.stack([attn0[3 * size :], attn1[3 * size :]]),
-        jnp.stack([up_part(mlp0), up_part(mlp1)]),
+        jnp.stack([columns([qkva[:size], qkvb[:size], third]), blocks(attn1, 3)]),
+        jnp.stack([down0[down_size:], attn1[3 * size :]]),
+        jnp.stack([blocks(up0, 4), blocks(up1, 4)]),
         mine(small[1::2, 4:].reshape(2, hidden)),
-        jnp.stack([mlp0[4 * size :], mlp1[4 * size :]]),
+        jnp.stack([down0[:down_size], down1]),
         mine(small[1::2, 2]),
     )
 

time: 242 us -> 299 us (1.24)
  starting transfers between devices: 27.8 us -> 57 us
  local copies, waits for them, and re-layouts: 11.9 us -> 29.5 us
  waiting for transfers between devices: 70.5 us -> 84.9 us
  other arithmetic: 18.4 us -> 9.61 us
  Pallas kernels: 112 us -> 116 us
    ppermute x29 -> x44, starting transfers between devices: 27.8 us -> 57 us  [swap(): return lax.ppermute(array, axis, [(i, i ^ 1 << bit) for i in range(size)])]
    unnamed x44 -> x76, local copies, waits for them, and re-layouts: 8.66 us -> 27.5 us
    ppermute x29 -> x44, waiting for transfers between devices: 70.5 us -> 84.9 us  [swap(): return lax.ppermute(array, axis, [(i, i ^ 1 << bit) for i in range(size)])]
    convert_element_type x20 -> x32, other arithmetic: 12.9 us -> 3.93 us  [add_low(): return (a.astype(F32) + b.astype(F32)).astype(BF16)]
    pallas_call x7 -> x8, Pallas kernels: 60.4 us -> 65.1 us  [the longest x1 17.2 us: shards(): pl.pallas_call(space_attn_back_kernel, grid=(frames,), in_specs=[any_spec...]
  transfers between devices with their start and end apart: 29 -> 44, of which waited for: 16 -> 23; matrix products, arithmetic and copies ran while one was open for 8% -> 3% of each run, Pallas kernels for 22% -> 21%
where the time goes in v2:
time: 299 us
  Pallas kernels  116 us (39%)
  waiting for transfers between devices  84.9 us (28%)
  starting transfers between devices  57 us (19%)
  local copies, waits for them, and re-layouts  29.5 us (10%)
  other arithmetic  9.61 us (3%)
    ppermute x44, waiting for transfers between devices, swap(): return lax.ppermute(array, axis, [(i, i ^ 1 << bit) for i in range(size)])  84.9 us
    ppermute x44, starting transfers between devices, swap(): return lax.ppermute(array, axis, [(i, i ^ 1 << bit) for i in range(size)])  57 us
    pallas_call x1, Pallas kernels, shards(): pl.pallas_call(time_forward_kernel, grid=(steps,), in_specs=[smem, place_...  28.7 us
    unnamed x76, local copies, waits for them, and re-layouts  27.5 us
    pallas_call x1, Pallas kernels, shards(): pl.pallas_call(space_forward_kernel, grid=(frames,), in_specs=[frame_bloc...  22.6 us
    pallas_call x1, Pallas kernels, shards(): pl.pallas_call(space_attn_back_kernel, grid=(frames,), in_specs=[any_spec...  17.2 us
    pallas_call x2, Pallas kernels, mlp_weights(): pl.pallas_call(functools.partial(mlp_weights_kernel, (order_a, order_b)),...  14.1 us
    pallas_call x1, Pallas kernels, shards(): pl.pallas_call(space_mlp_back_kernel, grid=(frames,), in_specs=[any_spec,...  11.4 us
  transfers between devices with their start and end apart: 44, of which 23 were waited for; matrix products, arithmetic and copies ran while one was open for 3% of the time, Pallas kernels for 21%

profile of v2, /device:TPU:0, one launch (start us, length us, event | category | flops | bytes accessed | tf_op | source)
XLA Modules:
  0.0 298.7 jit_solution(18275267718761044185)
XLA Ops:
  1.2 22.6 %shard_map.186 = (bf16[4,128,512]{2,1,0:T(8,128)(2,1)}, bf16[4,128,512]{2,1,0:T(8,128)(2,1)}, bf16[4,256,512]{2,1,0:T(8,128)(2,1)}, bf16[4,256,1536]{2,1,0:T(8,1...) custom-call(bf16[4,256,512]{2,1,0:T(8,128)(2,1)} %tok_ref.3, ...), custom_call_target="tpu_custom_call" | custom-call | flops 6442450944 | bytes 30000000 | tf_op jit(solution)/shard_map/pallas_call | solution.py:543
  23.9 2.1 collective-permute-done.recv_ref
  27.2 28.7 %shard_map.187 = (bf16[4,128,512]{2,1,0:T(8,128)(2,1)}, bf16[4,128,512]{2,1,0:T(8,128)(2,1)}, bf16[1024,512]{1,0:T(8,128)(2,1)}, bf16[1024,512]{1,0:T(8,128)(2,1...) custom-call(s32[8,8]{1,0:T(8,128)} %slots_ref.3, ...), custom_call_target="tpu_custom_call" | custom-call | flops 10737418240 | bytes 30000000 | tf_op jit(solution)/shard_map/pallas_call | solution.py:581
  55.9 2.2 copy-done.27
  60.5 6.6 %shard_map.188 = (bf16[8,128,512]{2,1,0:T(8,128)(2,1)S(1)}, bf16[8,128,512]{2,1,0:T(8,128)(2,1)S(1)}, bf16[8,128,512]{2,1,0:T(8,128)(2,1)S(1)}, bf16[8,128,512]{2,1,0:T(8,128)(2,1)S(1)}) custom-call(bf16[1024,512]{1,0:T(8,128)(2,1)S(1)} %copy-done.28, bf16[1024,2048]{1,0:T(8,128)(2,1)S(1)} %copy-done.27, bf16[1024,2048]{1,0:T(8,128)(2,1)} %get-tuple-element.66.refs_2_, ...), custom_call_target="tpu_custom_call" | custom-call | flops 4294967296 | bytes 14000000 | tf_op jit(solution)/shard_map/pallas_call | solution.py:621
  71.1 11.1 %shard_map.189 = (bf16[4,128,512]{2,1,0:T(8,128)(2,1)}, bf16[4,128,512]{2,1,0:T(8,128)(2,1)}, bf16[1024,512]{1,0:T(8,128)(2,1)}, bf16[1024,1536]{1,0:T(8,128)(2,1)}, f32[8,512]{1,0:T(8,128)}) custom-call(bf16[8,128,512]{2,1,0:T(8,128)(2,1)} %copy-done.2, s32[8,8]{1,0:T(8,128)} %slots_ref.3, bf16[1024,512]{1,0:T(8,128)(2,1)} %get-tuple-element.69.x_ref, ...), custom_call_target="tpu_custom_call" | custom-call | flops 2147483648 | bytes 15000000 | tf_op jit(solution)/shard_map/pallas_call | solution.py:643
  83.6 1.9 copy-done.12
  86.7 2.4 shard_map.190
  91.8 11.4 %shard_map.191 = (bf16[4,256,512]{2,1,0:T(8,128)(2,1)}, bf16[4,256,2048]{2,1,0:T(8,128)(2,1)}, f32[4,256,512]{2,1,0:T(8,128)}, bf16[4,256,512]{2,1,0:T(8,128)(2,1)}, f32[8,512]{1,0:T(8,128)}) custom-call(bf16[8,128,512]{2,1,0:T(8,128)(2,1)} %copy-done, bf16[4,128,512]{2,1,0:T(8,128)(2,1)} %get-tuple-element.76.own_ref, bf16[4,128,512]{2,1,0:T(8,128)(2,1)} %copy-done.30, ...), custom_call_target="tpu_custom_call" | custom-call | flops 4294967296 | bytes 20000000 | tf_op jit(solution)/shard_map/pallas_call | solution.py:671
  103.2 2.2 copy-done.11
  107.9 7.4 %shard_map.192 = (bf16[8,128,512]{2,1,0:T(8,128)(2,1)S(1)}, bf16[8,128,512]{2,1,0:T(8,128)(2,1)S(1)}, bf16[8,160,512]{2,1,0:T(8,128)(2,1)S(1)}, bf16[8,160,512]{2,1,0:T(8,128)(2,1)S(1)}) custom-call(bf16[1024,512]{1,0:T(8,128)(2,1)S(1)} %bitcast.69, bf16[1024,2048]{1,0:T(8,128)(2,1)S(1)} %bitcast.64, bf16[1024,2048]{1,0:T(8,128)(2,1)} %bitcast.74, ...), custom_call_target="tpu_custom_call" | custom-call | flops 4294967296 | bytes 14000000 | tf_op jit(solution)/shard_map/pallas_call | solution.py:621
  118.4 17.2 %shard_map.193.dqkv_ref = bf16[4,256,1536]{2,1,0:T(8,128)(2,1)} custom-call(bf16[8,128,512]{2,1,0:T(8,128)(2,1)} %copy-done.7, f32[4,256,512]{2,1,0:T(8,128)} %get-tuple-element.86.dxa_ref, bf16[4,256,1536]{2,1,0:T(8,128)(2,1)} %get-tuple-element.87.qkv_ref, f32[4,8,256]{2,1,0:T(8,128)} %get-tuple-element.88.lse_ref, ...), custom_call_target="tpu_custom_call" | custom-call | flops 3221225472 | bytes 20000000 | tf_op jit(solution)/shard_map/pallas_call | solution.py:695
  135.6 1.9 copy-done.4
  137.5 1.8 shard_map.194
  141.6 7.1 %shard_map.195 = (bf16[4,256,512]{2,1,0:T(8,128)(2,1)}, bf16[4,256,512]{2,1,0:T(8,128)(2,1)}, f32[8,512]{1,0:T(8,128)}) custom-call(bf16[8,48,512]{2,1,0:T(8,128)(2,1)} %copy-done.5, bf16[4,256,512]{2,1,0:T(8,128)(2,1)} %tok_ref.3, f32[4,256,512]{2,1,0:T(8,128)} %get-tuple-element.86.dxa_ref, bf16[4,256,1536]{2,1,0:T(8,128)(2,1)} %shard_map.193.dqkv_ref, ...), custom_call_target="tpu_custom_call" | custom-call | flops 1610612736 | bytes 8000000 | tf_op jit(solution)/shard_map/pallas_call | solution.py:721
  150.8 2.7 collective-permute-start.5
  153.5 1.9 collective-permute-done.5
  155.4 2.2 collective-permute-start.6
  157.6 1.9 collective-permute-done.6
  159.5 3.1 %collective-permute-start.7 = (bf16[32,512]{1,0:T(8,128)(2,1)S(1)}, bf16[32,512]{1,0:T(8,128)(2,1)S(1)}, u32[]{:S(2)}, u32[]{:S(2)}) collective-permute-start(bf16[32,512]{1,0:T(8,128)(2,1)S(1)} %add_convert_fusion.58), channel_id=1, source_target_pairs={{0,8},{1,9},{2,10},{3,11},{4,12},{5,13},{6,14},{7,15},{8,0},{9,1},... | collective-permute-start | bytes 98312 | tf_op jit(solution)/shard_map/ppermute | solution.py:509
  162.6 1.9 collective-permute-done.7
  165.1 1.9 collective-permute-start.8
  172.0 1.9 collective-permute-done.9
  176.7 1.6 collective-permute-start.15
  179.6 3.0 collective-permute-done.10
  185.1 11.9 %collective-permute-done.11 = bf16[2,48,512]{2,1,0:T(8,128)(2,1)S(1)} collective-permute-done((bf16[2,48,512]{2,1,0:T(8,128)(2,1)S(1)}, bf16[2,48,512]{2,1,0:T(8,128)(2,1)S(1)}, u32[]{:S(2)}, u32[]{:S(2)}) %collective-permute-start.11) | collective-permute-done | bytes 98336 | tf_op jit(solution)/shard_map/ppermute | solution.py:509
  198.6 3.0 %collective-permute-done.16 = bf16[2,48,512]{2,1,0:T(8,128)(2,1)S(1)} collective-permute-done((bf16[2,48,512]{2,1,0:T(8,128)(2,1)S(1)}, bf16[2,48,512]{2,1,0:T(8,128)(2,1)S(1)}, u32[]{:S(2)}, u32[]{:S(2)}) %collective-permute-start.16) | collective-permute-done | bytes 98336 | tf_op jit(solution)/shard_map/ppermute | solution.py:509
  201.6 2.7 collective-permute-start.12
  204.4 2.4 collective-permute-done.12
  206.8 2.7 collective-permute-start.17
  209.5 2.3 collective-permute-done.17
  212.4 3.5 %collective-permute-done.13 = bf16[1,48,512]{2,1,0:T(8,128)(2,1)S(1)} collective-permute-done((bf16[1,48,512]{2,1,0:T(8,128)(2,1)S(1)}, bf16[1,48,512]{2,1,0:T(8,128)(2,1)S(1)}, u32[]{:S(2)}, u32[]{:S(2)}) %collective-permute-start.13) | collective-permute-done | bytes 49184 | tf_op jit(solution)/shard_map/ppermute | solution.py:509
  216.4 3.5 %collective-permute-done.18 = bf16[1,48,512]{2,1,0:T(8,128)(2,1)S(1)} collective-permute-done((bf16[1,48,512]{2,1,0:T(8,128)(2,1)S(1)}, bf16[1,48,512]{2,1,0:T(8,128)(2,1)S(1)}, u32[]{:S(2)}, u32[]{:S(2)}) %collective-permute-start.18) | collective-permute-done | bytes 49184 | tf_op jit(solution)/shard_map/ppermute | solution.py:509
  221.6 2.2 collective-permute-start.36
  224.7 7.8 %collective-permute-done.20 = bf16[4,128,512]{2,1,0:T(8,128)(2,1)S(1)} collective-permute-done((bf16[4,128,512]{2,1,0:T(8,128)(2,1)S(1)}, bf16[4,128,512]{2,1,0:T(8,128)(2,1)S(1)}, u32[]{:S(2)}, u32[]{:S(2)}) %collective-permute-start.20) | collective-permute-done | bytes 524320 | tf_op jit(solution)/shard_map/ppermute | solution.py:509
  232.7 4.3 %collective-permute-start.21 = (bf16[2,128,512]{2,1,0:T(8,128)(2,1)S(1)}, bf16[2,128,512]{2,1,0:T(8,128)(2,1)S(1)}, u32[]{:S(2)}, u32[]{:S(2)}) collective-permute-start(bf16[2,128,512]{2,1,0:T(8,128)(2,1)S(1)} %get-tuple-element.127), channel_id=1, source_target_pairs={{0,4},{1,5},{2,6},{3,7},{4,0},{5,1},{6,2},{7,3},{8,12},{9,13},{10,... | collective-permute-start | bytes 786440 | tf_op jit(solution)/shard_map/ppermute | solution.py:509
  238.9 2.9 collective-permute-start.37
  242.0 3.6 %collective-permute-done.21 = bf16[2,128,512]{2,1,0:T(8,128)(2,1)S(1)} collective-permute-done((bf16[2,128,512]{2,1,0:T(8,128)(2,1)S(1)}, bf16[2,128,512]{2,1,0:T(8,128)(2,1)S(1)}, u32[]{:S(2)}, u32[]{:S(2)}) %collective-permute-start.21) | collective-permute-done | bytes 262176 | tf_op jit(solution)/shard_map/ppermute | solution.py:509
  245.6 4.1 %collective-permute-start.22 = (bf16[1,128,512]{2,1,0:T(8,128)(2,1)S(1)}, bf16[1,128,512]{2,1,0:T(8,128)(2,1)S(1)}, u32[]{:S(2)}, u32[]{:S(2)}) collective-permute-start(bf16[1,128,512]{2,1,0:T(8,128)(2,1)S(1)} %add_convert_fusion.42), channel_id=1, source_target_pairs={{0,8},{1,9},{2,10},{3,11},{4,12},{5,13},{6,14},{7,15},{8,0},{9,1},... | collective-permute-start | bytes 393224 | tf_op jit(solution)/shard_map/ppermute | solution.py:509
  250.2 2.5 collective-permute-start.25
  255.6 3.6 %collective-permute-done.23 = bf16[1,128,512]{2,1,0:T(8,128)(2,1)S(1)} collective-permute-done((bf16[1,128,512]{2,1,0:T(8,128)(2,1)S(1)}, bf16[1,128,512]{2,1,0:T(8,128)(2,1)S(1)}, u32[]{:S(2)}, u32[]{:S(2)}) %collective-permute-start.23) | collective-permute-done | bytes 131104 | tf_op jit(solution)/shard_map/ppermute | solution.py:509
  261.7 4.1 %collective-permute-done.31 = bf16[2,128,512]{2,1,0:T(8,128)(2,1)S(1)} collective-permute-done((bf16[2,128,512]{2,1,0:T(8,128)(2,1)S(1)}, bf16[2,128,512]{2,1,0:T(8,128)(2,1)S(1)}, u32[]{:S(2)}, u32[]{:S(2)}) %collective-permute-start.31) | collective-permute-done | bytes 262176 | tf_op jit(solution)/shard_map/ppermute | solution.py:509
  265.9 2.8 collective-permute-start.32
  268.8 7.5 %collective-permute-done.32 = bf16[1,128,512]{2,1,0:T(8,128)(2,1)S(1)} collective-permute-done((bf16[1,128,512]{2,1,0:T(8,128)(2,1)S(1)}, bf16[1,128,512]{2,1,0:T(8,128)(2,1)S(1)}, u32[]{:S(2)}, u32[]{:S(2)}) %collective-permute-start.32) | collective-permute-done | bytes 131104 | tf_op jit(solution)/shard_map/ppermute | solution.py:509
  278.7 3.6 %collective-permute-done.33 = bf16[1,128,512]{2,1,0:T(8,128)(2,1)S(1)} collective-permute-done((bf16[1,128,512]{2,1,0:T(8,128)(2,1)S(1)}, bf16[1,128,512]{2,1,0:T(8,128)(2,1)S(1)}, u32[]{:S(2)}, u32[]{:S(2)}) %collective-permute-start.33) | collective-permute-done | bytes 131104 | tf_op jit(solution)/shard_map/ppermute | solution.py:509
  282.4 1.9 collective-permute-done.26
  284.5 7.2 %collective-permute-done.27 = bf16[1,160,512]{2,1,0:T(8,128)(2,1)S(1)} collective-permute-done((bf16[1,160,512]{2,1,0:T(8,128)(2,1)S(1)}, bf16[1,160,512]{2,1,0:T(8,128)(2,1)S(1)}, u32[]{:S(2)}, u32[]{:S(2)}) %collective-permute-start.27) | collective-permute-done | bytes 163872 | tf_op jit(solution)/shard_map/ppermute | solution.py:509
  293.2 3.9 %collective-permute-done.28 = bf16[1,160,512]{2,1,0:T(8,128)(2,1)S(1)} collective-permute-done((bf16[1,160,512]{2,1,0:T(8,128)(2,1)S(1)}, bf16[1,160,512]{2,1,0:T(8,128)(2,1)S(1)}, u32[]{:S(2)}, u32[]{:S(2)}) %collective-permute-start.28) | collective-permute-done | bytes 163872 | tf_op jit(solution)/shard_map/ppermute | solution.py:509
  (191 shorter events, 54.7 us)
Async XLA Ops:
  0.6 25.4 %collective-permute-start.1 = (bf16[4,256,512]{2,1,0:T(8,128)(2,1)}, bf16[4,256,512]{2,1,0:T(8,128)(2,1)S(1)}, u32[]{:S(2)}, u32[]{:S(2)}) collective-permute-start(bf16[4,256,512]{2,1,0:T(8,128)(2,1)} %cot_ref.1), channel_id=1, source_target_pairs={{0,1},{1,0},{2,3},{3,2},{4,5},{5,4},{6,7},{7,6},{8,9},{9,8},{10,11... | collective-permute-start | bytes 3145736 | tf_op jit(solution)/shard_map/ppermute | solution.py:509
  23.8 2.2 collective-permute-start
  82.2 8.8 %collective-permute-start.2 = (bf16[4,128,512]{2,1,0:T(8,128)(2,1)}, bf16[4,128,512]{2,1,0:T(8,128)(2,1)S(1)}, u32[]{:S(2)}, u32[]{:S(2)}) collective-permute-start(bf16[4,128,512]{2,1,0:T(8,128)(2,1)} %get-tuple-element.77), channel_id=1, source_target_pairs={{0,1},{1,0},{2,3},{3,2},{4,5},{5,4},{6,7},{7,6},{8,9},{9,8},{10,11... | collective-permute-start | bytes 1572872 | tf_op jit(solution)/shard_map/ppermute | solution.py:509
  82.4 58.4 %collective-permute-start.3 = (bf16[4,128,512]{2,1,0:T(8,128)(2,1)S(1)}, bf16[4,128,512]{2,1,0:T(8,128)(2,1)S(1)}, u32[]{:S(2)}, u32[]{:S(2)}) collective-permute-start(bf16[4,128,512]{2,1,0:T(8,128)(2,1)S(1)} %copy-done.35), channel_id=1, source_target_pairs={{0,1},{1,0},{2,3},{3,2},{4,5},{5,4},{6,7},{7,6},{8,9},{9,8},{10,11... | collective-permute-start | bytes 1572872 | tf_op jit(solution)/shard_map/ppermute | solution.py:509
  118.4 17.2 %copy-start.22 = (bf16[4,256,512]{2,1,0:T(8,128)(2,1)S(1)}, bf16[4,256,512]{2,1,0:T(8,128)(2,1)}, u32[]{:S(2)}) copy-start(bf16[4,256,512]{2,1,0:T(8,128)(2,1)} %get-tuple-element.59) | copy-start | bytes 3145732
  141.6 32.4 %copy-start.6 = (bf16[8,48,512]{2,1,0:T(8,128)(2,1)S(1)}, bf16[8,48,512]{2,1,0:T(8,128)(2,1)}, u32[]{:S(2)}) copy-start(bf16[8,48,512]{2,1,0:T(8,128)(2,1)} %copy-done.5) | copy-start | bytes 1179652
  148.7 27.6 %copy-start.3 = (bf16[8,128,512]{2,1,0:T(8,128)(2,1)S(1)}, bf16[8,128,512]{2,1,0:T(8,128)(2,1)}, u32[]{:S(2)}) copy-start(bf16[8,128,512]{2,1,0:T(8,128)(2,1)} %copy-done.2) | copy-start | bytes 3145732
  149.6 1.2 collective-permute-start.4
  150.8 4.6 %collective-permute-start.5 = (bf16[32,512]{1,0:T(8,128)(2,1)S(1)}, bf16[32,512]{1,0:T(8,128)(2,1)S(1)}, u32[]{:S(2)}, u32[]{:S(2)}) collective-permute-start(bf16[32,512]{1,0:T(8,128)(2,1)S(1)} %add_convert_fusion.60), channel_id=1, source_target_pairs={{0,2},{1,3},{2,0},{3,1},{4,6},{5,7},{6,4},{7,5},{8,10},{9,11},{10,... | collective-permute-start | bytes 98312 | tf_op jit(solution)/shard_map/ppermute | solution.py:509
  155.4 4.1 %collective-permute-start.6 = (bf16[32,512]{1,0:T(8,128)(2,1)S(1)}, bf16[32,512]{1,0:T(8,128)(2,1)S(1)}, u32[]{:S(2)}, u32[]{:S(2)}) collective-permute-start(bf16[32,512]{1,0:T(8,128)(2,1)S(1)} %add_convert_fusion.59), channel_id=1, source_target_pairs={{0,4},{1,5},{2,6},{3,7},{4,0},{5,1},{6,2},{7,3},{8,12},{9,13},{10,... | collective-permute-start | bytes 98312 | tf_op jit(solution)/shard_map/ppermute | solution.py:509
  159.5 5.0 %collective-permute-start.7 = (bf16[32,512]{1,0:T(8,128)(2,1)S(1)}, bf16[32,512]{1,0:T(8,128)(2,1)S(1)}, u32[]{:S(2)}, u32[]{:S(2)}) collective-permute-start(bf16[32,512]{1,0:T(8,128)(2,1)S(1)} %add_convert_fusion.58), channel_id=1, source_target_pairs={{0,8},{1,9},{2,10},{3,11},{4,12},{5,13},{6,14},{7,15},{8,0},{9,1},... | collective-permute-start | bytes 98312 | tf_op jit(solution)/shard_map/ppermute | solution.py:509
  165.1 4.2 %collective-permute-start.8 = (bf16[32,512]{1,0:T(8,128)(2,1)}, bf16[32,512]{1,0:T(8,128)(2,1)}, u32[]{:S(2)}, u32[]{:S(2)}) collective-permute-start(bf16[32,512]{1,0:T(8,128)(2,1)} %add_convert_fusion.57), channel_id=1, source_target_pairs={{0,16},{16,0},{1,17},{17,1},{2,18},{18,2},{3,19},{19,3},{4,20},{20... | collective-permute-start | bytes 98312 | tf_op jit(solution)/shard_map/ppermute | solution.py:509
  166.9 7.8 %collective-permute-start.34 = (bf16[8,128,512]{2,1,0:T(8,128)(2,1)}, bf16[8,128,512]{2,1,0:T(8,128)(2,1)S(1)}, u32[]{:S(2)}, u32[]{:S(2)}) collective-permute-start(bf16[8,128,512]{2,1,0:T(8,128)(2,1)} %copy-done.16), channel_id=1, source_target_pairs={{0,1},{1,0},{2,3},{3,2},{4,5},{5,4},{6,7},{7,6},{8,9},{9,8},{10,11... | collective-permute-start | bytes 3145736 | tf_op jit(solution)/shard_map/ppermute | solution.py:509
  166.9 11.7 %collective-permute-start.39 = (bf16[8,128,512]{2,1,0:T(8,128)(2,1)}, bf16[8,128,512]{2,1,0:T(8,128)(2,1)S(1)}, u32[]{:S(2)}, u32[]{:S(2)}) collective-permute-start(bf16[8,128,512]{2,1,0:T(8,128)(2,1)} %copy-done.15), channel_id=1, source_target_pairs={{0,1},{1,0},{2,3},{3,2},{4,5},{5,4},{6,7},{7,6},{8,9},{9,8},{10,11... | collective-permute-start | bytes 3145736 | tf_op jit(solution)/shard_map/ppermute | solution.py:509
  167.5 9.3 %collective-permute-start.19 = (bf16[8,128,512]{2,1,0:T(8,128)(2,1)}, bf16[8,128,512]{2,1,0:T(8,128)(2,1)S(1)}, u32[]{:S(2)}, u32[]{:S(2)}) collective-permute-start(bf16[8,128,512]{2,1,0:T(8,128)(2,1)} %copy-done.17), channel_id=1, source_target_pairs={{0,1},{1,0},{2,3},{3,2},{4,5},{5,4},{6,7},{7,6},{8,9},{9,8},{10,11... | collective-permute-start | bytes 3145736 | tf_op jit(solution)/shard_map/ppermute | solution.py:509
  167.5 6.5 %collective-permute-start.9 = (bf16[8,48,512]{2,1,0:T(8,128)(2,1)}, bf16[8,48,512]{2,1,0:T(8,128)(2,1)S(1)}, u32[]{:S(2)}, u32[]{:S(2)}) collective-permute-start(bf16[8,48,512]{2,1,0:T(8,128)(2,1)} %copy-done.21), channel_id=1, source_target_pairs={{0,1},{1,0},{2,3},{3,2},{4,5},{5,4},{6,7},{7,6},{8,9},{9,8},{10,11... | collective-permute-start | bytes 1179656 | tf_op jit(solution)/shard_map/ppermute | solution.py:509
  169.3 4.9 %collective-permute-start.14 = (bf16[8,48,512]{2,1,0:T(8,128)(2,1)S(1)}, bf16[8,48,512]{2,1,0:T(8,128)(2,1)S(1)}, u32[]{:S(2)}, u32[]{:S(2)}) collective-permute-start(bf16[8,48,512]{2,1,0:T(8,128)(2,1)S(1)} %get-tuple-element.100), channel_id=1, source_target_pairs={{0,1},{1,0},{2,3},{3,2},{4,5},{5,4},{6,7},{7,6},{8,9},{9,8},{10,11... | collective-permute-start | bytes 1179656 | tf_op jit(solution)/shard_map/ppermute | solution.py:509
  173.9 63.0 %collective-permute-start.29 = (bf16[8,128,512]{2,1,0:T(8,128)(2,1)}, bf16[8,128,512]{2,1,0:T(8,128)(2,1)S(1)}, u32[]{:S(2)}, u32[]{:S(2)}) collective-permute-start(bf16[8,128,512]{2,1,0:T(8,128)(2,1)} %copy-done.14), channel_id=1, source_target_pairs={{0,1},{1,0},{2,3},{3,2},{4,5},{5,4},{6,7},{7,6},{8,9},{9,8},{10,11... | collective-permute-start | bytes 3145736 | tf_op jit(solution)/shard_map/ppermute | solution.py:509
  174.2 75.6 %collective-permute-start.24 = (bf16[8,160,512]{2,1,0:T(8,128)(2,1)}, bf16[8,160,512]{2,1,0:T(8,128)(2,1)S(1)}, u32[]{:S(2)}, u32[]{:S(2)}) collective-permute-start(bf16[8,160,512]{2,1,0:T(8,128)(2,1)} %copy-done.13), channel_id=1, source_target_pairs={{0,1},{1,0},{2,3},{3,2},{4,5},{5,4},{6,7},{7,6},{8,9},{9,8},{10,11... | collective-permute-start | bytes 3932168 | tf_op jit(solution)/shard_map/ppermute | solution.py:509
  174.8 7.8 %collective-permute-start.10 = (bf16[4,48,512]{2,1,0:T(8,128)(2,1)S(1)}, bf16[4,48,512]{2,1,0:T(8,128)(2,1)S(1)}, u32[]{:S(2)}, u32[]{:S(2)}) collective-permute-start(bf16[4,48,512]{2,1,0:T(8,128)(2,1)S(1)} %get-tuple-element.129), channel_id=1, source_target_pairs={{0,2},{1,3},{2,0},{3,1},{4,6},{5,7},{6,4},{7,5},{8,10},{9,11},{10,... | collective-permute-start | bytes 589832 | tf_op jit(solution)/shard_map/ppermute | solution.py:509
  176.7 7.5 %collective-permute-start.15 = (bf16[4,48,512]{2,1,0:T(8,128)(2,1)S(1)}, bf16[4,48,512]{2,1,0:T(8,128)(2,1)S(1)}, u32[]{:S(2)}, u32[]{:S(2)}) collective-permute-start(bf16[4,48,512]{2,1,0:T(8,128)(2,1)S(1)} %get-tuple-element.131), channel_id=1, source_target_pairs={{0,4},{1,5},{2,6},{3,7},{4,0},{5,1},{6,2},{7,3},{8,12},{9,13},{10,... | collective-permute-start | bytes 589832 | tf_op jit(solution)/shard_map/ppermute | solution.py:509
  178.7 42.7 %collective-permute-start.35 = (bf16[4,128,512]{2,1,0:T(8,128)(2,1)S(1)}, bf16[4,128,512]{2,1,0:T(8,128)(2,1)S(1)}, u32[]{:S(2)}, u32[]{:S(2)}) collective-permute-start(bf16[4,128,512]{2,1,0:T(8,128)(2,1)S(1)} %get-tuple-element.115), channel_id=1, source_target_pairs={{0,2},{1,3},{2,0},{3,1},{4,6},{5,7},{6,4},{7,5},{8,10},{9,11},{10,... | collective-permute-start | bytes 1572872 | tf_op jit(solution)/shard_map/ppermute | solution.py:509
  182.6 41.2 %collective-permute-start.40 = (bf16[4,128,512]{2,1,0:T(8,128)(2,1)S(1)}, bf16[4,128,512]{2,1,0:T(8,128)(2,1)S(1)}, u32[]{:S(2)}, u32[]{:S(2)}) collective-permute-start(bf16[4,128,512]{2,1,0:T(8,128)(2,1)S(1)} %get-tuple-element.111), channel_id=1, source_target_pairs={{0,4},{1,5},{2,6},{3,7},{4,0},{5,1},{6,2},{7,3},{8,12},{9,13},{10,... | collective-permute-start | bytes 1572872 | tf_op jit(solution)/shard_map/ppermute | solution.py:509
  184.2 12.8 %collective-permute-start.11 = (bf16[2,48,512]{2,1,0:T(8,128)(2,1)S(1)}, bf16[2,48,512]{2,1,0:T(8,128)(2,1)S(1)}, u32[]{:S(2)}, u32[]{:S(2)}) collective-permute-start(bf16[2,48,512]{2,1,0:T(8,128)(2,1)S(1)} %get-tuple-element.133), channel_id=1, source_target_pairs={{0,4},{1,5},{2,6},{3,7},{4,0},{5,1},{6,2},{7,3},{8,12},{9,13},{10,... | collective-permute-start | bytes 294920 | tf_op jit(solution)/shard_map/ppermute | solution.py:509
  197.0 4.6 %collective-permute-start.16 = (bf16[2,48,512]{2,1,0:T(8,128)(2,1)S(1)}, bf16[2,48,512]{2,1,0:T(8,128)(2,1)S(1)}, u32[]{:S(2)}, u32[]{:S(2)}) collective-permute-start(bf16[2,48,512]{2,1,0:T(8,128)(2,1)S(1)} %get-tuple-element.135), channel_id=1, source_target_pairs={{0,2},{1,3},{2,0},{3,1},{4,6},{5,7},{6,4},{7,5},{8,10},{9,11},{10,... | collective-permute-start | bytes 294920 | tf_op jit(solution)/shard_map/ppermute | solution.py:509
  201.6 5.1 %collective-permute-start.12 = (bf16[1,48,512]{2,1,0:T(8,128)(2,1)S(1)}, bf16[1,48,512]{2,1,0:T(8,128)(2,1)S(1)}, u32[]{:S(2)}, u32[]{:S(2)}) collective-permute-start(bf16[1,48,512]{2,1,0:T(8,128)(2,1)S(1)} %add_convert_fusion.54), channel_id=1, source_target_pairs={{0,8},{1,9},{2,10},{3,11},{4,12},{5,13},{6,14},{7,15},{8,0},{9,1},... | collective-permute-start | bytes 147464 | tf_op jit(solution)/shard_map/ppermute | solution.py:509
  206.8 5.0 %collective-permute-start.17 = (bf16[1,48,512]{2,1,0:T(8,128)(2,1)S(1)}, bf16[1,48,512]{2,1,0:T(8,128)(2,1)S(1)}, u32[]{:S(2)}, u32[]{:S(2)}) collective-permute-start(bf16[1,48,512]{2,1,0:T(8,128)(2,1)S(1)} %add_convert_fusion.50), channel_id=1, source_target_pairs={{0,8},{1,9},{2,10},{3,11},{4,12},{5,13},{6,14},{7,15},{8,0},{9,1},... | collective-permute-start | bytes 147464 | tf_op jit(solution)/shard_map/ppermute | solution.py:509
  211.8 4.1 %collective-permute-start.13 = (bf16[1,48,512]{2,1,0:T(8,128)(2,1)S(1)}, bf16[1,48,512]{2,1,0:T(8,128)(2,1)S(1)}, u32[]{:S(2)}, u32[]{:S(2)}) collective-permute-start(bf16[1,48,512]{2,1,0:T(8,128)(2,1)S(1)} %add_convert_fusion.53), channel_id=1, source_target_pairs={{0,16},{16,0},{1,17},{17,1},{2,18},{18,2},{3,19},{19,3},{4,20},{20... | collective-permute-start | bytes 147464 | tf_op jit(solution)/shard_map/ppermute | solution.py:509
  215.8 4.1 %collective-permute-start.18 = (bf16[1,48,512]{2,1,0:T(8,128)(2,1)S(1)}, bf16[1,48,512]{2,1,0:T(8,128)(2,1)S(1)}, u32[]{:S(2)}, u32[]{:S(2)}) collective-permute-start(bf16[1,48,512]{2,1,0:T(8,128)(2,1)S(1)} %add_convert_fusion.49), channel_id=1, source_target_pairs={{0,16},{16,0},{1,17},{17,1},{2,18},{18,2},{3,19},{19,3},{4,20},{20... | collective-permute-start | bytes 147464 | tf_op jit(solution)/shard_map/ppermute | solution.py:509
  219.9 12.6 %collective-permute-start.20 = (bf16[4,128,512]{2,1,0:T(8,128)(2,1)S(1)}, bf16[4,128,512]{2,1,0:T(8,128)(2,1)S(1)}, u32[]{:S(2)}, u32[]{:S(2)}) collective-permute-start(bf16[4,128,512]{2,1,0:T(8,128)(2,1)S(1)} %get-tuple-element.117), channel_id=1, source_target_pairs={{0,2},{1,3},{2,0},{3,1},{4,6},{5,7},{6,4},{7,5},{8,10},{9,11},{10,... | collective-permute-start | bytes 1572872 | tf_op jit(solution)/shard_map/ppermute | solution.py:509
  221.4 15.6 %copy-start.8 = (bf16[8,128,512]{2,1,0:T(8,128)(2,1)S(1)}, bf16[8,128,512]{2,1,0:T(8,128)(2,1)}, u32[]{:S(2)}) copy-start(bf16[8,128,512]{2,1,0:T(8,128)(2,1)} %copy-done.7) | copy-start | bytes 3145732
  221.6 17.3 %collective-permute-start.36 = (bf16[2,128,512]{2,1,0:T(8,128)(2,1)S(1)}, bf16[2,128,512]{2,1,0:T(8,128)(2,1)S(1)}, u32[]{:S(2)}, u32[]{:S(2)}) collective-permute-start(bf16[2,128,512]{2,1,0:T(8,128)(2,1)S(1)} %get-tuple-element.125), channel_id=1, source_target_pairs={{0,4},{1,5},{2,6},{3,7},{4,0},{5,1},{6,2},{7,3},{8,12},{9,13},{10,... | collective-permute-start | bytes 786440 | tf_op jit(solution)/shard_map/ppermute | solution.py:509
  223.9 17.9 %collective-permute-start.41 = (bf16[2,128,512]{2,1,0:T(8,128)(2,1)S(1)}, bf16[2,128,512]{2,1,0:T(8,128)(2,1)S(1)}, u32[]{:S(2)}, u32[]{:S(2)}) collective-permute-start(bf16[2,128,512]{2,1,0:T(8,128)(2,1)S(1)} %get-tuple-element.121), channel_id=1, source_target_pairs={{0,2},{1,3},{2,0},{3,1},{4,6},{5,7},{6,4},{7,5},{8,10},{9,11},{10,... | collective-permute-start | bytes 786440 | tf_op jit(solution)/shard_map/ppermute | solution.py:509
  232.7 12.9 %collective-permute-start.21 = (bf16[2,128,512]{2,1,0:T(8,128)(2,1)S(1)}, bf16[2,128,512]{2,1,0:T(8,128)(2,1)S(1)}, u32[]{:S(2)}, u32[]{:S(2)}) collective-permute-start(bf16[2,128,512]{2,1,0:T(8,128)(2,1)S(1)} %get-tuple-element.127), channel_id=1, source_target_pairs={{0,4},{1,5},{2,6},{3,7},{4,0},{5,1},{6,2},{7,3},{8,12},{9,13},{10,... | collective-permute-start | bytes 786440 | tf_op jit(solution)/shard_map/ppermute | solution.py:509
  237.3 22.0 %collective-permute-start.30 = (bf16[4,128,512]{2,1,0:T(8,128)(2,1)S(1)}, bf16[4,128,512]{2,1,0:T(8,128)(2,1)S(1)}, u32[]{:S(2)}, u32[]{:S(2)}) collective-permute-start(bf16[4,128,512]{2,1,0:T(8,128)(2,1)S(1)} %get-tuple-element.113), channel_id=1, source_target_pairs={{0,2},{1,3},{2,0},{3,1},{4,6},{5,7},{6,4},{7,5},{8,10},{9,11},{10,... | collective-permute-start | bytes 1572872 | tf_op jit(solution)/shard_map/ppermute | solution.py:509
  238.9 13.8 %collective-permute-start.37 = (bf16[1,128,512]{2,1,0:T(8,128)(2,1)S(1)}, bf16[1,128,512]{2,1,0:T(8,128)(2,1)S(1)}, u32[]{:S(2)}, u32[]{:S(2)}) collective-permute-start(bf16[1,128,512]{2,1,0:T(8,128)(2,1)S(1)} %add_convert_fusion.34), channel_id=1, source_target_pairs={{0,8},{1,9},{2,10},{3,11},{4,12},{5,13},{6,14},{7,15},{8,0},{9,1},... | collective-permute-start | bytes 393224 | tf_op jit(solution)/shard_map/ppermute | solution.py:509
  241.9 13.1 %collective-permute-start.42 = (bf16[1,128,512]{2,1,0:T(8,128)(2,1)S(1)}, bf16[1,128,512]{2,1,0:T(8,128)(2,1)S(1)}, u32[]{:S(2)}, u32[]{:S(2)}) collective-permute-start(bf16[1,128,512]{2,1,0:T(8,128)(2,1)S(1)} %add_convert_fusion.30), channel_id=1, source_target_pairs={{0,8},{1,9},{2,10},{3,11},{4,12},{5,13},{6,14},{7,15},{8,0},{9,1},... | collective-permute-start | bytes 393224 | tf_op jit(solution)/shard_map/ppermute | solution.py:509
  245.6 7.7 %collective-permute-start.22 = (bf16[1,128,512]{2,1,0:T(8,128)(2,1)S(1)}, bf16[1,128,512]{2,1,0:T(8,128)(2,1)S(1)}, u32[]{:S(2)}, u32[]{:S(2)}) collective-permute-start(bf16[1,128,512]{2,1,0:T(8,128)(2,1)S(1)} %add_convert_fusion.42), channel_id=1, source_target_pairs={{0,8},{1,9},{2,10},{3,11},{4,12},{5,13},{6,14},{7,15},{8,0},{9,1},... | collective-permute-start | bytes 393224 | tf_op jit(solution)/shard_map/ppermute | solution.py:509
  250.2 26.8 %collective-permute-start.25 = (bf16[4,160,512]{2,1,0:T(8,128)(2,1)S(1)}, bf16[4,160,512]{2,1,0:T(8,128)(2,1)S(1)}, u32[]{:S(2)}, u32[]{:S(2)}) collective-permute-start(bf16[4,160,512]{2,1,0:T(8,128)(2,1)S(1)} %get-tuple-element.109), channel_id=1, source_target_pairs={{0,4},{1,5},{2,6},{3,7},{4,0},{5,1},{6,2},{7,3},{8,12},{9,13},{10,... | collective-permute-start | bytes 1966088 | tf_op jit(solution)/shard_map/ppermute | solution.py:509
  252.8 8.9 %collective-permute-start.38 = (bf16[1,128,512]{2,1,0:T(8,128)(2,1)S(1)}, bf16[1,128,512]{2,1,0:T(8,128)(2,1)S(1)}, u32[]{:S(2)}, u32[]{:S(2)}) collective-permute-start(bf16[1,128,512]{2,1,0:T(8,128)(2,1)S(1)} %add_convert_fusion.33), channel_id=1, source_target_pairs={{0,16},{16,0},{1,17},{17,1},{2,18},{18,2},{3,19},{19,3},{4,20},{20... | collective-permute-start | bytes 393224 | tf_op jit(solution)/shard_map/ppermute | solution.py:509
  253.4 5.8 %collective-permute-start.23 = (bf16[1,128,512]{2,1,0:T(8,128)(2,1)S(1)}, bf16[1,128,512]{2,1,0:T(8,128)(2,1)S(1)}, u32[]{:S(2)}, u32[]{:S(2)}) collective-permute-start(bf16[1,128,512]{2,1,0:T(8,128)(2,1)S(1)} %add_convert_fusion.41), channel_id=1, source_target_pairs={{0,16},{16,0},{1,17},{17,1},{2,18},{18,2},{3,19},{19,3},{4,20},{20... | collective-permute-start | bytes 393224 | tf_op jit(solution)/shard_map/ppermute | solution.py:509
  255.1 6.6 %collective-permute-start.43 = (bf16[1,128,512]{2,1,0:T(8,128)(2,1)S(1)}, bf16[1,128,512]{2,1,0:T(8,128)(2,1)S(1)}, u32[]{:S(2)}, u32[]{:S(2)}) collective-permute-start(bf16[1,128,512]{2,1,0:T(8,128)(2,1)S(1)} %add_convert_fusion.29), channel_id=1, source_target_pairs={{0,16},{16,0},{1,17},{17,1},{2,18},{18,2},{3,19},{19,3},{4,20},{20... | collective-permute-start | bytes 393224 | tf_op jit(solution)/shard_map/ppermute | solution.py:509
  259.4 6.4 %collective-permute-start.31 = (bf16[2,128,512]{2,1,0:T(8,128)(2,1)S(1)}, bf16[2,128,512]{2,1,0:T(8,128)(2,1)S(1)}, u32[]{:S(2)}, u32[]{:S(2)}) collective-permute-start(bf16[2,128,512]{2,1,0:T(8,128)(2,1)S(1)} %get-tuple-element.123), channel_id=1, source_target_pairs={{0,4},{1,5},{2,6},{3,7},{4,0},{5,1},{6,2},{7,3},{8,12},{9,13},{10,... | collective-permute-start | bytes 786440 | tf_op jit(solution)/shard_map/ppermute | solution.py:509
  265.9 10.4 %collective-permute-start.32 = (bf16[1,128,512]{2,1,0:T(8,128)(2,1)S(1)}, bf16[1,128,512]{2,1,0:T(8,128)(2,1)S(1)}, u32[]{:S(2)}, u32[]{:S(2)}) collective-permute-start(bf16[1,128,512]{2,1,0:T(8,128)(2,1)S(1)} %add_convert_fusion.38), channel_id=1, source_target_pairs={{0,8},{1,9},{2,10},{3,11},{4,12},{5,13},{6,14},{7,15},{8,0},{9,1},... | collective-permute-start | bytes 393224 | tf_op jit(solution)/shard_map/ppermute | solution.py:509
  276.4 5.9 %collective-permute-start.33 = (bf16[1,128,512]{2,1,0:T(8,128)(2,1)S(1)}, bf16[1,128,512]{2,1,0:T(8,128)(2,1)S(1)}, u32[]{:S(2)}, u32[]{:S(2)}) collective-permute-start(bf16[1,128,512]{2,1,0:T(8,128)(2,1)S(1)} %add_convert_fusion.37), channel_id=1, source_target_pairs={{0,16},{16,0},{1,17},{17,1},{2,18},{18,2},{3,19},{19,3},{4,20},{20... | collective-permute-start | bytes 393224 | tf_op jit(solution)/shard_map/ppermute | solution.py:509
  277.1 7.1 %collective-permute-start.26 = (bf16[2,160,512]{2,1,0:T(8,128)(2,1)S(1)}, bf16[2,160,512]{2,1,0:T(8,128)(2,1)S(1)}, u32[]{:S(2)}, u32[]{:S(2)}) collective-permute-start(bf16[2,160,512]{2,1,0:T(8,128)(2,1)S(1)} %get-tuple-element.119), channel_id=1, source_target_pairs={{0,2},{1,3},{2,0},{3,1},{4,6},{5,7},{6,4},{7,5},{8,10},{9,11},{10,... | collective-permute-start | bytes 983048 | tf_op jit(solution)/shard_map/ppermute | solution.py:509
  284.3 7.3 %collective-permute-start.27 = (bf16[1,160,512]{2,1,0:T(8,128)(2,1)S(1)}, bf16[1,160,512]{2,1,0:T(8,128)(2,1)S(1)}, u32[]{:S(2)}, u32[]{:S(2)}) collective-permute-start(bf16[1,160,512]{2,1,0:T(8,128)(2,1)S(1)} %add_convert_fusion.26), channel_id=1, source_target_pairs={{0,8},{1,9},{2,10},{3,11},{4,12},{5,13},{6,14},{7,15},{8,0},{9,1},... | collective-permute-start | bytes 491528 | tf_op jit(solution)/shard_map/ppermute | solution.py:509
  291.7 5.4 %collective-permute-start.28 = (bf16[1,160,512]{2,1,0:T(8,128)(2,1)S(1)}, bf16[1,160,512]{2,1,0:T(8,128)(2,1)S(1)}, u32[]{:S(2)}, u32[]{:S(2)}) collective-permute-start(bf16[1,160,512]{2,1,0:T(8,128)(2,1)S(1)} %add_convert_fusion.25), channel_id=1, source_target_pairs={{0,16},{16,0},{1,17},{17,1},{2,18},{18,2},{3,19},{19,3},{4,20},{20... | collective-permute-start | bytes 491528 | tf_op jit(solution)/shard_map/ppermute | solution.py:509
  (33 other events, 115.6 us)

commit v3 on v2

--- a/solution.py
+++ b/solution.py
@@ -263,7 +263,7 @@
 
 
 def time_backward_kernel(
-    after_ref, slots_ref, x_ref, qkv_ref, dxb_ref, gain_ref, shift_ref, wqkv_ref, wout_ref,
+    slots_ref, x_ref, qkv_ref, dxb_ref, gain_ref, shift_ref, wqkv_ref, wout_ref,
     own_ref, send_ref, ar_ref, dqkv_ref, small_ref,
     where_scr, both_scr,
 ):
@@ -339,7 +339,7 @@
 
 
 def space_mlp_back_kernel(
-    after_ref, own_ref, recv_ref, xa_ref, slope_ref, gain_ref, shift_ref, wup_ref, wdown_ref,
+    own_ref, recv_ref, xa_ref, slope_ref, gain_ref, shift_ref, wup_ref, wdown_ref,
     gr_ref, du_ref, dxa_ref, ar_ref, small_ref,
 ):
     part = lax.rem(lax.axis_index("sp"), 2)
@@ -361,7 +361,7 @@
 
 
 def space_attn_back_kernel(
-    after_ref, dxa_ref, qkv_ref, lse_ref, o_ref, wout_ref, dqkv_ref,
+    dxa_ref, qkv_ref, lse_ref, o_ref, wout_ref, dqkv_ref,
 ):
     do = dot_nt(dxa_ref[0].astype(BF16), wout_ref[0]).astype(BF16)
     both = do.astype(F32) * o_ref[0].astype(F32)
@@ -394,7 +394,7 @@
 
 
 def finish_kernel(
-    after_ref, tok_ref, dxa_ref, dqkv_ref, own_ref, recv_ref, gain_ref, shift_ref, wqkv_ref,
+    tok_ref, dxa_ref, dqkv_ref, own_ref, recv_ref, gain_ref, shift_ref, wqkv_ref,
     gtok_ref, out_ref, small_ref,
 ):
     part = lax.rem(lax.axis_index("sp"), 2)
@@ -501,25 +501,56 @@
     return jax.ShapeDtypeStruct(shape, dtype)
 
 
+def run(kernel, after, in_specs, args, aliases=None, **rest):
+    skip = len(after)
+    extra = skip if aliases is None else skip + len(aliases)
+
+    def body(*refs):
+        kernel(*refs[extra:])
+
+    alias_args = [] if aliases is None else aliases
+    marks = [pl.BlockSpec(memory_space=pl.ANY)] * extra
+    return pl.pallas_call(
+        body,
+        in_specs=marks + in_specs,
+        input_output_aliases={skip + i: i for i in range(len(alias_args))},
+        **rest,
+    )(*after, *alias_args, *args)
+
+
+class Chain:
+    def __init__(self, keep, send, order, sizes):
+        self.keep, self.send, self.sizes = keep, send, sizes
+        grp_size, sp_size = sizes
+        self.path = [("sp", sp_size, b) for b in order]
+        self.path += [("grp", grp_size, b) for b in range(grp_size.bit_length() - 1)]
+        self.swap()
+
+    def swap(self):
+        axis, size, bit = self.path.pop(0)
+        self.recv = swap(self.send, axis, size, bit)
+
+    def step(self):
+        if self.path and self.path[0][0] == "sp":
+            half = self.keep.shape[0] // 2
+            self.send = add_low(self.keep[half:], self.recv[half:])
+            self.keep = add_low(self.keep[:half], self.recv[:half])
+        else:
+            self.send = self.keep = add_low(self.keep, self.recv)
+        self.swap()
+
+    def finish(self):
+        while self.path:
+            self.step()
+        return self.keep[0].astype(F32) + self.recv[0].astype(F32)
+
+
 def add_low(a, b):
     return (a.astype(F32) + b.astype(F32)).astype(BF16)
 
 
 def swap(array, axis, size, bit):
     return lax.ppermute(array, axis, [(i, i ^ (1 << bit)) for i in range(size)])
-
-
-def sum_scatter(keep, send, order, sp_size, grp_size):
-    recv = swap(send, "sp", sp_size, order[0])
-    for b in order[1:]:
-        half = keep.shape[0] // 2
-        send = add_low(keep[half:], recv[half:])
-        keep = add_low(keep[:half], recv[:half])
-        recv = swap(send, "sp", sp_size, b)
-    now = add_low(keep, recv)
-    for b in range(grp_size.bit_length() - 1):
-        now = add_low(now, swap(now, "grp", grp_size, b))
-    return now[0].astype(F32)
 
 
 def shards(sizes, tokens, frame_slot, norm_gain, norm_shift, w_qkv, w_out, w_up, b_up, w_down, b_down, cotangent):
@@ -560,7 +591,7 @@
             frame_out(hidden, BF16),
         ],
         scratch_shapes=[pltpu.VMEM((patches, width), F32)],
-        compiler_params=params(56),
+        compiler_params=params(60),
         cost_estimate=cost(2 * macs * (4 * width + 2 * hidden), 30e6),
     )(tokens, norm_gain, norm_shift, w_qkv, w_out, w_up, b_up, w_down, b_down)
     x_recv = core_swap(x_send)
@@ -598,7 +629,7 @@
             sds((rows, width), F32), small_shape,
         ],
         scratch_shapes=place_scratch + [pltpu.VMEM((step_rows, hidden), BF16)],
-        compiler_params=params(56),
+        compiler_params=params(60),
         cost_estimate=cost(2 * macs * (4 * width + 4 * hidden), 30e6),
     )(
         frame_slot, x_keep, x_recv, cotangent, cot_recv, norm_gain, norm_shift, w_qkv, w_out, w_up,
@@ -616,65 +647,75 @@
             shapes += [sds((slots, height, TILE), BF16)] * 2
         return [pl.BlockSpec(s.shape, lambda i: (0, 0, 0)) for s in shapes], shapes
 
+    order_a = list(range(sp_bits))
+    order_b = [0, 2, 1] + list(range(3, sp_bits))
+    chain = functools.partial(Chain, sizes=sizes)
+    flat = lambda a: a.reshape(rows, a.shape[-1])
+
+    def meet(chains, *arrays):
+        out = lax.optimization_barrier(tuple(arrays) + tuple(c.recv for c in chains))
+        for c, recv in zip(chains, out[len(arrays) :]):
+            c.recv = recv
+            c.step()
+        return out[: len(arrays)]
+
     def mlp_weights(h, du, act, gr, *extra):
         specs, shapes = buffer_specs(4 * size, down_size + (size if extra else 0))
-        return pl.pallas_call(
+        tall = pl.BlockSpec((rows, TILE), lambda i: (0, i))
+        out = pl.pallas_call(
             functools.partial(mlp_weights_kernel, (order_a, order_b)),
+            in_specs=[whole_spec(h), tall, tall, whole_spec(gr)] + [whole_spec(e) for e in extra],
             grid=(hidden // TILE,),
-            in_specs=[
-                whole_spec(h), pl.BlockSpec((rows, TILE), lambda i: (0, i)),
-                pl.BlockSpec((rows, TILE), lambda i: (0, i)), whole_spec(gr),
-            ] + [whole_spec(e) for e in extra],
             out_specs=specs,
             out_shape=shapes,
-            compiler_params=params(40),
+            compiler_params=params(60),
             cost_estimate=cost(2 * macs * 2 * hidden, 14e6),
         )(h, du, act, gr, *extra)
-
-    order_a = list(range(sp_bits))
-    order_b = [0, 2, 1] + list(range(3, sp_bits))
-    any_spec = pl.BlockSpec(memory_space=pl.ANY)
-    collect = functools.partial(sum_scatter, sp_size=sp_size, grp_size=grp_size)
-
-    up1_keep, up1_send, down1_keep, down1_send = mlp_weights(h3, du1, act1, gr1)
-    up1 = collect(up1_keep, up1_send, order_a)
-    down1 = collect(down1_keep, down1_send, order_b)
+        return out
+
+    out = mlp_weights(h3, du1, act1, gr1)
+    out = lax.optimization_barrier(tuple(out) + (dxb,))
+    up1, down1 = chain(out[0], out[1], order_a), chain(out[2], out[3], order_b)
+    dxb = out[4]
 
     (dx_own, dx_send, ar1, dqkv1, small2) = pl.pallas_call(
         time_backward_kernel,
+        in_specs=[
+            smem, row_block(width), row_block(3 * width), row_block(width),
+            whole_spec(norm_gain), whole_spec(norm_shift), layer_spec(w_qkv, 1), layer_spec(w_out, 1),
+        ],
         grid=(steps,),
-        in_specs=[
-            any_spec, smem, row_block(width), row_block(3 * width), row_block(width),
-            whole_spec(norm_gain), whole_spec(norm_shift), layer_spec(w_qkv, 1), layer_spec(w_out, 1),
-        ],
         out_specs=[place_block, place_block, row_block(width), row_block(3 * width), small_spec],
         out_shape=[
             half_shape, half_shape, sds((rows, width), BF16), sds((rows, 3 * width), BF16), small_shape,
         ],
         scratch_shapes=place_scratch,
-        compiler_params=params(56),
+        compiler_params=params(60),
         cost_estimate=cost(2 * macs * 4 * width, 15e6),
-    )(up1_keep, frame_slot, xt, qkv1, dxb, norm_gain, norm_shift, w_qkv, w_out)
+    )(frame_slot, xt, qkv1, dxb, norm_gain, norm_shift, w_qkv, w_out)
+    dx_own, dx_send, dqkv1 = meet((up1, down1), dx_own, dx_send, dqkv1)
     dx_recv = core_swap(dx_send)
+
     specs, shapes = buffer_specs(4 * size)
-    attn1_keep, attn1_send = pl.pallas_call(
+    attn1 = pl.pallas_call(
         functools.partial(attn_weights_kernel, order_a),
+        in_specs=[whole_spec(h2), whole_spec(dqkv1), whole_spec(o1), whole_spec(ar1)],
         grid=(1,),
-        in_specs=[whole_spec(h2), whole_spec(dqkv1), whole_spec(o1), whole_spec(ar1)],
         out_specs=specs,
         out_shape=shapes,
-        compiler_params=params(40),
+        compiler_params=params(60),
         cost_estimate=cost(2 * macs * 4 * width, 8e6),
     )(h2, dqkv1, o1, ar1)
-    attn1 = collect(attn1_keep, attn1_send, order_a)
+    keep, send, dx_recv = lax.optimization_barrier((*attn1, dx_recv))
+    attn1 = chain(keep, send, order_a)
 
     (gr0, du0, dxa, ar0, small1) = pl.pallas_call(
         space_mlp_back_kernel,
+        in_specs=[
+            half_block, half_block, frame_block(width), frame_block(hidden),
+            whole_spec(norm_gain), whole_spec(norm_shift), layer_spec(w_up, 0), layer_spec(w_down, 0),
+        ],
         grid=(frames,),
-        in_specs=[
-            any_spec, half_block, half_block, frame_block(width), frame_block(hidden),
-            whole_spec(norm_gain), whole_spec(norm_shift), layer_spec(w_up, 0), layer_spec(w_down, 0),
-        ],
         out_specs=[
             frame_block(width), frame_block(hidden), frame_block(width), frame_block(width), small_spec,
         ],
@@ -682,54 +723,69 @@
             frame_out(width, BF16), frame_out(hidden, BF16), frame_out(width, F32),
             frame_out(width, BF16), small_shape,
         ],
-        compiler_params=params(56),
+        compiler_params=params(60),
         cost_estimate=cost(2 * macs * 2 * hidden, 20e6),
-    )(attn1_keep, dx_own, dx_recv, xa, slope0, norm_gain, norm_shift, w_up, w_down)
-    flat = lambda a: a.reshape(rows, a.shape[-1])
-    up0_keep, up0_send, down0_keep, down0_send = mlp_weights(
-        flat(h1), flat(du0), flat(act0), flat(gr0), flat(o0), flat(ar0)
-    )
-    up0 = collect(up0_keep, up0_send, order_a)
-    down0 = collect(down0_keep, down0_send, order_b)
-
-    dqkv0 = pl.pallas_call(
-        space_attn_back_kernel,
-        grid=(frames,),
-        in_specs=[
-            any_spec, frame_block(width), frame_block(3 * width), step_spec((1, HEADS, patches)),
-            frame_block(width), layer_spec(w_out, 0),
-        ],
-        out_specs=frame_block(3 * width),
-        out_shape=frame_out(3 * width, BF16),
-        compiler_params=params(56),
-        cost_estimate=cost(2 * macs * 6 * width, 20e6),
-    )(up0_keep, dxa, qkv0, lse0, o0, w_out)
-
+    )(dx_own, dx_recv, xa, slope0, norm_gain, norm_shift, w_up, w_down)
+    gr0, du0, ar0 = meet((attn1, up1, down1), gr0, du0, ar0)
+    out = mlp_weights(flat(h1), flat(du0), flat(act0), flat(gr0), flat(o0), flat(ar0))
+    out = meet((), *out, dxa)
+    dxa = out[4]
+    up0, down0 = chain(out[0], out[1], order_a), chain(out[2], out[3], order_b)
+
+    def attn_back(grad, first, count, before):
+        offset_spec = lambda shape: pl.BlockSpec(shape, lambda i: (i + first,) + (0,) * (len(shape) - 1))
+        return run(
+            space_attn_back_kernel,
+            [],
+            [
+                offset_spec((1, patches, width)), offset_spec((1, patches, 3 * width)),
+                offset_spec((1, HEADS, patches)), offset_spec((1, patches, width)), layer_spec(w_out, 0),
+            ],
+            (grad, qkv0, lse0, o0, w_out),
+            aliases=before,
+            grid=(count,),
+            out_specs=[offset_spec((1, patches, 3 * width))],
+            out_shape=[frame_out(3 * width, BF16)],
+            compiler_params=params(60),
+            cost_estimate=cost(macs * 6 * width, 20e6),
+        )
+
+    (dqkv0,) = attn_back(dxa, 0, frames // 2, None)
+    (dqkv0,) = meet((up0, down0, up1, down1, attn1), dqkv0)
+    (dqkv0,) = attn_back(dxa, frames // 2, frames // 2, [dqkv0])
+    (dqkv0,) = meet((up1, down1), dqkv0)
     specs, shapes = buffer_specs(size + size // 2, size + size // 2)
-    qkva_keep, qkva_send, qkvb_keep, qkvb_send = pl.pallas_call(
+    out = pl.pallas_call(
         functools.partial(qkv_weights_kernel, (order_a, order_b)),
+        in_specs=[whole_spec(flat(h0)), whole_spec(flat(dqkv0))],
         grid=(1,),
-        in_specs=[whole_spec(flat(h0)), whole_spec(flat(dqkv0))],
         out_specs=specs,
         out_shape=shapes,
-        compiler_params=params(40),
+        compiler_params=params(60),
         cost_estimate=cost(2 * macs * 3 * width, 8e6),
     )(flat(h0), flat(dqkv0))
-    qkva = collect(qkva_keep, qkva_send, order_a)
-    qkvb = collect(qkvb_keep, qkvb_send, order_b)
+    out = meet((attn1,), *out, dqkv0)
+    qkva = chain(out[0], out[1], order_a)
+    qkvb = chain(out[2], out[3], order_b)
 
     grad_tokens, output, small0 = pl.pallas_call(
         finish_kernel,
+        in_specs=[
+            frame_block(width), frame_block(width), frame_block(3 * width), half_block,
+            half_block, whole_spec(norm_gain), whole_spec(norm_shift), layer_spec(w_qkv, 0),
+        ],
         grid=(frames,),
-        in_specs=[
-            any_spec, frame_block(width), frame_block(width), frame_block(3 * width), half_block,
-            half_block, whole_spec(norm_gain), whole_spec(norm_shift), layer_spec(w_qkv, 0),
-        ],
         out_specs=[frame_block(width), frame_block(width), small_spec],
         out_shape=[frame_out(width, BF16), frame_out(width, BF16), small_shape],
-        compiler_params=params(56),
+        compiler_params=params(60),
         cost_estimate=cost(2 * macs * 3 * width, 8e6),
-    )(qkva_keep, tokens, dxa, dqkv0, out_own, out_recv, norm_gain, norm_shift, w_qkv)
+    )(tokens, dxa, out[4], out_own, out_recv, norm_gain, norm_shift, w_qkv)
+    (small0,) = meet((qkva, qkvb, up0, down0, attn1), small0)
+    meet((qkva, qkvb, up0, down0))
+    meet((qkva, qkvb, up0, down0))
+    up1, down1, attn1, up0, down0, qkva, qkvb = [
+        c.finish() for c in (up1, down1, attn1, up0, down0, qkva, qkvb)
+    ]
 
     small = jnp.concatenate([small0, small1, small2, small3], axis=0).astype(BF16)
     for b in range(sp_bits):

time: 299 us -> 243 us (0.81)
  waiting for transfers between devices: 84.9 us -> 31.7 us
  local copies, waits for them, and re-layouts: 29.5 us -> 4.11 us
  other arithmetic: 9.61 us -> 27.4 us
  Pallas kernels: 116 us -> 133 us
  starting transfers between devices: 57 us -> 44.1 us
    ppermute x44, waiting for transfers between devices: 84.9 us -> 31.7 us  [swap(): return lax.ppermute(array, axis, [(i, i ^ 1 << bit) for i in range(size)])]
    unnamed x76 -> x44, local copies, waits for them, and re-layouts: 27.5 us -> 2.12 us
    convert_element_type x32, other arithmetic: 3.93 us -> 23.3 us  [add_low(): return (a.astype(F32) + b.astype(F32)).astype(BF16)]
    ppermute x44, starting transfers between devices: 57 us -> 44.1 us  [swap(): return lax.ppermute(array, axis, [(i, i ^ 1 << bit) for i in range(size)])]
    pallas_call x2, Pallas kernels: 14.1 us -> 21 us  [mlp_weights(): pl.pallas_call(functools.partial(mlp_weights_kernel, (order_a, order_b)),...]
    pallas_call x5 -> x6, Pallas kernels: 49.2 us -> 55.9 us  [the longest x2 20.2 us: run(): pl.pallas_call(body, in_specs=marks + in_specs, input_output_aliases={ski...]
    pallas_call x1, Pallas kernels: 1.82 us -> 5.16 us  [shards(): pl.pallas_call(functools.partial(qkv_weights_kernel, (order_a, order_b)),...]
  transfers between devices with their start and end apart: 44 -> 44, of which waited for: 23 -> 15; matrix products, arithmetic and copies ran while one was open for 3% -> 11% of each run, Pallas kernels for 21% -> 35%
where the time goes in v3:
time: 243 us; the launch traced here: 242 us
  Pallas kernels  133 us (55%)
  starting transfers between devices  44.1 us (18%)
  waiting for transfers between devices  31.7 us (13%)
  other arithmetic  27.4 us (11%)
  local copies, waits for them, and re-layouts  4.11 us (2%)
    ppermute x44, starting transfers between devices, swap(): return lax.ppermute(array, axis, [(i, i ^ 1 << bit) for i in range(size)])  44.1 us
    ppermute x44, waiting for transfers between devices, swap(): return lax.ppermute(array, axis, [(i, i ^ 1 << bit) for i in range(size)])  31.7 us
    pallas_call x1, Pallas kernels, shards(): pl.pallas_call(time_forward_kernel, grid=(steps,), in_specs=[smem, place_...  28.7 us
    convert_element_type x32, other arithmetic, add_low(): return (a.astype(F32) + b.astype(F32)).astype(BF16)  23.3 us
    pallas_call x1, Pallas kernels, shards(): pl.pallas_call(space_forward_kernel, grid=(frames,), in_specs=[frame_bloc...  22.6 us
    pallas_call x2, Pallas kernels, mlp_weights(): pl.pallas_call(functools.partial(mlp_weights_kernel, (order_a, order_b)),...  21 us
    pallas_call x2, Pallas kernels, run(): pl.pallas_call(body, in_specs=marks + in_specs, input_output_aliases={ski...  20.2 us
    pallas_call x1, Pallas kernels, shards(): pl.pallas_call(space_mlp_back_kernel, in_specs=[half_block, half_block, f...  11.3 us
  transfers between devices with their start and end apart: 44, of which 15 were waited for; matrix products, arithmetic and copies ran while one was open for 11% of the time, Pallas kernels for 35%

profile of v3, /device:TPU:0, one launch (start us, length us, event | category | flops | bytes accessed | tf_op | source)
XLA Modules:
  0.0 241.9 jit_solution(12621269462525196907)
XLA Ops:
  1.2 22.6 %shard_map.186 = (bf16[4,128,512]{2,1,0:T(8,128)(2,1)}, bf16[4,128,512]{2,1,0:T(8,128)(2,1)}, bf16[4,256,512]{2,1,0:T(8,128)(2,1)}, bf16[4,256,1536]{2,1,0:T(8,1...) custom-call(bf16[4,256,512]{2,1,0:T(8,128)(2,1)} %tok_ref.3, ...), custom_call_target="tpu_custom_call" | custom-call | flops 6442450944 | bytes 30000000 | tf_op jit(solution)/shard_map/pallas_call | solution.py:574
  23.9 2.1 collective-permute-done.recv_ref
  27.2 28.7 %shard_map.187 = (bf16[4,128,512]{2,1,0:T(8,128)(2,1)}, bf16[4,128,512]{2,1,0:T(8,128)(2,1)}, bf16[1024,512]{1,0:T(8,128)(2,1)}, bf16[1024,512]{1,0:T(8,128)(2,1...) custom-call(s32[8,8]{1,0:T(8,128)} %slots_ref.3, ...), custom_call_target="tpu_custom_call" | custom-call | flops 10737418240 | bytes 30000000 | tf_op jit(solution)/shard_map/pallas_call | solution.py:612
  55.9 9.2 %shard_map.188 = (bf16[8,128,512]{2,1,0:T(8,128)(2,1)}, bf16[8,128,512]{2,1,0:T(8,128)(2,1)}, bf16[8,128,512]{2,1,0:T(8,128)(2,1)}, bf16[8,128,512]{2,1,0:T(8,128)(2,1)}) custom-call(bf16[1024,512]{1,0:T(8,128)(2,1)} %get-tuple-element.117.refs_0_, bf16[1024,2048]{1,0:T(8,128)(2,1)} %get-tuple-element.118.refs_1_, ...), custom_call_target="tpu_custom_call" | custom-call | flops 4294967296 | bytes 14000000 | tf_op jit(solution)/shard_map/pallas_call | solution.py:665
  65.6 10.9 %shard_map.189 = (bf16[4,128,512]{2,1,0:T(8,128)(2,1)}, bf16[4,128,512]{2,1,0:T(8,128)(2,1)}, bf16[1024,512]{1,0:T(8,128)(2,1)}, bf16[1024,1536]{1,0:T(8,128)(2,1)}, f32[8,512]{1,0:T(8,128)}) custom-call(s32[8,8]{1,0:T(8,128)} %slots_ref.3, bf16[1024,512]{1,0:T(8,128)(2,1)} %get-tuple-element.115.x_ref, bf16[1024,1536]{1,0:T(8,128)(2,1)} %get-tuple-element.116.qkv_ref, ...), custom_call_target="tpu_custom_call" | custom-call | flops 2147483648 | bytes 15000000 | tf_op jit(solution)/shard_map/pallas_call | solution.py:681
  77.6 6.5 %shard_map.190 = (bf16[8,128,512]{2,1,0:T(8,128)(2,1)}, bf16[8,128,512]{2,1,0:T(8,128)(2,1)}) custom-call(bf16[1024,512]{1,0:T(8,128)(2,1)} %get-tuple-element.133.h_ref, bf16[1024,1536]{1,0:T(8,128)(2,1)} %get-tuple-element.134.dqkv_ref, bf16[1024,512]{1,0:T(8,128)(2,1)} %get-tuple-element.135.o_ref, bf16[1024,512]{1,0:T(8,128)(2,1)} %get-tuple-element.136.ar_ref), custom_call_target="tpu_custom_call" | custom-call | flops 2147483648 | bytes 8000000 | tf_op jit(solution)/shard_map/pallas_call | solution.py:700
  84.2 2.9 %add_convert_fusion.6 = (bf16[4,128,512]{2,1,0:T(8,128)(2,1)S(1)}, bf16[4,128,512]{2,1,0:T(8,128)(2,1)}) fusion(bf16[8,128,512]{2,1,0:T(8,128)(2,1)} %copy-done.6, bf16[8,128,512]{2,1,0:T(8,128)(2,1)} %get-tuple-element.149), kind=kLoop, calls=%fused_computation.6 | loop fusion | flops 2097152 | bytes 3145728 | tf_op jit(solution)/shard_map/convert_element_type | solution.py:549
  87.2 3.0 %collective-permute-start.7 = (bf16[4,128,512]{2,1,0:T(8,128)(2,1)}, bf16[4,128,512]{2,1,0:T(8,128)(2,1)S(1)}, u32[]{:S(2)}, u32[]{:S(2)}) collective-permute-start(bf16[4,128,512]{2,1,0:T(8,128)(2,1)} %get-tuple-element.221), channel_id=1, source_target_pairs={{0,4},{1,5},{2,6},{3,7},{4,0},{5,1},{6,2},{7,3},{8,12},{9,13},{10,... | collective-permute-start | bytes 1572872 | tf_op jit(solution)/shard_map/ppermute | solution.py:553
  90.2 1.1 add_convert_fusion.7
  91.3 1.5 collective-permute-start.6
  92.8 11.3 %shard_map.191 = (bf16[4,256,512]{2,1,0:T(8,128)(2,1)}, bf16[4,256,2048]{2,1,0:T(8,128)(2,1)}, f32[4,256,512]{2,1,0:T(8,128)}, bf16[4,256,512]{2,1,0:T(8,128)(2,1)}, f32[8,512]{1,0:T(8,128)}) custom-call(bf16[4,128,512]{2,1,0:T(8,128)(2,1)} %get-tuple-element.132.own_ref, bf16[4,128,512]{2,1,0:T(8,128)(2,1)} %copy-done.19, ...), custom_call_target="tpu_custom_call" | custom-call | flops 4294967296 | bytes 20000000 | tf_op jit(solution)/shard_map/pallas_call | solution.py:712
  105.1 11.8 %shard_map.192 = (bf16[8,128,512]{2,1,0:T(8,128)(2,1)}, bf16[8,128,512]{2,1,0:T(8,128)(2,1)}, bf16[8,160,512]{2,1,0:T(8,128)(2,1)}, bf16[8,160,512]{2,1,0:T(8,128)(2,1)}) custom-call(bf16[1024,512]{1,0:T(8,128)(2,1)} %bitcast.72, bf16[1024,2048]{1,0:T(8,128)(2,1)} %bitcast.70, bf16[1024,2048]{1,0:T(8,128)(2,1)} %bitcast.69, bf16[1024,512]{1,0:T(8,128)(2,1)} %bitcast.73, ...), custom_call_target="tpu_custom_call" | custom-call | flops 4294967296 | bytes 14000000 | tf_op jit(solution)/shard_map/pallas_call | solution.py:665
  117.6 2.6 %add_convert_fusion.4 = (bf16[4,128,512]{2,1,0:T(8,128)(2,1)S(1)}, bf16[4,128,512]{2,1,0:T(8,128)(2,1)}) fusion(bf16[8,128,512]{2,1,0:T(8,128)(2,1)} %copy-done.2, bf16[8,128,512]{2,1,0:T(8,128)(2,1)} %get-tuple-element.169), kind=kLoop, calls=%fused_computation.4 | loop fusion | flops 2097152 | bytes 3145728 | tf_op jit(solution)/shard_map/convert_element_type | solution.py:549
  120.2 1.6 collective-permute-start.12
  124.5 10.0 %shard_map.193.refs_0_ = bf16[4,256,1536]{2,1,0:T(8,128)(2,1)} custom-call(f32[4,256,512]{2,1,0:T(8,128)} %get-tuple-element.161.refs_0_.refs_1_.dxa_ref, bf16[4,256,1536]{2,1,0:T(8,128)(2,1)} %get-tuple-element.163.refs_1_.refs_2_, f32[4,8,256]{2,1,0:T(8,128)} %get-tuple-element.164.refs_2_.refs_3_, ...), custom_call_target="tpu_custom_call" | custom-call | flops 1610612736 | bytes 20000000 | tf_op jit(solution)/shard_map/pallas_call | solution.py:513
  134.5 5.6 %collective-permute-done.11 = bf16[2,128,512]{2,1,0:T(8,128)(2,1)} collective-permute-done((bf16[2,128,512]{2,1,0:T(8,128)(2,1)}, bf16[2,128,512]{2,1,0:T(8,128)(2,1)}, u32[]{:S(2)}, u32[]{:S(2)}) %collective-permute-start.11) | collective-permute-done | bytes 262176 | tf_op jit(solution)/shard_map/ppermute | solution.py:553
  140.2 1.6 add_convert_fusion.37
  141.7 2.6 %collective-permute-start.14 = (bf16[1,128,512]{2,1,0:T(8,128)(2,1)}, bf16[1,128,512]{2,1,0:T(8,128)(2,1)}, u32[]{:S(2)}, u32[]{:S(2)}) collective-permute-start(bf16[1,128,512]{2,1,0:T(8,128)(2,1)} %add_convert_fusion.37), channel_id=1, source_target_pairs={{0,8},{1,9},{2,10},{3,11},{4,12},{5,13},{6,14},{7,15},{8,0},{9,1},... | collective-permute-start | bytes 393224 | tf_op jit(solution)/shard_map/ppermute | solution.py:553
  144.4 1.6 add_convert_fusion.38
  146.3 2.0 add_convert_fusion.14
  148.6 1.1 add_convert_fusion.2
  149.7 1.7 collective-permute-start.19
  151.7 10.2 %shard_map.194.dqkv_ref = bf16[4,256,1536]{2,1,0:T(8,128)(2,1)} custom-call(bf16[4,256,1536]{2,1,0:T(8,128)(2,1)} %shard_map.193.refs_0_, f32[4,256,512]{2,1,0:T(8,128)} %get-tuple-element.161.refs_0_.refs_1_.dxa_ref, bf16[4,256,1536]{2,1,0:T(8,128)(2,1)} %get-tuple-element.163.refs_1_.refs_2_, ...), custom_call_target="tpu_custom_call", output_to_operand_aliasing={{}: (0, {})} | custom-call | flops 1610612736 | bytes 20000000 | tf_op jit(solution)/shard_map/pallas_call | solution.py:513
  161.9 1.6 collective-permute-start.20
  165.6 1.6 collective-permute-start.42
  167.1 5.2 %shard_map.195 = (bf16[8,48,512]{2,1,0:T(8,128)(2,1)}, bf16[8,48,512]{2,1,0:T(8,128)(2,1)}, bf16[8,48,512]{2,1,0:T(8,128)(2,1)}, bf16[8,48,512]{2,1,0:T(8,128)(2,1)}) custom-call(bf16[1024,512]{1,0:T(8,128)(2,1)} %bitcast.71, bf16[1024,1536]{1,0:T(8,128)(2,1)} %bitcast.63), custom_call_target="tpu_custom_call" | custom-call | flops 1610612736 | bytes 8000000 | tf_op jit(solution)/shard_map/pallas_call | solution.py:758
  173.9 3.3 %collective-permute-done.43 = bf16[1,128,512]{2,1,0:T(8,128)(2,1)S(1)} collective-permute-done((bf16[1,128,512]{2,1,0:T(8,128)(2,1)S(1)}, bf16[1,128,512]{2,1,0:T(8,128)(2,1)S(1)}, u32[]{:S(2)}, u32[]{:S(2)}) %collective-permute-start.43) | collective-permute-done | bytes 131104 | tf_op jit(solution)/shard_map/ppermute | solution.py:553
  177.3 2.7 %collective-permute-start.21 = (bf16[1,128,512]{2,1,0:T(8,128)(2,1)S(1)}, bf16[1,128,512]{2,1,0:T(8,128)(2,1)S(1)}, u32[]{:S(2)}, u32[]{:S(2)}) collective-permute-start(bf16[1,128,512]{2,1,0:T(8,128)(2,1)S(1)} %add_convert_fusion.36), channel_id=1, source_target_pairs={{0,8},{1,9},{2,10},{3,11},{4,12},{5,13},{6,14},{7,15},{8,0},{9,1},... | collective-permute-start | bytes 393224 | tf_op jit(solution)/shard_map/ppermute | solution.py:553
  180.0 7.0 %shard_map.196 = (bf16[4,256,512]{2,1,0:T(8,128)(2,1)}, bf16[4,256,512]{2,1,0:T(8,128)(2,1)}, f32[8,512]{1,0:T(8,128)}) custom-call(bf16[4,256,512]{2,1,0:T(8,128)(2,1)} %tok_ref.3, f32[4,256,512]{2,1,0:T(8,128)} %get-tuple-element.161.refs_0_.refs_1_.dxa_ref, bf16[4,256,1536]{2,1,0:T(8,128)(2,1)} %shard_map.194.dqkv_ref, ...), custom_call_target="tpu_custom_call" | custom-call | flops 1610612736 | bytes 8000000 | tf_op jit(solution)/shard_map/pallas_call | solution.py:771
  189.6 1.3 add_convert_fusion.21
  192.1 1.1 add_convert_fusion.23
  193.2 1.6 collective-permute-start.27
  195.6 1.7 collective-permute-start.24
  197.3 1.2 add_convert_fusion.12
  199.6 2.5 %collective-permute-start.25 = (bf16[32,512]{1,0:T(8,128)(2,1)S(1)}, bf16[32,512]{1,0:T(8,128)(2,1)S(1)}, u32[]{:S(2)}, u32[]{:S(2)}) collective-permute-start(bf16[32,512]{1,0:T(8,128)(2,1)S(1)} %add_convert_fusion.51), channel_id=1, source_target_pairs={{0,8},{1,9},{2,10},{3,11},{4,12},{5,13},{6,14},{7,15},{8,0},{9,1},... | collective-permute-start | bytes 98312 | tf_op jit(solution)/shard_map/ppermute | solution.py:553
  202.3 2.3 collective-permute-done.25
  205.0 1.6 collective-permute-start.26
  206.7 2.3 collective-permute-done.26
  210.4 2.2 collective-permute-done.30
  212.9 3.2 %collective-permute-start.33 = (bf16[1,128,512]{2,1,0:T(8,128)(2,1)S(1)}, bf16[1,128,512]{2,1,0:T(8,128)(2,1)S(1)}, u32[]{:S(2)}, u32[]{:S(2)}) collective-permute-start(bf16[1,128,512]{2,1,0:T(8,128)(2,1)S(1)} %add_convert_fusion.35), channel_id=1, source_target_pairs={{0,8},{1,9},{2,10},{3,11},{4,12},{5,13},{6,14},{7,15},{8,0},{9,1},... | collective-permute-start | bytes 393224 | tf_op jit(solution)/shard_map/ppermute | solution.py:553
  216.2 2.9 %collective-permute-start.31 = (bf16[2,48,512]{2,1,0:T(8,128)(2,1)S(1)}, bf16[2,48,512]{2,1,0:T(8,128)(2,1)S(1)}, u32[]{:S(2)}, u32[]{:S(2)}) collective-permute-start(bf16[2,48,512]{2,1,0:T(8,128)(2,1)S(1)} %get-tuple-element.239), channel_id=1, source_target_pairs={{0,4},{1,5},{2,6},{3,7},{4,0},{5,1},{6,2},{7,3},{8,12},{9,13},{10,... | collective-permute-start | bytes 294920 | tf_op jit(solution)/shard_map/ppermute | solution.py:553
  219.7 2.0 collective-permute-done.31
  221.7 3.3 %collective-permute-done.33 = bf16[1,128,512]{2,1,0:T(8,128)(2,1)S(1)} collective-permute-done((bf16[1,128,512]{2,1,0:T(8,128)(2,1)S(1)}, bf16[1,128,512]{2,1,0:T(8,128)(2,1)S(1)}, u32[]{:S(2)}, u32[]{:S(2)}) %collective-permute-start.33) | collective-permute-done | bytes 131104 | tf_op jit(solution)/shard_map/ppermute | solution.py:553
  224.9 1.8 collective-permute-done.34
  227.0 3.0 %collective-permute-start.35 = (bf16[1,48,512]{2,1,0:T(8,128)(2,1)S(1)}, bf16[1,48,512]{2,1,0:T(8,128)(2,1)S(1)}, u32[]{:S(2)}, u32[]{:S(2)}) collective-permute-start(bf16[1,48,512]{2,1,0:T(8,128)(2,1)S(1)} %add_convert_fusion.47), channel_id=1, source_target_pairs={{0,8},{1,9},{2,10},{3,11},{4,12},{5,13},{6,14},{7,15},{8,0},{9,1},... | collective-permute-start | bytes 147464 | tf_op jit(solution)/shard_map/ppermute | solution.py:553
  229.9 1.7 collective-permute-start.41
  232.5 1.8 collective-permute-start.38
  234.8 3.2 %collective-permute-done.38 = bf16[1,48,512]{2,1,0:T(8,128)(2,1)S(1)} collective-permute-done((bf16[1,48,512]{2,1,0:T(8,128)(2,1)S(1)}, bf16[1,48,512]{2,1,0:T(8,128)(2,1)S(1)}, u32[]{:S(2)}, u32[]{:S(2)}) %collective-permute-start.38) | collective-permute-done | bytes 49184 | tf_op jit(solution)/shard_map/ppermute | solution.py:553
  (161 shorter events, 26.4 us)
Async XLA Ops:
  0.6 25.4 %collective-permute-start.1 = (bf16[4,256,512]{2,1,0:T(8,128)(2,1)}, bf16[4,256,512]{2,1,0:T(8,128)(2,1)S(1)}, u32[]{:S(2)}, u32[]{:S(2)}) collective-permute-start(bf16[4,256,512]{2,1,0:T(8,128)(2,1)} %cot_ref.1), channel_id=1, source_target_pairs={{0,1},{1,0},{2,3},{3,2},{4,5},{5,4},{6,7},{7,6},{8,9},{9,8},{10,11... | collective-permute-start | bytes 3145736 | tf_op jit(solution)/shard_map/ppermute | solution.py:553
  23.8 2.2 collective-permute-start
  65.1 11.5 %collective-permute-start.2 = (bf16[8,128,512]{2,1,0:T(8,128)(2,1)}, bf16[8,128,512]{2,1,0:T(8,128)(2,1)S(1)}, u32[]{:S(2)}, u32[]{:S(2)}) collective-permute-start(bf16[8,128,512]{2,1,0:T(8,128)(2,1)} %get-tuple-element.130), channel_id=1, source_target_pairs={{0,1},{1,0},{2,3},{3,2},{4,5},{5,4},{6,7},{7,6},{8,9},{9,8},{10,11... | collective-permute-start | bytes 3145736 | tf_op jit(solution)/shard_map/ppermute | solution.py:553
  65.2 11.4 %collective-permute-start.3 = (bf16[8,128,512]{2,1,0:T(8,128)(2,1)}, bf16[8,128,512]{2,1,0:T(8,128)(2,1)S(1)}, u32[]{:S(2)}, u32[]{:S(2)}) collective-permute-start(bf16[8,128,512]{2,1,0:T(8,128)(2,1)} %get-tuple-element.131), channel_id=1, source_target_pairs={{0,1},{1,0},{2,3},{3,2},{4,5},{5,4},{6,7},{7,6},{8,9},{9,8},{10,11... | collective-permute-start | bytes 3145736 | tf_op jit(solution)/shard_map/ppermute | solution.py:553
  76.5 7.5 %collective-permute-start.4 = (bf16[4,128,512]{2,1,0:T(8,128)(2,1)}, bf16[4,128,512]{2,1,0:T(8,128)(2,1)S(1)}, u32[]{:S(2)}, u32[]{:S(2)}) collective-permute-start(bf16[4,128,512]{2,1,0:T(8,128)(2,1)} %get-tuple-element.139), channel_id=1, source_target_pairs={{0,1},{1,0},{2,3},{3,2},{4,5},{5,4},{6,7},{7,6},{8,9},{9,8},{10,11... | collective-permute-start | bytes 1572872 | tf_op jit(solution)/shard_map/ppermute | solution.py:553
  84.1 21.1 %collective-permute-start.5 = (bf16[8,128,512]{2,1,0:T(8,128)(2,1)}, bf16[8,128,512]{2,1,0:T(8,128)(2,1)S(1)}, u32[]{:S(2)}, u32[]{:S(2)}) collective-permute-start(bf16[8,128,512]{2,1,0:T(8,128)(2,1)} %get-tuple-element.146), channel_id=1, source_target_pairs={{0,1},{1,0},{2,3},{3,2},{4,5},{5,4},{6,7},{7,6},{8,9},{9,8},{10,11... | collective-permute-start | bytes 3145736 | tf_op jit(solution)/shard_map/ppermute | solution.py:553
  87.2 16.9 %collective-permute-start.7 = (bf16[4,128,512]{2,1,0:T(8,128)(2,1)}, bf16[4,128,512]{2,1,0:T(8,128)(2,1)S(1)}, u32[]{:S(2)}, u32[]{:S(2)}) collective-permute-start(bf16[4,128,512]{2,1,0:T(8,128)(2,1)} %get-tuple-element.221), channel_id=1, source_target_pairs={{0,4},{1,5},{2,6},{3,7},{4,0},{5,1},{6,2},{7,3},{8,12},{9,13},{10,... | collective-permute-start | bytes 1572872 | tf_op jit(solution)/shard_map/ppermute | solution.py:553
  91.3 13.8 %collective-permute-start.6 = (bf16[4,128,512]{2,1,0:T(8,128)(2,1)}, bf16[4,128,512]{2,1,0:T(8,128)(2,1)S(1)}, u32[]{:S(2)}, u32[]{:S(2)}) collective-permute-start(bf16[4,128,512]{2,1,0:T(8,128)(2,1)} %get-tuple-element.223), channel_id=1, source_target_pairs={{0,2},{1,3},{2,0},{3,1},{4,6},{5,7},{6,4},{7,5},{8,10},{9,11},{10,... | collective-permute-start | bytes 1572872 | tf_op jit(solution)/shard_map/ppermute | solution.py:553
  104.1 12.9 %copy-start.12 = (bf16[4,128,512]{2,1,0:T(8,128)(2,1)}, bf16[4,128,512]{2,1,0:T(8,128)(2,1)S(1)}, u32[]{:S(2)}) copy-start(bf16[4,128,512]{2,1,0:T(8,128)(2,1)S(1)} %collective-permute-done.7) | copy-start | bytes 1572868
  117.0 23.1 %collective-permute-start.9 = (bf16[8,160,512]{2,1,0:T(8,128)(2,1)}, bf16[8,160,512]{2,1,0:T(8,128)(2,1)S(1)}, u32[]{:S(2)}, u32[]{:S(2)}) collective-permute-start(bf16[8,160,512]{2,1,0:T(8,128)(2,1)} %get-tuple-element.166), channel_id=1, source_target_pairs={{0,1},{1,0},{2,3},{3,2},{4,5},{5,4},{6,7},{7,6},{8,9},{9,8},{10,11... | collective-permute-start | bytes 3932168 | tf_op jit(solution)/shard_map/ppermute | solution.py:553
  117.1 23.0 %collective-permute-start.8 = (bf16[8,128,512]{2,1,0:T(8,128)(2,1)}, bf16[8,128,512]{2,1,0:T(8,128)(2,1)S(1)}, u32[]{:S(2)}, u32[]{:S(2)}) collective-permute-start(bf16[8,128,512]{2,1,0:T(8,128)(2,1)} %get-tuple-element.165), channel_id=1, source_target_pairs={{0,1},{1,0},{2,3},{3,2},{4,5},{5,4},{6,7},{7,6},{8,9},{9,8},{10,11... | collective-permute-start | bytes 3145736 | tf_op jit(solution)/shard_map/ppermute | solution.py:553
  120.2 19.9 %collective-permute-start.12 = (bf16[4,128,512]{2,1,0:T(8,128)(2,1)}, bf16[4,128,512]{2,1,0:T(8,128)(2,1)}, u32[]{:S(2)}, u32[]{:S(2)}) collective-permute-start(bf16[4,128,512]{2,1,0:T(8,128)(2,1)} %get-tuple-element.219), channel_id=1, source_target_pairs={{0,2},{1,3},{2,0},{3,1},{4,6},{5,7},{6,4},{7,5},{8,10},{9,11},{10,... | collective-permute-start | bytes 1572872 | tf_op jit(solution)/shard_map/ppermute | solution.py:553
  122.8 17.3 %collective-permute-start.11 = (bf16[2,128,512]{2,1,0:T(8,128)(2,1)}, bf16[2,128,512]{2,1,0:T(8,128)(2,1)}, u32[]{:S(2)}, u32[]{:S(2)}) collective-permute-start(bf16[2,128,512]{2,1,0:T(8,128)(2,1)} %get-tuple-element.231), channel_id=1, source_target_pairs={{0,2},{1,3},{2,0},{3,1},{4,6},{5,7},{6,4},{7,5},{8,10},{9,11},{10,... | collective-permute-start | bytes 786440 | tf_op jit(solution)/shard_map/ppermute | solution.py:553
  124.1 20.2 %copy-start.8 = (bf16[2,128,512]{2,1,0:T(8,128)(2,1)}, bf16[2,128,512]{2,1,0:T(8,128)(2,1)S(1)}, u32[]{:S(2)}) copy-start(bf16[2,128,512]{2,1,0:T(8,128)(2,1)S(1)} %get-tuple-element.232) | copy-start | bytes 786436
  124.1 16.0 %collective-permute-start.10 = (bf16[2,128,512]{2,1,0:T(8,128)(2,1)}, bf16[2,128,512]{2,1,0:T(8,128)(2,1)}, u32[]{:S(2)}, u32[]{:S(2)}) collective-permute-start(bf16[2,128,512]{2,1,0:T(8,128)(2,1)} %get-tuple-element.233), channel_id=1, source_target_pairs={{0,4},{1,5},{2,6},{3,7},{4,0},{5,1},{6,2},{7,3},{8,12},{9,13},{10,... | collective-permute-start | bytes 786440 | tf_op jit(solution)/shard_map/ppermute | solution.py:553
  124.4 15.7 %copy-start.7 = (bf16[2,128,512]{2,1,0:T(8,128)(2,1)S(1)}, bf16[2,128,512]{2,1,0:T(8,128)(2,1)}, u32[]{:S(2)}) copy-start(bf16[2,128,512]{2,1,0:T(8,128)(2,1)} %get-tuple-element.230) | copy-start | bytes 786436
  134.5 14.1 %copy-start.1 = (bf16[8,128,512]{2,1,0:T(8,128)(2,1)S(1)}, bf16[8,128,512]{2,1,0:T(8,128)(2,1)}, u32[]{:S(2)}) copy-start(bf16[8,128,512]{2,1,0:T(8,128)(2,1)} %get-tuple-element.188) | copy-start | bytes 3145732
  140.1 37.2 %collective-permute-start.16 = (bf16[4,128,512]{2,1,0:T(8,128)(2,1)}, bf16[4,128,512]{2,1,0:T(8,128)(2,1)}, u32[]{:S(2)}, u32[]{:S(2)}) collective-permute-start(bf16[4,128,512]{2,1,0:T(8,128)(2,1)} %get-tuple-element.182), channel_id=1, source_target_pairs={{0,1},{1,0},{2,3},{3,2},{4,5},{5,4},{6,7},{7,6},{8,9},{9,8},{10,11... | collective-permute-start | bytes 1572872 | tf_op jit(solution)/shard_map/ppermute | solution.py:553
  141.7 20.2 %collective-permute-start.14 = (bf16[1,128,512]{2,1,0:T(8,128)(2,1)}, bf16[1,128,512]{2,1,0:T(8,128)(2,1)}, u32[]{:S(2)}, u32[]{:S(2)}) collective-permute-start(bf16[1,128,512]{2,1,0:T(8,128)(2,1)} %add_convert_fusion.37), channel_id=1, source_target_pairs={{0,8},{1,9},{2,10},{3,11},{4,12},{5,13},{6,14},{7,15},{8,0},{9,1},... | collective-permute-start | bytes 393224 | tf_op jit(solution)/shard_map/ppermute | solution.py:553
  145.9 17.6 %collective-permute-start.13 = (bf16[1,128,512]{2,1,0:T(8,128)(2,1)}, bf16[1,128,512]{2,1,0:T(8,128)(2,1)}, u32[]{:S(2)}, u32[]{:S(2)}) collective-permute-start(bf16[1,128,512]{2,1,0:T(8,128)(2,1)} %add_convert_fusion.38), channel_id=1, source_target_pairs={{0,8},{1,9},{2,10},{3,11},{4,12},{5,13},{6,14},{7,15},{8,0},{9,1},... | collective-permute-start | bytes 393224 | tf_op jit(solution)/shard_map/ppermute | solution.py:553
  148.2 24.7 %collective-permute-start.15 = (bf16[2,128,512]{2,1,0:T(8,128)(2,1)}, bf16[2,128,512]{2,1,0:T(8,128)(2,1)}, u32[]{:S(2)}, u32[]{:S(2)}) collective-permute-start(bf16[2,128,512]{2,1,0:T(8,128)(2,1)} %get-tuple-element.229), channel_id=1, source_target_pairs={{0,4},{1,5},{2,6},{3,7},{4,0},{5,1},{6,2},{7,3},{8,12},{9,13},{10,... | collective-permute-start | bytes 786440 | tf_op jit(solution)/shard_map/ppermute | solution.py:553
  149.7 37.5 %collective-permute-start.19 = (bf16[4,128,512]{2,1,0:T(8,128)(2,1)}, bf16[4,128,512]{2,1,0:T(8,128)(2,1)}, u32[]{:S(2)}, u32[]{:S(2)}) collective-permute-start(bf16[4,128,512]{2,1,0:T(8,128)(2,1)} %get-tuple-element.217), channel_id=1, source_target_pairs={{0,2},{1,3},{2,0},{3,1},{4,6},{5,7},{6,4},{7,5},{8,10},{9,11},{10,... | collective-permute-start | bytes 1572872 | tf_op jit(solution)/shard_map/ppermute | solution.py:553
  161.9 25.2 %collective-permute-start.20 = (bf16[4,160,512]{2,1,0:T(8,128)(2,1)S(1)}, bf16[4,160,512]{2,1,0:T(8,128)(2,1)S(1)}, u32[]{:S(2)}, u32[]{:S(2)}) collective-permute-start(bf16[4,160,512]{2,1,0:T(8,128)(2,1)S(1)} %get-tuple-element.215), channel_id=1, source_target_pairs={{0,4},{1,5},{2,6},{3,7},{4,0},{5,1},{6,2},{7,3},{8,12},{9,13},{10,... | collective-permute-start | bytes 1966088 | tf_op jit(solution)/shard_map/ppermute | solution.py:553
  165.6 6.7 %collective-permute-start.42 = (bf16[1,128,512]{2,1,0:T(8,128)(2,1)S(1)}, bf16[1,128,512]{2,1,0:T(8,128)(2,1)S(1)}, u32[]{:S(2)}, u32[]{:S(2)}) collective-permute-start(bf16[1,128,512]{2,1,0:T(8,128)(2,1)S(1)} %add_convert_fusion.29), channel_id=1, source_target_pairs={{0,16},{16,0},{1,17},{17,1},{2,18},{18,2},{3,19},{19,3},{4,20},{20... | collective-permute-start | bytes 393224 | tf_op jit(solution)/shard_map/ppermute | solution.py:553
  172.3 5.0 %collective-permute-start.43 = (bf16[1,128,512]{2,1,0:T(8,128)(2,1)S(1)}, bf16[1,128,512]{2,1,0:T(8,128)(2,1)S(1)}, u32[]{:S(2)}, u32[]{:S(2)}) collective-permute-start(bf16[1,128,512]{2,1,0:T(8,128)(2,1)S(1)} %add_convert_fusion.27), channel_id=1, source_target_pairs={{0,16},{16,0},{1,17},{17,1},{2,18},{18,2},{3,19},{19,3},{4,20},{20... | collective-permute-start | bytes 393224 | tf_op jit(solution)/shard_map/ppermute | solution.py:553
  172.9 14.2 %collective-permute-start.17 = (bf16[8,48,512]{2,1,0:T(8,128)(2,1)}, bf16[8,48,512]{2,1,0:T(8,128)(2,1)}, u32[]{:S(2)}, u32[]{:S(2)}) collective-permute-start(bf16[8,48,512]{2,1,0:T(8,128)(2,1)} %get-tuple-element.186), channel_id=1, source_target_pairs={{0,1},{1,0},{2,3},{3,2},{4,5},{5,4},{6,7},{7,6},{8,9},{9,8},{10,11... | collective-permute-start | bytes 1179656 | tf_op jit(solution)/shard_map/ppermute | solution.py:553
  177.3 9.9 %collective-permute-start.18 = (bf16[8,48,512]{2,1,0:T(8,128)(2,1)}, bf16[8,48,512]{2,1,0:T(8,128)(2,1)}, u32[]{:S(2)}, u32[]{:S(2)}) collective-permute-start(bf16[8,48,512]{2,1,0:T(8,128)(2,1)} %get-tuple-element.187), channel_id=1, source_target_pairs={{0,1},{1,0},{2,3},{3,2},{4,5},{5,4},{6,7},{7,6},{8,9},{9,8},{10,11... | collective-permute-start | bytes 1179656 | tf_op jit(solution)/shard_map/ppermute | solution.py:553
  177.3 9.8 %collective-permute-start.21 = (bf16[1,128,512]{2,1,0:T(8,128)(2,1)S(1)}, bf16[1,128,512]{2,1,0:T(8,128)(2,1)S(1)}, u32[]{:S(2)}, u32[]{:S(2)}) collective-permute-start(bf16[1,128,512]{2,1,0:T(8,128)(2,1)S(1)} %add_convert_fusion.36), channel_id=1, source_target_pairs={{0,8},{1,9},{2,10},{3,11},{4,12},{5,13},{6,14},{7,15},{8,0},{9,1},... | collective-permute-start | bytes 393224 | tf_op jit(solution)/shard_map/ppermute | solution.py:553
  188.9 2.6 %collective-permute-start.22 = (bf16[32,512]{1,0:T(8,128)(2,1)S(1)}, bf16[32,512]{1,0:T(8,128)(2,1)S(1)}, u32[]{:S(2)}, u32[]{:S(2)}) collective-permute-start(bf16[32,512]{1,0:T(8,128)(2,1)S(1)} %pad_maximum_fusion.4), channel_id=1, source_target_pairs={{0,1},{1,0},{2,3},{3,2},{4,5},{5,4},{6,7},{7,6},{8,9},{9,8},{10,11... | collective-permute-start | bytes 98312 | tf_op jit(solution)/shard_map/ppermute | solution.py:553
  189.1 15.9 %collective-permute-start.39 = (bf16[1,128,512]{2,1,0:T(8,128)(2,1)S(1)}, bf16[1,128,512]{2,1,0:T(8,128)(2,1)S(1)}, u32[]{:S(2)}, u32[]{:S(2)}) collective-permute-start(bf16[1,128,512]{2,1,0:T(8,128)(2,1)S(1)} %add_convert_fusion.33), channel_id=1, source_target_pairs={{0,16},{16,0},{1,17},{17,1},{2,18},{18,2},{3,19},{19,3},{4,20},{20... | collective-permute-start | bytes 393224 | tf_op jit(solution)/shard_map/ppermute | solution.py:553
  191.0 19.4 %collective-permute-start.28 = (bf16[4,48,512]{2,1,0:T(8,128)(2,1)S(1)}, bf16[4,48,512]{2,1,0:T(8,128)(2,1)S(1)}, u32[]{:S(2)}, u32[]{:S(2)}) collective-permute-start(bf16[4,48,512]{2,1,0:T(8,128)(2,1)S(1)} %get-tuple-element.236), channel_id=1, source_target_pairs={{0,4},{1,5},{2,6},{3,7},{4,0},{5,1},{6,2},{7,3},{8,12},{9,13},{10,... | collective-permute-start | bytes 589832 | tf_op jit(solution)/shard_map/ppermute | solution.py:553
  191.5 4.1 %collective-permute-start.23 = (bf16[32,512]{1,0:T(8,128)(2,1)S(1)}, bf16[32,512]{1,0:T(8,128)(2,1)S(1)}, u32[]{:S(2)}, u32[]{:S(2)}) collective-permute-start(bf16[32,512]{1,0:T(8,128)(2,1)S(1)} %add_convert_fusion.53), channel_id=1, source_target_pairs={{0,2},{1,3},{2,0},{3,1},{4,6},{5,7},{6,4},{7,5},{8,10},{9,11},{10,... | collective-permute-start | bytes 98312 | tf_op jit(solution)/shard_map/ppermute | solution.py:553
  193.2 17.2 %collective-permute-start.27 = (bf16[4,48,512]{2,1,0:T(8,128)(2,1)S(1)}, bf16[4,48,512]{2,1,0:T(8,128)(2,1)S(1)}, u32[]{:S(2)}, u32[]{:S(2)}) collective-permute-start(bf16[4,48,512]{2,1,0:T(8,128)(2,1)S(1)} %get-tuple-element.235), channel_id=1, source_target_pairs={{0,2},{1,3},{2,0},{3,1},{4,6},{5,7},{6,4},{7,5},{8,10},{9,11},{10,... | collective-permute-start | bytes 589832 | tf_op jit(solution)/shard_map/ppermute | solution.py:553
  195.6 4.0 %collective-permute-start.24 = (bf16[32,512]{1,0:T(8,128)(2,1)S(1)}, bf16[32,512]{1,0:T(8,128)(2,1)S(1)}, u32[]{:S(2)}, u32[]{:S(2)}) collective-permute-start(bf16[32,512]{1,0:T(8,128)(2,1)S(1)} %add_convert_fusion.52), channel_id=1, source_target_pairs={{0,4},{1,5},{2,6},{3,7},{4,0},{5,1},{6,2},{7,3},{8,12},{9,13},{10,... | collective-permute-start | bytes 98312 | tf_op jit(solution)/shard_map/ppermute | solution.py:553
  198.5 11.9 %collective-permute-start.29 = (bf16[2,128,512]{2,1,0:T(8,128)(2,1)S(1)}, bf16[2,128,512]{2,1,0:T(8,128)(2,1)S(1)}, u32[]{:S(2)}, u32[]{:S(2)}) collective-permute-start(bf16[2,128,512]{2,1,0:T(8,128)(2,1)S(1)} %get-tuple-element.227), channel_id=1, source_target_pairs={{0,4},{1,5},{2,6},{3,7},{4,0},{5,1},{6,2},{7,3},{8,12},{9,13},{10,... | collective-permute-start | bytes 786440 | tf_op jit(solution)/shard_map/ppermute | solution.py:553
  199.6 5.0 %collective-permute-start.25 = (bf16[32,512]{1,0:T(8,128)(2,1)S(1)}, bf16[32,512]{1,0:T(8,128)(2,1)S(1)}, u32[]{:S(2)}, u32[]{:S(2)}) collective-permute-start(bf16[32,512]{1,0:T(8,128)(2,1)S(1)} %add_convert_fusion.51), channel_id=1, source_target_pairs={{0,8},{1,9},{2,10},{3,11},{4,12},{5,13},{6,14},{7,15},{8,0},{9,1},... | collective-permute-start | bytes 98312 | tf_op jit(solution)/shard_map/ppermute | solution.py:553
  204.6 8.0 %collective-permute-start.30 = (bf16[2,160,512]{2,1,0:T(8,128)(2,1)S(1)}, bf16[2,160,512]{2,1,0:T(8,128)(2,1)S(1)}, u32[]{:S(2)}, u32[]{:S(2)}) collective-permute-start(bf16[2,160,512]{2,1,0:T(8,128)(2,1)S(1)} %get-tuple-element.225), channel_id=1, source_target_pairs={{0,2},{1,3},{2,0},{3,1},{4,6},{5,7},{6,4},{7,5},{8,10},{9,11},{10,... | collective-permute-start | bytes 983048 | tf_op jit(solution)/shard_map/ppermute | solution.py:553
  205.0 4.0 %collective-permute-start.26 = (bf16[32,512]{1,0:T(8,128)(2,1)S(1)}, bf16[32,512]{1,0:T(8,128)(2,1)S(1)}, u32[]{:S(2)}, u32[]{:S(2)}) collective-permute-start(bf16[32,512]{1,0:T(8,128)(2,1)S(1)} %add_convert_fusion.50), channel_id=1, source_target_pairs={{0,16},{16,0},{1,17},{17,1},{2,18},{18,2},{3,19},{19,3},{4,20},{20... | collective-permute-start | bytes 98312 | tf_op jit(solution)/shard_map/ppermute | solution.py:553
  212.7 7.0 %collective-permute-start.32 = (bf16[2,48,512]{2,1,0:T(8,128)(2,1)S(1)}, bf16[2,48,512]{2,1,0:T(8,128)(2,1)S(1)}, u32[]{:S(2)}, u32[]{:S(2)}) collective-permute-start(bf16[2,48,512]{2,1,0:T(8,128)(2,1)S(1)} %get-tuple-element.240), channel_id=1, source_target_pairs={{0,2},{1,3},{2,0},{3,1},{4,6},{5,7},{6,4},{7,5},{8,10},{9,11},{10,... | collective-permute-start | bytes 294920 | tf_op jit(solution)/shard_map/ppermute | solution.py:553
  212.9 12.1 %collective-permute-start.33 = (bf16[1,128,512]{2,1,0:T(8,128)(2,1)S(1)}, bf16[1,128,512]{2,1,0:T(8,128)(2,1)S(1)}, u32[]{:S(2)}, u32[]{:S(2)}) collective-permute-start(bf16[1,128,512]{2,1,0:T(8,128)(2,1)S(1)} %add_convert_fusion.35), channel_id=1, source_target_pairs={{0,8},{1,9},{2,10},{3,11},{4,12},{5,13},{6,14},{7,15},{8,0},{9,1},... | collective-permute-start | bytes 393224 | tf_op jit(solution)/shard_map/ppermute | solution.py:553
  216.1 10.6 %collective-permute-start.34 = (bf16[1,160,512]{2,1,0:T(8,128)(2,1)S(1)}, bf16[1,160,512]{2,1,0:T(8,128)(2,1)S(1)}, u32[]{:S(2)}, u32[]{:S(2)}) collective-permute-start(bf16[1,160,512]{2,1,0:T(8,128)(2,1)S(1)} %add_convert_fusion.26), channel_id=1, source_target_pairs={{0,8},{1,9},{2,10},{3,11},{4,12},{5,13},{6,14},{7,15},{8,0},{9,1},... | collective-permute-start | bytes 491528 | tf_op jit(solution)/shard_map/ppermute | solution.py:553
  216.2 5.5 %collective-permute-start.31 = (bf16[2,48,512]{2,1,0:T(8,128)(2,1)S(1)}, bf16[2,48,512]{2,1,0:T(8,128)(2,1)S(1)}, u32[]{:S(2)}, u32[]{:S(2)}) collective-permute-start(bf16[2,48,512]{2,1,0:T(8,128)(2,1)S(1)} %get-tuple-element.239), channel_id=1, source_target_pairs={{0,4},{1,5},{2,6},{3,7},{4,0},{5,1},{6,2},{7,3},{8,12},{9,13},{10,... | collective-permute-start | bytes 294920 | tf_op jit(solution)/shard_map/ppermute | solution.py:553
  226.9 5.6 %collective-permute-start.37 = (bf16[1,48,512]{2,1,0:T(8,128)(2,1)S(1)}, bf16[1,48,512]{2,1,0:T(8,128)(2,1)S(1)}, u32[]{:S(2)}, u32[]{:S(2)}) collective-permute-start(bf16[1,48,512]{2,1,0:T(8,128)(2,1)S(1)} %add_convert_fusion.44), channel_id=1, source_target_pairs={{0,8},{1,9},{2,10},{3,11},{4,12},{5,13},{6,14},{7,15},{8,0},{9,1},... | collective-permute-start | bytes 147464 | tf_op jit(solution)/shard_map/ppermute | solution.py:553
  227.0 7.3 %collective-permute-start.35 = (bf16[1,48,512]{2,1,0:T(8,128)(2,1)S(1)}, bf16[1,48,512]{2,1,0:T(8,128)(2,1)S(1)}, u32[]{:S(2)}, u32[]{:S(2)}) collective-permute-start(bf16[1,48,512]{2,1,0:T(8,128)(2,1)S(1)} %add_convert_fusion.47), channel_id=1, source_target_pairs={{0,8},{1,9},{2,10},{3,11},{4,12},{5,13},{6,14},{7,15},{8,0},{9,1},... | collective-permute-start | bytes 147464 | tf_op jit(solution)/shard_map/ppermute | solution.py:553
  229.9 9.5 %collective-permute-start.41 = (bf16[1,128,512]{2,1,0:T(8,128)(2,1)S(1)}, bf16[1,128,512]{2,1,0:T(8,128)(2,1)S(1)}, u32[]{:S(2)}, u32[]{:S(2)}) collective-permute-start(bf16[1,128,512]{2,1,0:T(8,128)(2,1)S(1)} %add_convert_fusion.31), channel_id=1, source_target_pairs={{0,16},{16,0},{1,17},{17,1},{2,18},{18,2},{3,19},{19,3},{4,20},{20... | collective-permute-start | bytes 393224 | tf_op jit(solution)/shard_map/ppermute | solution.py:553
  231.6 8.7 %collective-permute-start.40 = (bf16[1,160,512]{2,1,0:T(8,128)(2,1)S(1)}, bf16[1,160,512]{2,1,0:T(8,128)(2,1)S(1)}, u32[]{:S(2)}, u32[]{:S(2)}) collective-permute-start(bf16[1,160,512]{2,1,0:T(8,128)(2,1)S(1)} %add_convert_fusion.24), channel_id=1, source_target_pairs={{0,16},{16,0},{1,17},{17,1},{2,18},{18,2},{3,19},{19,3},{4,20},{20... | collective-permute-start | bytes 491528 | tf_op jit(solution)/shard_map/ppermute | solution.py:553
  232.5 5.6 %collective-permute-start.38 = (bf16[1,48,512]{2,1,0:T(8,128)(2,1)S(1)}, bf16[1,48,512]{2,1,0:T(8,128)(2,1)S(1)}, u32[]{:S(2)}, u32[]{:S(2)}) collective-permute-start(bf16[1,48,512]{2,1,0:T(8,128)(2,1)S(1)} %add_convert_fusion.43), channel_id=1, source_target_pairs={{0,16},{16,0},{1,17},{17,1},{2,18},{18,2},{3,19},{19,3},{4,20},{20... | collective-permute-start | bytes 147464 | tf_op jit(solution)/shard_map/ppermute | solution.py:553
  234.3 4.2 %collective-permute-start.36 = (bf16[1,48,512]{2,1,0:T(8,128)(2,1)S(1)}, bf16[1,48,512]{2,1,0:T(8,128)(2,1)S(1)}, u32[]{:S(2)}, u32[]{:S(2)}) collective-permute-start(bf16[1,48,512]{2,1,0:T(8,128)(2,1)S(1)} %add_convert_fusion.46), channel_id=1, source_target_pairs={{0,16},{16,0},{1,17},{17,1},{2,18},{18,2},{3,19},{19,3},{4,20},{20... | collective-permute-start | bytes 147464 | tf_op jit(solution)/shard_map/ppermute | solution.py:553
  (17 other events, 96.2 us)
